TPU v7x, 512 devices: a whole 4x4x16 slice. The times are simulated.
512 devices in a mesh: ctx: 64 (over z, y_lo, core), head: 8 (over x, y_hi).
Axes of the slice: x: 4, y: 4 (y_hi: 2, y_lo: 2; y = y_hi * 2 + y_lo), z: 16, core: 2. Of those that a mesh axis runs over, the one named last changes fastest.
Arguments:
- queries: bfloat16 [2, 64, 64, 128], P(None, 'ctx', 'head'), may hold values from -120 to 120
- new_keys: bfloat16 [2, 64, 8, 128], P(None, 'ctx', 'head'), may hold values from -6 to 6
- new_values: bfloat16 [2, 64, 8, 128], P(None, 'ctx', 'head'), may hold values from -6 to 6
- suffix_keys: bfloat16 [64, 512, 8, 128], P('ctx', None, 'head'), may hold values from -6 to 6
- suffix_values: bfloat16 [64, 512, 8, 128], P('ctx', None, 'head'), may hold values from -6 to 6
- suffix_lengths: int32 [64], P('ctx'), may hold values from 1 to 512, 16384 in all
- prefix_keys: bfloat16 [65536, 8, 128], P('ctx', 'head'), may hold values from -6 to 6
- prefix_values: bfloat16 [65536, 8, 128], P('ctx', 'head'), may hold values from -6 to 6
- out_weight: bfloat16 [8192, 5120], P('head', 'ctx'), may hold values from -0.0625 to 0.0625
- residual: bfloat16 [2, 64, 5120], P(None, 'head', 'ctx'), may hold values from -6 to 6
Outputs:
- layer_out: bfloat16 [2, 64, 5120], P(None, 'head', 'ctx')
All inputs are finite; a program needn't handle non-finite values. No bound on the sum of `suffix_lengths` on one device may be relied on, other than what follows from the above.
Results may differ from a plain program's by a relative error of at most 0.0068.
Values may be sent and summed in bfloat16 or wider, within the bound.
No kernel may reach another device: no remote copies, remote signals or barrier semaphores. Data moves between devices by JAX's collectives and lax.ppermute only.
A program may use at most 128 MiB of HBM per device.

v0:
```python
import math

import jax
import jax.numpy as jnp
from jax import lax
from jax.sharding import PartitionSpec as P

NEG_FILL = -1e30


def initial_state(row_shape, head_dim):
    return (
        jnp.zeros(row_shape + (head_dim,), jnp.float32),
        jnp.full(row_shape, NEG_FILL, jnp.float32),
        jnp.zeros(row_shape, jnp.float32),
    )


def combine(former, latter):
    highest = jnp.maximum(former[1], latter[1])
    factor_a = jnp.exp(former[1] - highest)
    factor_b = jnp.exp(latter[1] - highest)
    weighted = former[0] * factor_a[..., None] + latter[0] * factor_b[..., None]
    return (weighted, highest, former[2] * factor_a + latter[2] * factor_b)


def local_part(query_five, suffix_keys, suffix_values, new_keys, new_values, suffix_lengths):
    scaling = 1.0 / math.sqrt(query_five.shape[-1])
    suffix_scores = (
        jnp.einsum("tbkgd,bskd->tbkgs", query_five, suffix_keys, preferred_element_type=jnp.float32)
        * scaling
    )
    slot_count = suffix_keys.shape[1]
    usable = jnp.arange(slot_count, dtype=jnp.int32)[None, :] < suffix_lengths[:, None]
    usable = usable[None, :, None, None, :]
    suffix_scores = jnp.where(usable, suffix_scores, NEG_FILL)
    new_scores = (
        jnp.einsum("tbkgd,ubkd->tbkgu", query_five, new_keys, preferred_element_type=jnp.float32)
        * scaling
    )
    step_count = new_keys.shape[0]
    causal = jnp.arange(step_count)[None, :] <= jnp.arange(step_count)[:, None]
    causal = causal[:, None, None, None, :]
    new_scores = jnp.where(causal, new_scores, NEG_FILL)
    highest = jnp.maximum(suffix_scores.max(-1), new_scores.max(-1))
    suffix_weights = jnp.where(usable, jnp.exp(suffix_scores - highest[..., None]), 0.0)
    new_weights = jnp.where(causal, jnp.exp(new_scores - highest[..., None]), 0.0)
    weight_sum = suffix_weights.sum(-1) + new_weights.sum(-1)
    weighted = jnp.einsum(
        "tbkgs,bskd->tbkgd",
        suffix_weights.astype(jnp.bfloat16),
        suffix_values,
        preferred_element_type=jnp.float32,
    )
    weighted = weighted + jnp.einsum(
        "tbkgu,ubkd->tbkgd",
        new_weights.astype(jnp.bfloat16),
        new_values,
        preferred_element_type=jnp.float32,
    )
    return (weighted, highest, weight_sum)


def prefix_part(query_five, keys, values, carried, block_width):
    scaling = 1.0 / math.sqrt(query_five.shape[-1])
    block_count = keys.shape[0] // block_width

    def one_block(block_index, running):
        weighted, run_max, weight_sum = running
        key_block = lax.dynamic_slice_in_dim(keys, block_index * block_width, block_width, 0)
        value_block = lax.dynamic_slice_in_dim(values, block_index * block_width, block_width, 0)
        scores = (
            jnp.einsum(
                "sbkgd,nkd->sbkgn", query_five, key_block, preferred_element_type=jnp.float32
            )
            * scaling
        )
        highest = jnp.maximum(run_max, scores.max(-1))
        factor = jnp.exp(run_max - highest)
        weights = jnp.exp(scores - highest[..., None])
        weight_sum = weight_sum * factor + weights.sum(-1)
        weighted = weighted * factor[..., None] + jnp.einsum(
            "sbkgn,nkd->sbkgd",
            weights.astype(jnp.bfloat16),
            value_block,
            preferred_element_type=jnp.float32,
        )
        return (weighted, highest, weight_sum)

    return lax.fori_loop(0, block_count, one_block, carried)


def body(
    queries,
    new_keys,
    new_values,
    suffix_keys,
    suffix_values,
    suffix_lengths,
    prefix_keys,
    prefix_values,
    out_weight,
    residual,
):
    step_count, local_batch, local_heads, head_dim = queries.shape
    kv_local = prefix_keys.shape[1]
    group = local_heads // kv_local
    prompt_rows = prefix_keys.shape[0]
    query_five = queries.reshape(step_count, local_batch, kv_local, group, head_dim)
    own_state = local_part(
        query_five, suffix_keys, suffix_values, new_keys, new_values, suffix_lengths
    )
    every_query = lax.all_gather(query_five, "ctx", axis=1, tiled=True)
    starting = initial_state((step_count, every_query.shape[1], kv_local, group), head_dim)
    partial_state = prefix_part(
        every_query, prefix_keys, prefix_values, starting, min(prompt_rows, 512)
    )
    outgoing = (partial_state[0][None], partial_state[1][None], partial_state[2][None])
    received = (
        lax.all_to_all(outgoing[0], "ctx", split_axis=2, concat_axis=0, tiled=True),
        lax.all_to_all(outgoing[1], "ctx", split_axis=2, concat_axis=0, tiled=True),
        lax.all_to_all(outgoing[2], "ctx", split_axis=2, concat_axis=0, tiled=True),
    )
    highest = received[1].max(0)
    factor = jnp.exp(received[1] - highest)
    weighted = (received[0] * factor[..., None]).sum(0)
    weight_sum = (received[2] * factor).sum(0)
    total_state = combine((weighted, highest, weight_sum), own_state)
    attended = (
        (total_state[0] / total_state[2][..., None])
        .reshape(step_count, local_batch, local_heads, head_dim)
        .astype(jnp.bfloat16)
    )
    shard_piece = lax.all_gather(attended, "ctx", axis=1, tiled=True)
    row_count = shard_piece.shape[1]
    flattened = shard_piece.reshape(step_count * row_count, local_heads * head_dim)
    product = jnp.dot(flattened, out_weight, preferred_element_type=jnp.float32)
    partial_out = product.reshape(step_count, row_count, out_weight.shape[1])
    summed = lax.psum_scatter(partial_out, "head", scatter_dimension=1, tiled=True)
    return (summed + residual.astype(jnp.float32)).astype(jnp.bfloat16)


def solution(mesh):
    in_specs = (
        P(None, "ctx", "head", None),
        P(None, "ctx", "head", None),
        P(None, "ctx", "head", None),
        P("ctx", None, "head", None),
        P("ctx", None, "head", None),
        P("ctx"),
        P("ctx", "head", None),
        P("ctx", "head", None),
        P("head", "ctx"),
        P(None, "head", "ctx"),
    )
    out_specs = P(None, "head", "ctx")
    return jax.shard_map(body, mesh=mesh, in_specs=in_specs, out_specs=out_specs, check_vma=False)
```

profile of v0, /device:TPU:1, one launch (start us, length us, event | category | flops | bytes accessed | tf_op | source)
XLA Modules:
  0.0 304.0 jit_solution(15467510646765711285)
XLA Ops:
  6.5 72.1 %all-gather = bf16[2,64,8,128]{3,2,0,1:T(8,128)(2,1)S(1)} all-gather(bf16[2,1,8,128]{3,2,0,1:T(8,128)(2,1)} %bitcast.214), channel_id=2, replica_groups=mesh['ctx'=64,'head'=8] {'ctx'}, dimensions={1}, use_global_device_ids=true | all-gather | bytes 266240 | tf_op jit(solution)/shard_map/all_gather | solution.py:113
  78.7 0.1 copy.16
  78.7 6.0 %while.18 = (s32[]{:T(128)}, f32[2,64,1,8,128]{4,1,3,0,2:T(8,128)S(1)}, f32[2,64,1,8]{1,3,0,2:T(8,128)S(1)}, f32[2,64,1,8]{1,3,0,2:T(8,128)S(1)}, bf16[1024,1,12...) while((s32[]{:T(128)}, ...), condition=%wide.region_3.4_spmd.clone, body=%wide.region_0.0_spmd.clone.sunk | while | flops 273029120 | bytes 8986835 | solution.py:90
  78.8 1.5 bitcast_reduce_fusion.3
  80.2 0.6 fusion.70
  80.9 0.8 fusion.69
  81.8 1.5 bitcast_reduce_fusion.3
  83.2 0.6 fusion.70
  83.8 0.8 fusion.69
  84.8 0.7 copy.21
  85.5 6.9 %all-to-all-start.2 = ((f32[1,2,64,1,8]{4,1,3,0,2:T(2,128)}), f32[1,2,64,1,8]{4,1,3,0,2:T(2,128)S(1)}, u32[]{:S(2)}, u32[]{:S(2)}) async-start(f32[1,2,64,1,8]{4,1,3,0,2:T(2,128)} %bitcast.31), calls=%async_computation.2 | async-start | bytes 131072 | tf_op jit(solution)/shard_map/all_to_all | solution.py:122
  92.4 0.7 copy.18
  93.1 13.7 %all-to-all-done.2 = f32[1,2,64,1,8]{4,1,3,0,2:T(2,128)S(1)} async-done(((f32[1,2,64,1,8]{4,1,3,0,2:T(2,128)}), f32[1,2,64,1,8]{4,1,3,0,2:T(2,128)S(1)}, u32[]{:S(2)}, u32[]{:S(2)}) %all-to-all-start.2) | async-done | bytes 4128 | tf_op jit(solution)/shard_map/all_to_all | solution.py:122
  106.8 4.4 %all-to-all-start.1 = ((f32[1,2,64,1,8]{4,1,3,0,2:T(2,128)}), f32[1,2,64,1,8]{4,1,3,0,2:T(2,128)S(1)}, u32[]{:S(2)}, u32[]{:S(2)}) async-start(f32[1,2,64,1,8]{4,1,3,0,2:T(2,128)} %bitcast.6), calls=%async_computation.1 | async-start | bytes 131072 | tf_op jit(solution)/shard_map/all_to_all | solution.py:121
  111.3 1.1 copy.43
  112.4 13.5 %all-to-all-done.1 = f32[1,2,64,1,8]{4,1,3,0,2:T(2,128)S(1)} async-done(((f32[1,2,64,1,8]{4,1,3,0,2:T(2,128)}), f32[1,2,64,1,8]{4,1,3,0,2:T(2,128)S(1)}, u32[]{:S(2)}, u32[]{:S(2)}) %all-to-all-start.1) | async-done | bytes 4128 | tf_op jit(solution)/shard_map/all_to_all | solution.py:121
  125.9 4.5 %all-to-all-start = ((f32[1,2,64,1,8,128]{5,4,1,3,0,2:T(8,128)}), f32[1,2,64,1,8,128]{5,4,1,3,0,2:T(8,128)S(1)}, u32[]{:S(2)}, u32[]{:S(2)}) async-start(f32[1,2,64,1,8,128]{5,4,1,3,0,2:T(8,128)} %bitcast.187), calls=%async_computation | async-start | bytes 1048576 | tf_op jit(solution)/shard_map/all_to_all | solution.py:120
  131.1 0.1 convolution_multiply_fusion.1
  131.2 0.1 fusion.48
  131.3 0.2 fusion.60
  131.6 0.2 fusion.39
  131.7 0.1 fusion.57
  131.8 0.2 fusion.32
  132.0 0.1 bitcast_reduce_fusion.1
  132.1 0.1 fusion.38
  132.3 31.2 %all-to-all-done = f32[1,2,64,1,8,128]{5,4,1,3,0,2:T(8,128)S(1)} async-done(((f32[1,2,64,1,8,128]{5,4,1,3,0,2:T(8,128)}), f32[1,2,64,1,8,128]{5,4,1,3,0,2:T(8,128)S(1)}, u32[]{:S(2)}, u32[]{:S(2)}) %all-to-all-start) | async-done | bytes 524320 | tf_op jit(solution)/shard_map/all_to_all | solution.py:120
  163.4 0.2 fusion.28
  163.6 0.1 fusion.27
  163.8 62.4 %all-gather.1 = bf16[2,64,1,8,128]{4,3,2,0,1:T(8,128)(2,1)S(1)} all-gather(bf16[2,1,1,8,128]{4,3,2,0,1:T(8,128)(2,1)S(1)} %fusion.27), channel_id=3, replica_groups=mesh['ctx'=64,'head'=8] {'ctx'}, dimensions={1}, use_global_device_ids=true | all-gather | bytes 266240 | tf_op jit(solution)/shard_map/all_gather | solution.py:134
  226.3 0.8 fusion.29
  227.2 68.7 %reduce-scatter.2.cloned.1.call-done = f32[2,8,80]{2,1,0:T(8,128)} async-done(((f32[2,64,80]{2,1,0:T(8,128)}), f32[2,8,80]{2,1,0:T(8,128)}) %reduce-scatter.2.cloned.1.call-update) | async-done | bytes 5136 | tf_op jit(solution)/shard_map/reduce_scatter | solution.py:139
  295.8 1.3 add_convert_fusion
  (35 shorter events, 0.3 us)
Async XLA Ops:
  6.5 219.8 %copy-start = (bf16[1024,80]{0,1:T(8,128)(2,1)S(1)}, bf16[1024,80]{0,1:T(8,128)(2,1)}, u32[]{:S(2)}) copy-start(bf16[1024,80]{0,1:T(8,128)(2,1)} %param.20) | copy-start | bytes 491524
  78.8 2.1 copy-start.1
  81.7 2.1 copy-start.1
  84.7 46.4 %copy-start.4 = (bf16[2,1,8,128]{3,2,1,0:T(8,128)(2,1)S(1)}, bf16[2,1,8,128]{3,2,1,0:T(8,128)(2,1)}, u32[]{:S(2)}) copy-start(bf16[2,1,8,128]{3,2,1,0:T(8,128)(2,1)} %param.12) | copy-start | bytes 12292
  84.7 46.4 %copy-start.6 = (bf16[2,1,1,128]{3,0,2,1:T(2,128)(2,1)S(1)}, bf16[2,1,1,128]{3,0,2,1:T(2,128)(2,1)}, u32[]{:S(2)}) copy-start(bf16[2,1,1,128]{3,0,2,1:T(2,128)(2,1)} %param.13) | copy-start | bytes 1540
  84.7 46.6 %copy-start.2 = (bf16[1,512,1,128]{3,1,2,0:T(8,128)(2,1)S(1)}, bf16[1,512,1,128]{3,1,2,0:T(8,128)(2,1)}, u32[]{:S(2)}) copy-start(bf16[1,512,1,128]{3,1,2,0:T(8,128)(2,1)} %param.15) | copy-start | bytes 393220
  84.8 47.1 %copy-start.3 = (bf16[1,512,1,128]{3,1,2,0:T(8,128)(2,1)S(1)}, bf16[1,512,1,128]{3,1,2,0:T(8,128)(2,1)}, u32[]{:S(2)}) copy-start(bf16[1,512,1,128]{3,1,2,0:T(8,128)(2,1)} %param.16) | copy-start | bytes 393220
  84.8 78.9 %copy-start.7 = (bf16[2,1,1,128]{3,0,2,1:T(2,128)(2,1)S(1)}, bf16[2,1,1,128]{3,0,2,1:T(2,128)(2,1)}, u32[]{:S(2)}) copy-start(bf16[2,1,1,128]{3,0,2,1:T(2,128)(2,1)} %param.14) | copy-start | bytes 1540
  85.5 21.3 %all-to-all-start.2 = ((f32[1,2,64,1,8]{4,1,3,0,2:T(2,128)}), f32[1,2,64,1,8]{4,1,3,0,2:T(2,128)S(1)}, u32[]{:S(2)}, u32[]{:S(2)}) async-start(f32[1,2,64,1,8]{4,1,3,0,2:T(2,128)} %bitcast.31), calls=%async_computation.2 | async-start | bytes 131072 | tf_op jit(solution)/shard_map/all_to_all | solution.py:122
  106.8 19.1 %all-to-all-start.1 = ((f32[1,2,64,1,8]{4,1,3,0,2:T(2,128)}), f32[1,2,64,1,8]{4,1,3,0,2:T(2,128)S(1)}, u32[]{:S(2)}, u32[]{:S(2)}) async-start(f32[1,2,64,1,8]{4,1,3,0,2:T(2,128)} %bitcast.6), calls=%async_computation.1 | async-start | bytes 131072 | tf_op jit(solution)/shard_map/all_to_all | solution.py:121
  112.4 183.5 %copy-start.5 = (bf16[2,8,80]{2,1,0:T(8,128)(2,1)S(1)}, bf16[2,8,80]{2,1,0:T(8,128)(2,1)}, u32[]{:S(2)}) copy-start(bf16[2,8,80]{2,1,0:T(8,128)(2,1)} %param.21) | copy-start | bytes 7684
  125.9 37.5 %all-to-all-start = ((f32[1,2,64,1,8,128]{5,4,1,3,0,2:T(8,128)}), f32[1,2,64,1,8,128]{5,4,1,3,0,2:T(8,128)S(1)}, u32[]{:S(2)}, u32[]{:S(2)}) async-start(f32[1,2,64,1,8,128]{5,4,1,3,0,2:T(8,128)} %bitcast.187), calls=%async_computation | async-start | bytes 1048576 | tf_op jit(solution)/shard_map/all_to_all | solution.py:120
  130.3 165.5 %reduce-scatter.2.cloned.1.call-start = ((), (), s32[]{:S(2)}) async-start(), calls=%async_computation.4 | async-start | bytes 73728 | tf_op jit(solution)/shard_map/reduce_scatter | solution.py:139
Sparse Core Ops, SparseCore 0:
  227.3 68.4 reduce-scatter.1
where the time goes:
time: 305 us; the launch traced here: 304 us
  blocking collectives  135 us (44%)
  waiting for transfers between devices  127 us (42%)
  starting transfers between devices  15.8 us (5%)
  between operations  14.2 us (5%)
  matrix products  6.12 us (2%)
  other arithmetic  3.33 us (1%)
    all_gather x1, blocking collectives, body(): every_query = lax.all_gather(query_five, 'ctx', axis=1, tiled=True)  72.1 us
    reduce_scatter x1, waiting for transfers between devices, body(): lax.psum_scatter(partial_out, 'head', scatter_dimension=1, tiled=True)  68.7 us
    all_gather x1, blocking collectives, body(): shard_piece = lax.all_gather(attended, 'ctx', axis=1, tiled=True)  62.4 us
    all_to_all x1, waiting for transfers between devices, body(): lax.all_to_all(outgoing[0], 'ctx', split_axis=2, concat_axis=0, tiled=True)  31.2 us
    all_to_all x1, waiting for transfers between devices, body(): lax.all_to_all(outgoing[2], 'ctx', split_axis=2, concat_axis=0, tiled=True)  13.7 us
    all_to_all x1, waiting for transfers between devices, body(): lax.all_to_all(outgoing[1], 'ctx', split_axis=2, concat_axis=0, tiled=True)  13.5 us
    all_to_all x1, starting transfers between devices, body(): lax.all_to_all(outgoing[2], 'ctx', split_axis=2, concat_axis=0, tiled=True)  6.88 us
  transfers between devices with their start and end apart: 4, of which 4 were waited for; matrix products, arithmetic and copies ran while one was open for 1% of the time, Pallas kernels for 0%

commit v1 on v0

v1 whole, which is shorter than its diff:
```python
import functools
import math

import jax
import jax.numpy as jnp
from jax import lax
from jax.experimental import pallas as pl
from jax.experimental.pallas import tpu as pltpu
from jax.sharding import PartitionSpec as P

NEG_FILL = -1e30
BF16, F32 = jnp.bfloat16, jnp.float32
SCALE = math.log2(math.e) / math.sqrt(128)
NT = (((1,), (1,)), ((), ()))
STAT_ROWS = 8


def split_three(x):
    high = x.astype(BF16).astype(F32)
    rest = x - high
    middle = rest.astype(BF16).astype(F32)
    return [high, middle, rest - middle]


def prefix_kernel(q_ref, k0_ref, k1_ref, v0_ref, v1_ref, out_ref):
    key_block, row_block = 256, 256
    blocks = k0_ref.shape[0] // key_block
    for at in range(q_ref.shape[0] // row_block):
        q = q_ref[at * row_block : (at + 1) * row_block, :]
        scores = [
            lax.dot_general(k_ref[i * key_block : (i + 1) * key_block, :], q, NT, preferred_element_type=F32)
            for k_ref in (k0_ref, k1_ref)
            for i in range(blocks)
        ]
        highest = functools.reduce(jnp.maximum, [s.max(0, keepdims=True) for s in scores])
        total = jnp.zeros_like(highest)
        weighted = jnp.zeros((128, row_block), F32)
        values = [v_ref[i * key_block : (i + 1) * key_block, :] for v_ref in (v0_ref, v1_ref) for i in range(blocks)]
        for s, v in zip(scores, values):
            p = jnp.exp2((s - highest) * SCALE)
            total = total + p.sum(0, keepdims=True)
            weighted = weighted + lax.dot_general(
                v, p.astype(BF16), (((0,), (0,)), ((), ())), preferred_element_type=F32
            )
        first, count = at * row_block // 16, row_block // 16
        out_ref[first : first + count, 0:16, :] = weighted.T.astype(BF16).reshape(count, 16, 128)
        zero = jnp.zeros_like(highest)
        stats = jnp.concatenate(split_three(highest) + split_three(total) + [zero, zero], 0).astype(BF16)
        for part in range(row_block // 128):
            piece = stats[:, part * 128 : (part + 1) * 128]
            out_ref[first + part * 8 : first + part * 8 + 8, 16:24, :] = jnp.broadcast_to(piece[None], (8, 8, 128))


def suffix_kernel(length_ref, q_ref, sk_ref, sv_ref, nk_ref, nv_ref, o_ref, m_ref, l_ref):
    q = q_ref[...]
    s = lax.dot_general(q, sk_ref[...], NT, preferred_element_type=F32)
    usable = lax.broadcasted_iota(jnp.int32, s.shape, 1) < length_ref[0]
    s = jnp.where(usable, s, NEG_FILL)
    q_wide = q.astype(F32)
    new_keys, new_values = nk_ref[...].astype(F32), nv_ref[...].astype(F32)
    rows = q.shape[0]
    second = lax.broadcasted_iota(jnp.int32, (rows, 1), 0) >= rows // 2
    n0 = (q_wide * new_keys[0:1]).sum(1, keepdims=True)
    n1 = jnp.where(second, (q_wide * new_keys[1:2]).sum(1, keepdims=True), NEG_FILL)
    highest = jnp.maximum(s.max(1, keepdims=True), jnp.maximum(n0, n1))
    p = jnp.where(usable, jnp.exp2((s - highest) * SCALE), 0.0)
    p0 = jnp.exp2((n0 - highest) * SCALE)
    p1 = jnp.where(second, jnp.exp2((n1 - highest) * SCALE), 0.0)
    weighted = jnp.dot(p.astype(BF16), sv_ref[...], preferred_element_type=F32)
    weighted = weighted + p0.astype(BF16).astype(F32) * new_values[0:1] + p1.astype(BF16).astype(F32) * new_values[1:2]
    o_ref[...] = weighted
    m_ref[...] = jnp.broadcast_to(highest, m_ref.shape)
    l_ref[...] = jnp.broadcast_to(p.sum(1, keepdims=True) + p0 + p1, l_ref.shape)


def combine_kernel(place_ref, got_ref, so_ref, sm_ref, sl_ref, out_ref, turned):
    sources = got_ref.shape[0]
    stats = got_ref[:, 16:24, :].astype(F32)
    highest = stats[:, 0, :] + (stats[:, 1, :] + stats[:, 2, :])
    total = stats[:, 3, :] + (stats[:, 4, :] + stats[:, 5, :])
    rest = jnp.zeros((128 - 2 * sources, 128), F32)
    turned[...] = jnp.concatenate([highest, total, rest], 0).T
    mine = turned[pl.ds(pl.multiple_of(place_ref[0] * 16, 16), 16), :]
    maxima, totals = mine[:, 0:sources], mine[:, sources : 2 * sources]
    own_max, own_total = sm_ref[:, 0:1], sl_ref[:, 0:1]
    top = jnp.maximum(maxima.max(1, keepdims=True), own_max)
    factor = jnp.exp2((maxima - top) * SCALE)
    own_factor = jnp.exp2((own_max - top) * SCALE)
    weight_total = (factor * totals).sum(1, keepdims=True) + own_factor * own_total
    weighted = own_factor * so_ref[...]
    for i in range(sources):
        weighted = weighted + factor[:, i : i + 1] * got_ref[i, 0:16, :].astype(F32)
    out_ref[...] = (weighted / weight_total).astype(BF16)


def vmem(n):
    return [pl.BlockSpec(memory_space=pltpu.VMEM)] * n


SMEM = pl.BlockSpec(memory_space=pltpu.SMEM)
PARAMS = pltpu.CompilerParams(vmem_limit_bytes=32 * 1024 * 1024)


def body(
    queries,
    new_keys,
    new_values,
    suffix_keys,
    suffix_values,
    suffix_lengths,
    prefix_keys,
    prefix_values,
    out_weight,
    residual,
):
    steps, _, group, hd = queries.shape
    rows = steps * group
    ctx = lax.axis_size("ctx")
    heads = lax.axis_size("head")
    half = ctx // 2
    same_core = [[2 * i + core for i in range(half)] for core in range(2)]
    pairs = [[2 * i, 2 * i + 1] for i in range(half)]
    swap = [(i, i ^ 1) for i in range(ctx)]

    def spread(x):
        copies = jnp.broadcast_to(x[None], (half,) + x.shape)
        return lax.all_to_all(copies, "ctx", 0, 0, axis_index_groups=same_core, tiled=True)

    query_rows = queries.reshape(rows, hd)
    keys, values = prefix_keys.reshape(-1, hd), prefix_values.reshape(-1, hd)
    other_keys = lax.ppermute(keys, "ctx", swap)
    other_values = lax.ppermute(values, "ctx", swap)
    class_queries = spread(query_rows).reshape(half * rows, hd)

    own = pl.pallas_call(
        suffix_kernel,
        out_shape=[jax.ShapeDtypeStruct((rows, hd), F32)] * 3,
        in_specs=[SMEM] + vmem(5),
        out_specs=vmem(3),
        compiler_params=PARAMS,
        name="suffix_state",
    )(
        suffix_lengths,
        query_rows,
        suffix_keys.reshape(-1, hd),
        suffix_values.reshape(-1, hd),
        new_keys.reshape(-1, hd),
        new_values.reshape(-1, hd),
    )

    partial = pl.pallas_call(
        prefix_kernel,
        out_shape=jax.ShapeDtypeStruct((half, rows + STAT_ROWS, hd), BF16),
        in_specs=vmem(5),
        out_specs=vmem(1)[0],
        compiler_params=PARAMS,
        name="prefix_state",
    )(class_queries, keys, other_keys, values, other_values)
    received = lax.all_to_all(partial, "ctx", 0, 0, axis_index_groups=same_core, tiled=True)

    place = (lax.axis_index("ctx") // 2) % 8
    attended = pl.pallas_call(
        combine_kernel,
        out_shape=jax.ShapeDtypeStruct((rows, hd), BF16),
        in_specs=[SMEM] + vmem(4),
        out_specs=vmem(1)[0],
        scratch_shapes=[pltpu.VMEM((128, 128), F32)],
        compiler_params=PARAMS,
        name="combine",
    )(place.astype(jnp.int32).reshape(1), received, *own)

    class_rows = spread(attended)
    every = lax.all_gather(class_rows, "ctx", axis=0, axis_index_groups=pairs)
    every = every.reshape(2, half, steps, group, hd)
    weight = out_weight.reshape(group, hd, -1)
    product = jnp.einsum("citgd,gdn->citn", every, weight, preferred_element_type=F32)
    product = product.reshape(2, heads, half // heads, steps, -1).transpose(1, 3, 2, 0, 4)
    product = product.reshape(heads, steps, ctx // heads, -1)
    terms = lax.all_to_all(product, "head", 0, 0, tiled=True)
    return (terms.sum(0) + residual.astype(F32)).astype(BF16)


def solution(mesh):
    in_specs = (
        P(None, "ctx", "head", None),
        P(None, "ctx", "head", None),
        P(None, "ctx", "head", None),
        P("ctx", None, "head", None),
        P("ctx", None, "head", None),
        P("ctx"),
        P("ctx", "head", None),
        P("ctx", "head", None),
        P("head", "ctx"),
        P(None, "head", "ctx"),
    )
    out_specs = P(None, "head", "ctx")
    return jax.shard_map(body, mesh=mesh, in_specs=in_specs, out_specs=out_specs, check_vma=False)
```

time: 305 us -> 98.5 us (0.32)
  blocking collectives: 135 us -> 18.5 us
  waiting for transfers between devices: 127 us -> 37.4 us
  starting transfers between devices: 15.8 us -> 32.2 us
  between operations: 14.2 us -> 0.82 us
  matrix products: 6.12 us -> 0.27 us
  Pallas kernels: 0 us -> 3.8 us
    all_gather x2 -> x1, blocking collectives: 135 us -> 5.7 us  [body(): every = lax.all_gather(class_rows, 'ctx', axis=0, axis_index_groups=pairs)]
    reduce_scatter x1 -> x0, waiting for transfers between devices: 68.7 us -> none  [body(): lax.psum_scatter(partial_out, 'head', scatter_dimension=1, tiled=True)]
    all_to_all x3, waiting for transfers between devices: 58.4 us -> 35.7 us  [the longest x2 21.3 us: spread(): lax.all_to_all(copies, 'ctx', 0, 0, axis_index_groups=same_core, tiled=True)]
    all_to_all x0 -> x1, blocking collectives: none -> 12.8 us  [body(): terms = lax.all_to_all(product, 'head', 0, 0, tiled=True)]
    all_to_all x3, starting transfers between devices: 15.8 us -> 27.4 us  [the longest x2 22 us: spread(): lax.all_to_all(copies, 'ctx', 0, 0, axis_index_groups=same_core, tiled=True)]
    dot_general x9 -> x1, matrix products: 6.12 us -> 0.27 us  [body(): jnp.einsum('citgd,gdn->citn', every, weight, preferred_element_type=F32)]
    ppermute x0 -> x2, starting transfers between devices: none -> 4.79 us  [the longest x1 2.86 us: body(): other_keys = lax.ppermute(keys, 'ctx', swap)]
    pallas_call x0 -> x3, Pallas kernels: none -> 3.8 us  [the longest x1 2.9 us: body(): pl.pallas_call(prefix_kernel, out_shape=jax.ShapeDtypeStruct((half, rows...]
  transfers between devices with their start and end apart: 4 -> 5, of which waited for: 4 -> 4; matrix products, arithmetic and copies ran while one was open for 1% -> 0% of each run, Pallas kernels for 0% -> 0%
where the time goes in v1:
time: 98.5 us; the launch traced here: 98 us
  waiting for transfers between devices  37.4 us (38%)
  starting transfers between devices  32.2 us (33%)
  blocking collectives  18.5 us (19%)
  local copies, waits for them, and re-layouts  4.42 us (4%)
  Pallas kernels  3.8 us (4%)
    all_to_all x2, starting transfers between devices, spread(): lax.all_to_all(copies, 'ctx', 0, 0, axis_index_groups=same_core, tiled=True)  22 us
    all_to_all x2, waiting for transfers between devices, spread(): lax.all_to_all(copies, 'ctx', 0, 0, axis_index_groups=same_core, tiled=True)  21.3 us
    all_to_all x1, waiting for transfers between devices, body(): lax.all_to_all(partial, 'ctx', 0, 0, axis_index_groups=same_core, tiled=T...  14.4 us
    all_to_all x1, blocking collectives, body(): terms = lax.all_to_all(product, 'head', 0, 0, tiled=True)  12.8 us
    all_gather x1, blocking collectives, body(): every = lax.all_gather(class_rows, 'ctx', axis=0, axis_index_groups=pairs)  5.7 us
    all_to_all x1, starting transfers between devices, body(): lax.all_to_all(partial, 'ctx', 0, 0, axis_index_groups=same_core, tiled=T...  5.41 us
    pallas_call x1, Pallas kernels, body(): pl.pallas_call(prefix_kernel, out_shape=jax.ShapeDtypeStruct((half, rows...  2.9 us
    ppermute x1, starting transfers between devices, body(): other_keys = lax.ppermute(keys, 'ctx', swap)  2.86 us
  transfers between devices with their start and end apart: 5, of which 4 were waited for; matrix products, arithmetic and copies ran while one was open for 0% of the time, Pallas kernels for 0%

profile of v1, /device:TPU:1, one launch (start us, length us, event | category | flops | bytes accessed | tf_op | source)
XLA Modules:
  0.0 98.0 jit_solution(3020431607121331093)
XLA Ops:
  0.0 0.0 copy-start
  0.0 1.4 %broadcast_in_dim.14 = bf16[32,16,128]{2,1,0:T(8,128)(2,1)} broadcast(bf16[16,128]{1,0:T(8,128)(2,1)} %bitcast.33), dimensions={1,2} | broadcast | bytes 135168 | tf_op jit(solution)/shard_map/broadcast_in_dim | solution.py:126
  1.4 17.0 %all-to-all-start = ((bf16[32,16,128]{2,1,0:T(8,128)(2,1)}), bf16[32,16,128]{2,1,0:T(8,128)(2,1)S(1)}, u32[]{:S(2)}, u32[]{:S(2)}) async-start(bf16[32,16,128]{2,1,0:T(8,128)(2,1)} %broadcast_in_dim.14), calls=%async_computation | async-start | bytes 262144 | tf_op jit(solution)/shard_map/all_to_all | solution.py:127
  18.5 0.0 copy-done
  18.5 2.9 %collective-permute-start = (bf16[1024,128]{1,0:T(8,128)(2,1)S(1)}, bf16[1024,128]{1,0:T(8,128)(2,1)S(1)}, u32[]{:S(2)}, u32[]{:S(2)}) collective-permute-start(bf16[1024,128]{1,0:T(8,128)(2,1)S(1)} %bitcast.27), channel_id=1, source_target_pairs={{0,8},{8,0},{16,24},{24,16},{32,40},{40,32},{48,56},{56,48},{64,72... | collective-permute-start | bytes 786440 | tf_op jit(solution)/shard_map/ppermute | solution.py:131
  21.3 1.9 %collective-permute-start.1 = (bf16[1024,128]{1,0:T(8,128)(2,1)}, bf16[1024,128]{1,0:T(8,128)(2,1)S(1)}, u32[]{:S(2)}, u32[]{:S(2)}) collective-permute-start(bf16[1024,128]{1,0:T(8,128)(2,1)} %bitcast.29), channel_id=1, source_target_pairs={{0,8},{8,0},{16,24},{24,16},{32,40},{40,32},{48,56},{56,48},{64,72... | collective-permute-start | bytes 786440 | tf_op jit(solution)/shard_map/ppermute | solution.py:132
  23.3 0.0 collective-permute-done.k1_ref
  23.3 1.7 %collective-permute-done.1.v1_ref = bf16[1024,128]{1,0:T(8,128)(2,1)S(1)} collective-permute-done((bf16[1024,128]{1,0:T(8,128)(2,1)}, bf16[1024,128]{1,0:T(8,128)(2,1)S(1)}, u32[]{:S(2)}, u32[]{:S(2)}) %collective-permute-start.1) | collective-permute-done | bytes 262176 | tf_op jit(solution)/shard_map/ppermute | solution.py:132
  25.0 7.5 %all-to-all-done = bf16[32,16,128]{2,1,0:T(8,128)(2,1)S(1)} async-done(((bf16[32,16,128]{2,1,0:T(8,128)(2,1)}), bf16[32,16,128]{2,1,0:T(8,128)(2,1)S(1)}, u32[]{:S(2)}, u32[]{:S(2)}) %all-to-all-start) | async-done | bytes 131104 | tf_op jit(solution)/shard_map/all_to_all | solution.py:127
  32.5 0.9 copy-done.1
  33.5 2.9 %prefix_state.1 = bf16[32,24,128]{2,1,0:T(8,128)(2,1)} custom-call(bf16[512,128]{1,0:T(8,128)(2,1)S(1)} %bitcast.26, bf16[1024,128]{1,0:T(8,128)(2,1)S(1)} %bitcast.28, bf16[1024,128]{1,0:T(8,128)(2,1)S(1)} %collective-permute-done.k1_ref, bf16[1024,128]{1,0:T(8,128)(2,1)S(1)} %bitcast.30, bf16[1024,128]{1,0:T(8,128)(2,1)S(1)} %collective-permute-done.1.v1_ref), custom_call_target="tpu_custom_call" | custom-call | tf_op jit(solution)/shard_map/prefix_state/pallas_call | solution.py:151
  36.4 5.4 %all-to-all-start.1 = ((bf16[32,24,128]{2,1,0:T(8,128)(2,1)}), bf16[32,24,128]{2,1,0:T(8,128)(2,1)S(1)}, u32[]{:S(2)}, u32[]{:S(2)}) async-start(bf16[32,24,128]{2,1,0:T(8,128)(2,1)} %prefix_state.1), calls=%async_computation.1 | async-start | bytes 393216 | tf_op jit(solution)/shard_map/all_to_all | solution.py:159
  42.5 0.0 copy-start.4
  42.5 0.0 copy-start.5
  42.5 0.0 copy-start.6
  42.5 0.0 copy-done.2
  42.5 0.0 copy-done.3
  42.5 0.6 copy-done.4
  43.1 0.0 copy-done.5
  43.1 0.0 copy-done.6
  43.1 0.4 suffix_state.1
  43.5 14.4 %all-to-all-done.1.got_ref = bf16[32,24,128]{2,1,0:T(8,128)(2,1)S(1)} async-done(((bf16[32,24,128]{2,1,0:T(8,128)(2,1)}), bf16[32,24,128]{2,1,0:T(8,128)(2,1)S(1)}, u32[]{:S(2)}, u32[]{:S(2)}) %all-to-all-start.1) | async-done | bytes 196640 | tf_op jit(solution)/shard_map/all_to_all | solution.py:159
  57.9 0.5 combine.1
  58.5 0.7 broadcast_in_dim.15
  59.1 4.9 %all-to-all-start.2 = ((bf16[32,16,128]{2,1,0:T(8,128)(2,1)}), bf16[32,16,128]{2,1,0:T(8,128)(2,1)S(1)}, u32[]{:S(2)}, u32[]{:S(2)}) async-start(bf16[32,16,128]{2,1,0:T(8,128)(2,1)} %broadcast_in_dim.15), calls=%async_computation.2 | async-start | bytes 262144 | tf_op jit(solution)/shard_map/all_to_all | solution.py:127
  64.1 0.0 copy-done.7
  64.1 13.8 %all-to-all-done.2 = bf16[32,16,128]{2,1,0:T(8,128)(2,1)S(1)} async-done(((bf16[32,16,128]{2,1,0:T(8,128)(2,1)}), bf16[32,16,128]{2,1,0:T(8,128)(2,1)S(1)}, u32[]{:S(2)}, u32[]{:S(2)}) %all-to-all-start.2) | async-done | bytes 131104 | tf_op jit(solution)/shard_map/all_to_all | solution.py:127
  77.9 5.7 %all-gather = bf16[64,16,128]{2,1,0:T(8,128)(2,1)S(1)} all-gather(bf16[32,16,128]{2,1,0:T(8,128)(2,1)S(1)} %all-to-all-done.2), channel_id=2, replica_groups={{0,8},{16,24},{32,40},{48,56},{64,72},{80,88},{96,104},{112,120},{128,1..., dimensions={0}, use_global_device_ids=true | all-gather | bytes 393216 | tf_op jit(solution)/shard_map/all_gather | solution.py:173
  83.6 0.3 convolution_bitcast_fusion
  83.9 12.8 %all_to_all.20 = f32[8,2,8,80]{3,2,1,0:T(8,128)S(1)} all-to-all(f32[8,2,8,80]{3,2,1,0:T(8,128)S(1)} %copy.18), channel_id=1, replica_groups=mesh['ctx'=64,'head'=8] {'head'}, dimensions={0} | all-to-all | bytes 81920 | tf_op jit(solution)/shard_map/all_to_all | solution.py:179
  96.7 0.7 copy-done.8
  97.4 0.6 add_convert_fusion
  (9 shorter events, 0.1 us)
Async XLA Ops:
  0.0 18.5 %copy-start = (bf16[1024,1,128]{2,0,1:T(8,128)(2,1)S(1)}, bf16[1024,1,128]{2,0,1:T(8,128)(2,1)}, u32[]{:S(2)}) copy-start(bf16[1024,1,128]{2,0,1:T(8,128)(2,1)} %param.16) | copy-start | bytes 786436
  1.4 31.1 %all-to-all-start = ((bf16[32,16,128]{2,1,0:T(8,128)(2,1)}), bf16[32,16,128]{2,1,0:T(8,128)(2,1)S(1)}, u32[]{:S(2)}, u32[]{:S(2)}) async-start(bf16[32,16,128]{2,1,0:T(8,128)(2,1)} %broadcast_in_dim.14), calls=%async_computation | async-start | bytes 262144 | tf_op jit(solution)/shard_map/all_to_all | solution.py:127
  18.5 4.8 %collective-permute-start = (bf16[1024,128]{1,0:T(8,128)(2,1)S(1)}, bf16[1024,128]{1,0:T(8,128)(2,1)S(1)}, u32[]{:S(2)}, u32[]{:S(2)}) collective-permute-start(bf16[1024,128]{1,0:T(8,128)(2,1)S(1)} %bitcast.27), channel_id=1, source_target_pairs={{0,8},{8,0},{16,24},{24,16},{32,40},{40,32},{48,56},{56,48},{64,72... | collective-permute-start | bytes 786440 | tf_op jit(solution)/shard_map/ppermute | solution.py:131
  21.3 3.6 %collective-permute-start.1 = (bf16[1024,128]{1,0:T(8,128)(2,1)}, bf16[1024,128]{1,0:T(8,128)(2,1)S(1)}, u32[]{:S(2)}, u32[]{:S(2)}) collective-permute-start(bf16[1024,128]{1,0:T(8,128)(2,1)} %bitcast.29), channel_id=1, source_target_pairs={{0,8},{8,0},{16,24},{24,16},{32,40},{40,32},{48,56},{56,48},{64,72... | collective-permute-start | bytes 786440 | tf_op jit(solution)/shard_map/ppermute | solution.py:132
  32.5 1.0 copy-start.1
  36.4 6.1 %copy-start.2 = (bf16[1,512,1,128]{3,1,2,0:T(8,128)(2,1)S(1)}, bf16[1,512,1,128]{3,1,2,0:T(8,128)(2,1)}, u32[]{:S(2)}) copy-start(bf16[1,512,1,128]{3,1,2,0:T(8,128)(2,1)} %param.13) | copy-start | bytes 393220
  36.4 6.1 %copy-start.3 = (bf16[1,512,1,128]{3,1,2,0:T(8,128)(2,1)S(1)}, bf16[1,512,1,128]{3,1,2,0:T(8,128)(2,1)}, u32[]{:S(2)}) copy-start(bf16[1,512,1,128]{3,1,2,0:T(8,128)(2,1)} %param.14) | copy-start | bytes 393220
  36.4 21.6 %all-to-all-start.1 = ((bf16[32,24,128]{2,1,0:T(8,128)(2,1)}), bf16[32,24,128]{2,1,0:T(8,128)(2,1)S(1)}, u32[]{:S(2)}, u32[]{:S(2)}) async-start(bf16[32,24,128]{2,1,0:T(8,128)(2,1)} %prefix_state.1), calls=%async_computation.1 | async-start | bytes 393216 | tf_op jit(solution)/shard_map/all_to_all | solution.py:159
  42.5 0.7 copy-start.4
  42.5 0.7 copy-start.5
  42.5 0.7 copy-start.6
  59.1 5.0 %copy-start.7 = (bf16[1024,80]{0,1:T(8,128)(2,1)S(1)}, bf16[1024,80]{0,1:T(8,128)(2,1)}, u32[]{:S(2)}) copy-start(bf16[1024,80]{0,1:T(8,128)(2,1)} %param.18) | copy-start | bytes 491524
  59.1 18.8 %all-to-all-start.2 = ((bf16[32,16,128]{2,1,0:T(8,128)(2,1)}), bf16[32,16,128]{2,1,0:T(8,128)(2,1)S(1)}, u32[]{:S(2)}, u32[]{:S(2)}) async-start(bf16[32,16,128]{2,1,0:T(8,128)(2,1)} %broadcast_in_dim.15), calls=%async_computation.2 | async-start | bytes 262144 | tf_op jit(solution)/shard_map/all_to_all | solution.py:127
  96.7 0.7 copy-start.8

commit v2 on v1

v2 whole, which is shorter than its diff:
```python
import functools
import math

import jax
import jax.numpy as jnp
from jax import lax
from jax.experimental import pallas as pl
from jax.experimental.pallas import tpu as pltpu
from jax.sharding import PartitionSpec as P

NEG_FILL = -1e30
BF16, F32 = jnp.bfloat16, jnp.float32
SCALE = math.log2(math.e) / math.sqrt(128)
NT = (((1,), (1,)), ((), ()))


def split_three(x):
    high = x.astype(BF16).astype(F32)
    rest = x - high
    middle = rest.astype(BF16).astype(F32)
    return [high, middle, rest - middle]


def sample_rows(parts, count):
    lanes = 16 * count
    sample = lax.broadcasted_iota(jnp.int32, (count, lanes), 0)
    mine = sample == lax.broadcasted_iota(jnp.int32, (count, lanes), 1) // 16
    stacked = jnp.concatenate([jnp.where(mine, part, 0.0) for part in parts], 0).astype(BF16)
    place = lax.broadcasted_iota(jnp.int32, (lanes, 128), 0) % 16
    fold = (place == lax.broadcasted_iota(jnp.int32, (lanes, 128), 1) % 16).astype(F32).astype(BF16)
    folded = jnp.dot(stacked, fold, preferred_element_type=F32)
    lane_part = lax.broadcasted_iota(jnp.int32, (count, 128), 1) // 16
    rows = jnp.zeros((count, 128), F32)
    for p in range(len(parts)):
        rows = jnp.where(lane_part == p, folded[p * count : (p + 1) * count], rows)
    return rows


def prefix_kernel(q_ref, k_ref, v_ref, out_ref):
    key_block, row_block = 256, 256
    starts = [(c, i * key_block) for c in range(k_ref.shape[0]) for i in range(k_ref.shape[1] // key_block)]
    for at in range(q_ref.shape[0] // row_block):
        q = q_ref[at * row_block : (at + 1) * row_block, :]
        scores = [
            lax.dot_general(k_ref[c, i : i + key_block, :], q, NT, preferred_element_type=F32) for c, i in starts
        ]
        highest = functools.reduce(jnp.maximum, [s.max(0, keepdims=True) for s in scores])
        total = jnp.zeros_like(highest)
        weighted = jnp.zeros((128, row_block), F32)
        for s, (c, i) in zip(scores, starts):
            p = jnp.exp2((s - highest) * SCALE)
            total = total + p.sum(0, keepdims=True)
            weighted = weighted + lax.dot_general(
                v_ref[c, i : i + key_block, :], p.astype(BF16), (((0,), (0,)), ((), ())), preferred_element_type=F32
            )
        first, count = at * row_block // 16, row_block // 16
        out_ref[first : first + count, 0:8] = weighted.T.astype(BF16).reshape(count, 8, 2, 128)
        rows = sample_rows(split_three(highest) + split_three(total), count).astype(BF16)
        out_ref[first : first + count, 8] = jnp.broadcast_to(rows[:, None, :], (count, 2, 128))


def suffix_kernel(length_ref, q_ref, sk_ref, sv_ref, nk_ref, nv_ref, o_ref, m_ref, l_ref):
    q = q_ref[...]
    s = lax.dot_general(q, sk_ref[...], NT, preferred_element_type=F32)
    usable = lax.broadcasted_iota(jnp.int32, s.shape, 1) < length_ref[0]
    s = jnp.where(usable, s, NEG_FILL)
    q_wide = q.astype(F32)
    new_keys, new_values = nk_ref[...].astype(F32), nv_ref[...].astype(F32)
    rows = q.shape[0]
    second = lax.broadcasted_iota(jnp.int32, (rows, 1), 0) >= rows // 2
    n0 = (q_wide * new_keys[0:1]).sum(1, keepdims=True)
    n1 = jnp.where(second, (q_wide * new_keys[1:2]).sum(1, keepdims=True), NEG_FILL)
    highest = jnp.maximum(s.max(1, keepdims=True), jnp.maximum(n0, n1))
    p = jnp.where(usable, jnp.exp2((s - highest) * SCALE), 0.0)
    p0 = jnp.exp2((n0 - highest) * SCALE)
    p1 = jnp.where(second, jnp.exp2((n1 - highest) * SCALE), 0.0)
    weighted = jnp.dot(p.astype(BF16), sv_ref[...], preferred_element_type=F32)
    weighted = weighted + p0.astype(BF16).astype(F32) * new_values[0:1] + p1.astype(BF16).astype(F32) * new_values[1:2]
    o_ref[...] = weighted
    m_ref[...] = jnp.broadcast_to(highest, m_ref.shape)
    l_ref[...] = jnp.broadcast_to(p.sum(1, keepdims=True) + p0 + p1, l_ref.shape)


def combine_kernel(got_ref, so_ref, sm_ref, sl_ref, out_ref):
    sources = got_ref.shape[0]
    stats = got_ref[:, 8].astype(F32)[:, 0, :]
    parts = jnp.concatenate([stats, jnp.zeros((128 - sources, 128), F32)], 0).T[:, 0:sources]
    maxima = parts[0:16] + (parts[16:32] + parts[32:48])
    totals = parts[48:64] + (parts[64:80] + parts[80:96])
    own_max, own_total = sm_ref[:, 0:1], sl_ref[:, 0:1]
    top = jnp.maximum(maxima.max(1, keepdims=True), own_max)
    factor = jnp.exp2((maxima - top) * SCALE)
    own_factor = jnp.exp2((own_max - top) * SCALE)
    weight_total = (factor * totals).sum(1, keepdims=True) + own_factor * own_total
    weighted = own_factor * so_ref[...]
    for i in range(sources):
        weighted = weighted + factor[:, i : i + 1] * got_ref[i, 0:8].astype(F32).reshape(16, 128)
    attended = (weighted / weight_total).astype(BF16)
    out_ref[...] = jnp.broadcast_to(attended[None], out_ref.shape)


def project_kernel(place_ref, x_ref, w_ref, far_ref, out_ref):
    samples, rows, hd = x_ref.shape
    group = w_ref.shape[2] // hd
    heads = out_ref.shape[1]
    x = x_ref[...].astype(F32).reshape(samples * rows // group, group, hd)
    x = jnp.swapaxes(x, 0, 1).astype(BF16)
    side = place_ref[0] // 2 * 2
    for ref, at in ((w_ref, side), (far_ref, 2 - side)):
        for core in range(2):
            y = functools.reduce(
                jnp.add,
                [
                    lax.dot_general(
                        x[g], ref[core, :, g * hd : (g + 1) * hd], NT, preferred_element_type=F32
                    )
                    for g in range(group)
                ],
            )
            out_ref[at + core] = y.reshape(heads, -1, y.shape[1])


def finish_kernel(terms_ref, residual_ref, out_ref):
    planes, heads = terms_ref.shape[:2]
    steps = residual_ref.shape[0]
    sums = [functools.reduce(jnp.add, [terms_ref[d, h] for h in range(heads)]) for d in range(planes)]
    for t in range(steps):
        rows = [sums[d][z * steps + t][None] for z in range(sums[0].shape[0] // steps) for d in range(planes)]
        out_ref[t] = (jnp.concatenate(rows, 0) + residual_ref[t].astype(F32)).astype(BF16)


def vmem(n):
    return [pl.BlockSpec(memory_space=pltpu.VMEM)] * n


SMEM = pl.BlockSpec(memory_space=pltpu.SMEM)
PARAMS = pltpu.CompilerParams(vmem_limit_bytes=32 * 1024 * 1024)


def body(
    queries,
    new_keys,
    new_values,
    suffix_keys,
    suffix_values,
    suffix_lengths,
    prefix_keys,
    prefix_values,
    out_weight,
    residual,
):
    steps, _, group, hd = queries.shape
    rows = steps * group
    ctx = lax.axis_size("ctx")
    heads = lax.axis_size("head")
    depth = ctx // 4
    lines = [[4 * z + j for z in range(depth)] for j in range(4)]
    halves = [[2 * i + core for i in range(ctx // 2)] for core in range(2)]
    pairs = [[2 * i, 2 * i + 1] for i in range(ctx // 2)]
    planes = [[(4 * z + j) * heads + h for j in range(4) for h in range(heads)] for z in range(depth)]
    place = lax.axis_index("ctx").astype(jnp.int32)

    def swap(x, bit):
        return lax.ppermute(x, "ctx", [(i, i ^ bit) for i in range(ctx)])

    def exchange(x, groups):
        return lax.all_to_all(x, "ctx", 0, 0, axis_index_groups=groups, tiled=True)

    def both(x):
        return lax.all_gather(x, "ctx", axis=0, axis_index_groups=pairs)

    query_rows = queries.reshape(rows, hd)
    keys, values = both(prefix_keys.reshape(-1, hd)), both(prefix_values.reshape(-1, hd))
    copies = jnp.broadcast_to(query_rows[None], (ctx // 2, rows, hd))
    half_queries = exchange(copies, halves).reshape(ctx // 2 * rows, hd)

    own = pl.pallas_call(
        suffix_kernel,
        out_shape=[jax.ShapeDtypeStruct((rows, hd), F32)] * 3,
        in_specs=[SMEM] + vmem(5),
        out_specs=vmem(3),
        compiler_params=PARAMS,
        name="suffix_state",
    )(
        suffix_lengths,
        query_rows,
        suffix_keys.reshape(-1, hd),
        suffix_values.reshape(-1, hd),
        new_keys.reshape(-1, hd),
        new_values.reshape(-1, hd),
    )

    partial = pl.pallas_call(
        prefix_kernel,
        out_shape=jax.ShapeDtypeStruct((ctx // 2, rows // 2 + 1, 2, hd), BF16),
        in_specs=vmem(3),
        out_specs=vmem(1)[0],
        compiler_params=PARAMS,
        name="prefix_state",
    )(half_queries, keys, values)
    received = exchange(partial, halves)

    weight = out_weight.T
    far_weight = swap(weight, 2)
    weights, far_weights = both(weight), both(far_weight)

    attended = pl.pallas_call(
        combine_kernel,
        out_shape=jax.ShapeDtypeStruct((depth, rows, hd), BF16),
        in_specs=vmem(4),
        out_specs=vmem(1)[0],
        compiler_params=PARAMS,
        name="combine",
    )(received, *own)

    line_rows = exchange(attended, lines)
    columns = weight.shape[0]
    product = pl.pallas_call(
        project_kernel,
        out_shape=jax.ShapeDtypeStruct((4, heads, depth * steps // heads, columns), F32),
        in_specs=[SMEM] + vmem(3),
        out_specs=vmem(1)[0],
        compiler_params=PARAMS,
        name="project",
    )((place % 4).reshape(1), line_rows, weights, far_weights)
    product = product.reshape(4 * heads, depth * steps // heads, columns)
    terms = lax.all_to_all(product, ("ctx", "head"), 0, 0, axis_index_groups=planes, tiled=True)
    return pl.pallas_call(
        finish_kernel,
        out_shape=jax.ShapeDtypeStruct(residual.shape, BF16),
        in_specs=vmem(2),
        out_specs=vmem(1)[0],
        compiler_params=PARAMS,
        name="finish",
    )(terms.reshape(4, heads, depth * steps // heads, columns), residual)


def solution(mesh):
    in_specs = (
        P(None, "ctx", "head", None),
        P(None, "ctx", "head", None),
        P(None, "ctx", "head", None),
        P("ctx", None, "head", None),
        P("ctx", None, "head", None),
        P("ctx"),
        P("ctx", "head", None),
        P("ctx", "head", None),
        P("head", "ctx"),
        P(None, "head", "ctx"),
    )
    out_specs = P(None, "head", "ctx")
    return jax.shard_map(body, mesh=mesh, in_specs=in_specs, out_specs=out_specs, check_vma=False)
```

time: 98.5 us -> 91.5 us (0.929)
  waiting for transfers between devices: 37.4 us -> 22.9 us
  blocking collectives: 18.5 us -> 30.2 us
  starting transfers between devices: 32.2 us -> 29.6 us
  local copies, waits for them, and re-layouts: 4.42 us -> 2.08 us
  Pallas kernels: 3.8 us -> 5.48 us
    all_to_all x3, waiting for transfers between devices: 35.7 us -> 22.8 us  [exchange(): return lax.all_to_all(x, 'ctx', 0, 0, axis_index_groups=groups, tiled=True)]
    all_gather x1 -> x4, blocking collectives: 5.7 us -> 12 us  [both(): return lax.all_gather(x, 'ctx', axis=0, axis_index_groups=pairs)]
    all_to_all x1, blocking collectives: 12.8 us -> 18.3 us  [body(): lax.all_to_all(product, ('ctx', 'head'), 0, 0, axis_index_groups=planes,...]
    ppermute x2 -> x1, waiting for transfers between devices: 1.7 us -> 0.01 us  [swap(): return lax.ppermute(x, 'ctx', [(i, i ^ bit) for i in range(ctx)])]
    pallas_call x2 -> x4, Pallas kernels: 3.45 us -> 5.12 us  [the longest x1 2.92 us: body(): pl.pallas_call(prefix_kernel, out_shape=jax.ShapeDtypeStruct((ctx // 2, r...]
    ppermute x2 -> x1, starting transfers between devices: 4.79 us -> 3.14 us  [swap(): return lax.ppermute(x, 'ctx', [(i, i ^ bit) for i in range(ctx)])]
    unnamed x19 -> x18, local copies, waits for them, and re-layouts: 2.31 us -> 0.68 us
    broadcast_in_dim x2 -> x1, local copies, waits for them, and re-layouts: 2.09 us -> 1.4 us  [body(): copies = jnp.broadcast_to(query_rows[None], (ctx // 2, rows, hd))]
  transfers between devices with their start and end apart: 5 -> 4, of which waited for: 4 -> 3; matrix products, arithmetic and copies ran while one was open for 0% -> 0% of each run, Pallas kernels for 0% -> 2%
where the time goes in v2:
time: 91.5 us; the launch traced here: 91 us
  blocking collectives  30.2 us (33%)
  starting transfers between devices  29.6 us (32%)
  waiting for transfers between devices  22.9 us (25%)
  Pallas kernels  5.48 us (6%)
  local copies, waits for them, and re-layouts  2.08 us (2%)
    all_to_all x3, starting transfers between devices, exchange(): return lax.all_to_all(x, 'ctx', 0, 0, axis_index_groups=groups, tiled=True)  26.5 us
    all_to_all x3, waiting for transfers between devices, exchange(): return lax.all_to_all(x, 'ctx', 0, 0, axis_index_groups=groups, tiled=True)  22.8 us
    all_to_all x1, blocking collectives, body(): lax.all_to_all(product, ('ctx', 'head'), 0, 0, axis_index_groups=planes,...  18.3 us
    all_gather x4, blocking collectives, both(): return lax.all_gather(x, 'ctx', axis=0, axis_index_groups=pairs)  12 us
    ppermute x1, starting transfers between devices, swap(): return lax.ppermute(x, 'ctx', [(i, i ^ bit) for i in range(ctx)])  3.14 us
    pallas_call x1, Pallas kernels, body(): pl.pallas_call(prefix_kernel, out_shape=jax.ShapeDtypeStruct((ctx // 2, r...  2.92 us
  transfers between devices with their start and end apart: 4, of which 3 were waited for; matrix products, arithmetic and copies ran while one was open for 0% of the time, Pallas kernels for 2%

profile of v2, /device:TPU:1, one launch (start us, length us, event | category | flops | bytes accessed | tf_op | source)
XLA Modules:
  0.0 91.0 jit_solution(1715258299800336301)
XLA Ops:
  0.0 1.4 %broadcast_in_dim.8 = bf16[32,16,128]{2,1,0:T(8,128)(2,1)} broadcast(bf16[16,128]{1,0:T(8,128)(2,1)} %bitcast.23), dimensions={1,2} | broadcast | bytes 135168 | tf_op jit(solution)/shard_map/broadcast_in_dim | solution.py:174
  1.4 17.0 %all-to-all-start = ((bf16[32,16,128]{2,1,0:T(8,128)(2,1)}), bf16[32,16,128]{2,1,0:T(8,128)(2,1)S(1)}, u32[]{:S(2)}, u32[]{:S(2)}) async-start(bf16[32,16,128]{2,1,0:T(8,128)(2,1)} %broadcast_in_dim.8), calls=%async_computation | async-start | bytes 262144 | tf_op jit(solution)/shard_map/all_to_all | solution.py:167
  18.5 0.0 copy-done.6
  18.5 0.0 copy-start.7
  18.5 2.9 %all-gather = bf16[2048,1,128]{2,0,1:T(8,128)(2,1)S(1)} all-gather(bf16[1024,1,128]{2,0,1:T(8,128)(2,1)S(1)} %copy-done.6), channel_id=2, replica_groups={{0,8},{16,24},{32,40},{48,56},{64,72},{80,88},{96,104},{112,120},{128,1..., dimensions={0}, use_global_device_ids=true | all-gather | bytes 786432 | tf_op jit(solution)/shard_map/all_gather | solution.py:170
  21.4 0.0 copy-done.7
  21.4 2.2 %all-gather.1 = bf16[2048,1,128]{2,0,1:T(8,128)(2,1)S(1)} all-gather(bf16[1024,1,128]{2,0,1:T(8,128)(2,1)S(1)} %copy-done.7), channel_id=3, replica_groups={{0,8},{16,24},{32,40},{48,56},{64,72},{80,88},{96,104},{112,120},{128,1..., dimensions={0}, use_global_device_ids=true | all-gather | bytes 786432 | tf_op jit(solution)/shard_map/all_gather | solution.py:170
  23.5 9.0 %all-to-all-done = bf16[32,16,128]{2,1,0:T(8,128)(2,1)S(1)} async-done(((bf16[32,16,128]{2,1,0:T(8,128)(2,1)}), bf16[32,16,128]{2,1,0:T(8,128)(2,1)S(1)}, u32[]{:S(2)}, u32[]{:S(2)}) %all-to-all-start) | async-done | bytes 131104 | tf_op jit(solution)/shard_map/all_to_all | solution.py:167
  32.5 2.9 %prefix_state.1 = bf16[32,9,2,128]{3,2,1,0:T(2,128)(2,1)} custom-call(bf16[512,128]{1,0:T(8,128)(2,1)S(1)} %bitcast.18, bf16[2,1024,128]{2,1,0:T(8,128)(2,1)S(1)} %bitcast.14, bf16[2,1024,128]{2,1,0:T(8,128)(2,1)S(1)} %bitcast.15), custom_call_target="tpu_custom_call" | custom-call | tf_op jit(solution)/shard_map/prefix_state/pallas_call | solution.py:193
  35.4 5.2 %all-to-all-start.1 = ((bf16[32,9,2,128]{3,2,1,0:T(2,128)(2,1)}), bf16[32,9,2,128]{3,2,1,0:T(2,128)(2,1)S(1)}, u32[]{:S(2)}, u32[]{:S(2)}) async-start(bf16[32,9,2,128]{3,2,1,0:T(2,128)(2,1)} %prefix_state.1), calls=%async_computation.1 | async-start | bytes 294912 | tf_op jit(solution)/shard_map/all_to_all | solution.py:167
  40.7 0.0 copy-done.8
  40.7 3.1 %collective-permute-start = (bf16[80,1024]{1,0:T(8,128)(2,1)S(1)}, bf16[80,1024]{1,0:T(8,128)(2,1)S(1)}, u32[]{:S(2)}, u32[]{:S(2)}) collective-permute-start(bf16[80,1024]{1,0:T(8,128)(2,1)S(1)} %bitcast.27), channel_id=1, source_target_pairs={{0,16},{8,24},{16,0},{24,8},{32,48},{40,56},{48,32},{56,40},{64,80... | collective-permute-start | bytes 491528 | tf_op jit(solution)/shard_map/ppermute | solution.py:164
  44.5 0.0 copy-start.2
  44.5 0.0 copy-start.4
  44.5 0.0 copy-start.5
  44.5 0.0 copy-done
  44.5 0.0 copy-done.1
  44.5 0.6 copy-done.2
  45.1 0.0 copy-done.4
  45.1 0.0 copy-done.5
  45.2 0.4 suffix_state.1
  45.5 9.2 %all-to-all-done.1.got_ref = bf16[32,9,2,128]{3,2,1,0:T(2,128)(2,1)S(1)} async-done(((bf16[32,9,2,128]{3,2,1,0:T(2,128)(2,1)}), bf16[32,9,2,128]{3,2,1,0:T(2,128)(2,1)S(1)}, u32[]{:S(2)}, u32[]{:S(2)}) %all-to-all-start.1) | async-done | bytes 147488 | tf_op jit(solution)/shard_map/all_to_all | solution.py:167
  54.7 1.2 %combine.1 = bf16[16,16,128]{2,1,0:T(8,128)(2,1)} custom-call(bf16[32,9,2,128]{3,2,1,0:T(2,128)(2,1)S(1)} %all-to-all-done.1.got_ref, f32[16,128]{1,0:T(8,128)S(1)} %get-tuple-element.8.so_ref, f32[16,128]{1,0:T(8,128)S(1)} %get-tuple-element.9.sm_ref, f32[16,128]{1,0:T(8,128)S(1)} %get-tuple-element.10.sl_ref), custom_call_target="tpu_custom_call" | custom-call | tf_op jit(solution)/shard_map/combine/pallas_call | solution.py:207
  55.9 4.2 %all-to-all-start.2 = ((bf16[16,16,128]{2,1,0:T(8,128)(2,1)}), bf16[16,16,128]{2,1,0:T(8,128)(2,1)S(1)}, u32[]{:S(2)}, u32[]{:S(2)}) async-start(bf16[16,16,128]{2,1,0:T(8,128)(2,1)} %combine.1), calls=%async_computation.2 | async-start | bytes 131072 | tf_op jit(solution)/shard_map/all_to_all | solution.py:167
  60.1 4.9 %all-gather.2 = bf16[160,1024]{1,0:T(8,128)(2,1)S(1)} all-gather(bf16[80,1024]{1,0:T(8,128)(2,1)S(1)} %bitcast.28), channel_id=4, replica_groups={{0,8},{16,24},{32,40},{48,56},{64,72},{80,88},{96,104},{112,120},{128,1..., dimensions={0}, use_global_device_ids=true | all-gather | bytes 491520 | tf_op jit(solution)/shard_map/all_gather | solution.py:170
  65.0 0.0 collective-permute-done
  65.0 2.0 %all-gather.3 = bf16[160,1024]{1,0:T(8,128)(2,1)S(1)} all-gather(bf16[80,1024]{1,0:T(8,128)(2,1)S(1)} %collective-permute-done), channel_id=5, replica_groups={{0,8},{16,24},{32,40},{48,56},{64,72},{80,88},{96,104},{112,120},{128,1..., dimensions={0}, use_global_device_ids=true | all-gather | bytes 491520 | tf_op jit(solution)/shard_map/all_gather | solution.py:170
  67.0 4.7 %all-to-all-done.2.x_ref = bf16[16,16,128]{2,1,0:T(8,128)(2,1)S(1)} async-done(((bf16[16,16,128]{2,1,0:T(8,128)(2,1)}), bf16[16,16,128]{2,1,0:T(8,128)(2,1)S(1)}, u32[]{:S(2)}, u32[]{:S(2)}) %all-to-all-start.2) | async-done | bytes 65568 | tf_op jit(solution)/shard_map/all_to_all | solution.py:167
  71.7 0.4 project.1
  72.1 18.3 %all_to_all.20 = f32[32,4,80]{2,1,0:T(4,128)S(1)} all-to-all(f32[32,4,80]{2,1,0:T(4,128)S(1)} %bitcast.20), channel_id=1, replica_groups={{0,1,2,3,4,5,6,7,8,9,10,11,12,13,14,15,16,17,18,19,20,21,22,23,24,25,26..., dimensions={0} | all-to-all | bytes 81920 | tf_op jit(solution)/shard_map/all_to_all | solution.py:227
  90.4 0.0 copy-done.3
  90.4 0.6 finish.1
  (5 shorter events, 0.0 us)
Async XLA Ops:
  0.0 18.5 %copy-start.6 = (bf16[1024,1,128]{2,0,1:T(8,128)(2,1)S(1)}, bf16[1024,1,128]{2,0,1:T(8,128)(2,1)}, u32[]{:S(2)}) copy-start(bf16[1024,1,128]{2,0,1:T(8,128)(2,1)} %param.16) | copy-start | bytes 786436
  1.4 31.1 %all-to-all-start = ((bf16[32,16,128]{2,1,0:T(8,128)(2,1)}), bf16[32,16,128]{2,1,0:T(8,128)(2,1)S(1)}, u32[]{:S(2)}, u32[]{:S(2)}) async-start(bf16[32,16,128]{2,1,0:T(8,128)(2,1)} %broadcast_in_dim.8), calls=%async_computation | async-start | bytes 262144 | tf_op jit(solution)/shard_map/all_to_all | solution.py:167
  18.5 2.9 %copy-start.7 = (bf16[1024,1,128]{2,0,1:T(8,128)(2,1)S(1)}, bf16[1024,1,128]{2,0,1:T(8,128)(2,1)}, u32[]{:S(2)}) copy-start(bf16[1024,1,128]{2,0,1:T(8,128)(2,1)} %param.17) | copy-start | bytes 786436
  32.5 8.2 %copy-start.8 = (bf16[1024,80]{0,1:T(8,128)(2,1)S(1)}, bf16[1024,80]{0,1:T(8,128)(2,1)}, u32[]{:S(2)}) copy-start(bf16[1024,80]{0,1:T(8,128)(2,1)} %param.18) | copy-start | bytes 491524
  35.4 9.1 %copy-start = (bf16[1,512,1,128]{3,1,2,0:T(8,128)(2,1)S(1)}, bf16[1,512,1,128]{3,1,2,0:T(8,128)(2,1)}, u32[]{:S(2)}) copy-start(bf16[1,512,1,128]{3,1,2,0:T(8,128)(2,1)} %param.13) | copy-start | bytes 393220
  35.4 9.1 %copy-start.1 = (bf16[1,512,1,128]{3,1,2,0:T(8,128)(2,1)S(1)}, bf16[1,512,1,128]{3,1,2,0:T(8,128)(2,1)}, u32[]{:S(2)}) copy-start(bf16[1,512,1,128]{3,1,2,0:T(8,128)(2,1)} %param.14) | copy-start | bytes 393220
  35.4 19.3 %all-to-all-start.1 = ((bf16[32,9,2,128]{3,2,1,0:T(2,128)(2,1)}), bf16[32,9,2,128]{3,2,1,0:T(2,128)(2,1)S(1)}, u32[]{:S(2)}, u32[]{:S(2)}) async-start(bf16[32,9,2,128]{3,2,1,0:T(2,128)(2,1)} %prefix_state.1), calls=%async_computation.1 | async-start | bytes 294912 | tf_op jit(solution)/shard_map/all_to_all | solution.py:167
  40.7 24.3 %collective-permute-start = (bf16[80,1024]{1,0:T(8,128)(2,1)S(1)}, bf16[80,1024]{1,0:T(8,128)(2,1)S(1)}, u32[]{:S(2)}, u32[]{:S(2)}) collective-permute-start(bf16[80,1024]{1,0:T(8,128)(2,1)S(1)} %bitcast.27), channel_id=1, source_target_pairs={{0,16},{8,24},{16,0},{24,8},{32,48},{40,56},{48,32},{56,40},{64,80... | collective-permute-start | bytes 491528 | tf_op jit(solution)/shard_map/ppermute | solution.py:164
  44.5 0.7 copy-start.2
  44.5 0.7 copy-start.4
  44.5 0.7 copy-start.5
  55.9 15.8 %all-to-all-start.2 = ((bf16[16,16,128]{2,1,0:T(8,128)(2,1)}), bf16[16,16,128]{2,1,0:T(8,128)(2,1)S(1)}, u32[]{:S(2)}, u32[]{:S(2)}) async-start(bf16[16,16,128]{2,1,0:T(8,128)(2,1)} %combine.1), calls=%async_computation.2 | async-start | bytes 131072 | tf_op jit(solution)/shard_map/all_to_all | solution.py:167
  72.1 18.3 %copy-start.3 = (bf16[2,8,80]{2,1,0:T(8,128)(2,1)S(1)}, bf16[2,8,80]{2,1,0:T(8,128)(2,1)}, u32[]{:S(2)}) copy-start(bf16[2,8,80]{2,1,0:T(8,128)(2,1)} %residual_ref.1) | copy-start | bytes 7684

commit v3 on v2

--- a/solution.py
+++ b/solution.py
@@ -36,26 +36,39 @@
     return rows
 
 
-def prefix_kernel(q_ref, k_ref, v_ref, out_ref):
+def prefix_kernel(q_ref, kv_ref, near_ref, fk_ref, fv_ref, out_ref):
     key_block, row_block = 256, 256
-    starts = [(c, i * key_block) for c in range(k_ref.shape[0]) for i in range(k_ref.shape[1] // key_block)]
+    depth = kv_ref.shape[0] // 2
+    starts = range(0, depth, key_block)
+    shards = [
+        (kv_ref.at[0:depth], kv_ref.at[depth : 2 * depth]),
+        (near_ref.at[0:depth], near_ref.at[depth : 2 * depth]),
+        (fk_ref.at[0], fv_ref.at[0]),
+        (fk_ref.at[1], fv_ref.at[1]),
+    ]
     for at in range(q_ref.shape[0] // row_block):
         q = q_ref[at * row_block : (at + 1) * row_block, :]
         scores = [
-            lax.dot_general(k_ref[c, i : i + key_block, :], q, NT, preferred_element_type=F32) for c, i in starts
+            lax.dot_general(q, k[i : i + key_block, :], NT, preferred_element_type=F32) for k, _ in shards for i in starts
         ]
-        highest = functools.reduce(jnp.maximum, [s.max(0, keepdims=True) for s in scores])
-        total = jnp.zeros_like(highest)
-        weighted = jnp.zeros((128, row_block), F32)
-        for s, (c, i) in zip(scores, starts):
+        values = [v[i : i + key_block, :] for _, v in shards for i in starts]
+        highest = functools.reduce(jnp.maximum, scores).max(1, keepdims=True)
+        totals, weighted = [], []
+        for s, v in zip(scores, values):
             p = jnp.exp2((s - highest) * SCALE)
-            total = total + p.sum(0, keepdims=True)
-            weighted = weighted + lax.dot_general(
-                v_ref[c, i : i + key_block, :], p.astype(BF16), (((0,), (0,)), ((), ())), preferred_element_type=F32
-            )
+            totals.append(p)
+            weighted.append(jnp.dot(p.astype(BF16), v, preferred_element_type=F32))
+        total = functools.reduce(jnp.add, totals).sum(1, keepdims=True)
+        weighted = functools.reduce(jnp.add, weighted)
         first, count = at * row_block // 16, row_block // 16
-        out_ref[first : first + count, 0:8] = weighted.T.astype(BF16).reshape(count, 8, 2, 128)
-        rows = sample_rows(split_three(highest) + split_three(total), count).astype(BF16)
+        out_ref[first : first + count, 0:8] = weighted.astype(BF16).reshape(count, 8, 2, 128)
+        lane = lax.broadcasted_iota(jnp.int32, (row_block, 128), 1)
+        stats = jnp.zeros((row_block, 128), F32)
+        parts = split_three(highest) + split_three(total)
+        for p, part in enumerate(parts):
+            stats = jnp.where(lane == p, part, stats)
+        stats = stats.T
+        rows = sample_rows([stats[p : p + 1] for p in range(len(parts))], count).astype(BF16)
         out_ref[first : first + count, 8] = jnp.broadcast_to(rows[:, None, :], (count, 2, 128))
 
 
@@ -170,9 +183,13 @@
         return lax.all_gather(x, "ctx", axis=0, axis_index_groups=pairs)
 
     query_rows = queries.reshape(rows, hd)
-    keys, values = both(prefix_keys.reshape(-1, hd)), both(prefix_values.reshape(-1, hd))
-    copies = jnp.broadcast_to(query_rows[None], (ctx // 2, rows, hd))
-    half_queries = exchange(copies, halves).reshape(ctx // 2 * rows, hd)
+    kv = jnp.concatenate([prefix_keys.reshape(-1, hd), prefix_values.reshape(-1, hd)], 0)
+    far = swap(kv, 2)
+    near = swap(kv, 1)
+    copies = jnp.broadcast_to(query_rows[None], (depth, rows, hd))
+    line_queries = exchange(copies, lines).reshape(depth * rows, hd)
+    half = kv.shape[0] // 2
+    far_keys, far_values = both(far[:half]), both(far[half:])
 
     own = pl.pallas_call(
         suffix_kernel,
@@ -192,13 +209,13 @@
 
     partial = pl.pallas_call(
         prefix_kernel,
-        out_shape=jax.ShapeDtypeStruct((ctx // 2, rows // 2 + 1, 2, hd), BF16),
-        in_specs=vmem(3),
+        out_shape=jax.ShapeDtypeStruct((depth, rows // 2 + 1, 2, hd), BF16),
+        in_specs=vmem(5),
         out_specs=vmem(1)[0],
         compiler_params=PARAMS,
         name="prefix_state",
-    )(half_queries, keys, values)
-    received = exchange(partial, halves)
+    )(line_queries, kv, near, far_keys, far_values)
+    received = exchange(partial, lines)
 
     weight = out_weight.T
     far_weight = swap(weight, 2)

time: 91.5 us -> 89.3 us (0.976)
  blocking collectives: 30.2 us -> 26.9 us
  starting transfers between devices: 29.6 us -> 32.4 us
  waiting for transfers between devices: 22.9 us -> 21.2 us
  other arithmetic: 0 us -> 1.08 us
    ppermute x1 -> x3, starting transfers between devices: 3.14 us -> 12.8 us  [swap(): return lax.ppermute(x, 'ctx', [(i, i ^ bit) for i in range(ctx)])]
    all_to_all x3, starting transfers between devices: 26.5 us -> 19.6 us  [exchange(): return lax.all_to_all(x, 'ctx', 0, 0, axis_index_groups=groups, tiled=True)]
    all_gather x4, blocking collectives: 12 us -> 9.85 us  [both(): return lax.all_gather(x, 'ctx', axis=0, axis_index_groups=pairs)]
    all_to_all x3, waiting for transfers between devices: 22.8 us -> 21.2 us  [exchange(): return lax.all_to_all(x, 'ctx', 0, 0, axis_index_groups=groups, tiled=True)]
    all_to_all x1, blocking collectives: 18.3 us -> 17 us  [body(): lax.all_to_all(product, ('ctx', 'head'), 0, 0, axis_index_groups=planes,...]
    concatenate x0 -> x1, other arithmetic: none -> 1.08 us  [body(): jnp.concatenate([prefix_keys.reshape(-1, hd), prefix_values.reshape(-1, h...]
  transfers between devices with their start and end apart: 4 -> 6, of which waited for: 3 -> 3; matrix products, arithmetic and copies ran while one was open for 0% -> 1% of each run, Pallas kernels for 2% -> 2%
where the time goes in v3:
time: 89.3 us; the launch traced here: 88.8 us
  starting transfers between devices  32.4 us (36%)
  blocking collectives  26.9 us (30%)
  waiting for transfers between devices  21.2 us (24%)
  Pallas kernels  5.11 us (6%)
  local copies, waits for them, and re-layouts  1.33 us (1%)
  other arithmetic  1.08 us (1%)
    all_to_all x3, waiting for transfers between devices, exchange(): return lax.all_to_all(x, 'ctx', 0, 0, axis_index_groups=groups, tiled=True)  21.2 us
    all_to_all x3, starting transfers between devices, exchange(): return lax.all_to_all(x, 'ctx', 0, 0, axis_index_groups=groups, tiled=True)  19.6 us
    all_to_all x1, blocking collectives, body(): lax.all_to_all(product, ('ctx', 'head'), 0, 0, axis_index_groups=planes,...  17 us
    ppermute x3, starting transfers between devices, swap(): return lax.ppermute(x, 'ctx', [(i, i ^ bit) for i in range(ctx)])  12.8 us
    all_gather x4, blocking collectives, both(): return lax.all_gather(x, 'ctx', axis=0, axis_index_groups=pairs)  9.85 us
    pallas_call x1, Pallas kernels, body(): pl.pallas_call(prefix_kernel, out_shape=jax.ShapeDtypeStruct((depth, rows...  2.6 us
  transfers between devices with their start and end apart: 6, of which 3 were waited for; matrix products, arithmetic and copies ran while one was open for 1% of the time, Pallas kernels for 2%

profile of v3, /device:TPU:1, one launch (start us, length us, event | category | flops | bytes accessed | tf_op | source)
XLA Modules:
  0.0 88.8 jit_solution(4785024855222219243)
XLA Ops:
  0.0 1.1 %pad_maximum_fusion.kv_ref = bf16[2048,128]{1,0:T(8,128)(2,1)S(1)} fusion(bf16[1024,128]{1,0:T(8,128)(2,1)} %bitcast.29, bf16[1024,128]{1,0:T(8,128)(2,1)} %bitcast.30), kind=kLoop, calls=%fused_computation | loop fusion | flops 1048576 | bytes 1048576 | tf_op jit(solution)/shard_map/concatenate | solution.py:186
  1.1 4.0 %collective-permute-start.1 = (bf16[2048,128]{1,0:T(8,128)(2,1)S(1)}, bf16[2048,128]{1,0:T(8,128)(2,1)S(1)}, u32[]{:S(2)}, u32[]{:S(2)}) collective-permute-start(bf16[2048,128]{1,0:T(8,128)(2,1)S(1)} %pad_maximum_fusion.kv_ref), channel_id=1, source_target_pairs={{0,16},{8,24},{16,0},{24,8},{32,48},{40,56},{48,32},{56,40},{64,80... | collective-permute-start | bytes 1572872 | tf_op jit(solution)/shard_map/ppermute | solution.py:177
  5.1 6.7 %collective-permute-start = (bf16[2048,128]{1,0:T(8,128)(2,1)S(1)}, bf16[2048,128]{1,0:T(8,128)(2,1)S(1)}, u32[]{:S(2)}, u32[]{:S(2)}) collective-permute-start(bf16[2048,128]{1,0:T(8,128)(2,1)S(1)} %pad_maximum_fusion.kv_ref), channel_id=1, source_target_pairs={{0,8},{8,0},{16,24},{24,16},{32,40},{40,32},{48,56},{56,48},{64,72... | collective-permute-start | bytes 1572872 | tf_op jit(solution)/shard_map/ppermute | solution.py:177
  11.8 0.0 copy-done.2
  11.8 0.6 broadcast_in_dim.8
  12.5 11.1 %all-to-all-start = ((bf16[16,16,128]{2,1,0:T(8,128)(2,1)}), bf16[16,16,128]{2,1,0:T(8,128)(2,1)S(1)}, u32[]{:S(2)}, u32[]{:S(2)}) async-start(bf16[16,16,128]{2,1,0:T(8,128)(2,1)} %broadcast_in_dim.8), calls=%async_computation | async-start | bytes 131072 | tf_op jit(solution)/shard_map/all_to_all | solution.py:180
  23.6 0.0 collective-permute-done.1
  23.6 2.2 %all-gather = bf16[2048,128]{1,0:T(8,128)(2,1)S(1)} all-gather(bf16[1024,128]{1,0:T(8,128)(2,1)S(1)} %get-tuple-element.12), channel_id=2, replica_groups={{0,8},{16,24},{32,40},{48,56},{64,72},{80,88},{96,104},{112,120},{128,1..., dimensions={0}, use_global_device_ids=true | all-gather | bytes 786432 | tf_op jit(solution)/shard_map/all_gather | solution.py:183
  25.8 2.2 %all-gather.1 = bf16[2048,128]{1,0:T(8,128)(2,1)S(1)} all-gather(bf16[1024,128]{1,0:T(8,128)(2,1)S(1)} %get-tuple-element.11), channel_id=3, replica_groups={{0,8},{16,24},{32,40},{48,56},{64,72},{80,88},{96,104},{112,120},{128,1..., dimensions={0}, use_global_device_ids=true | all-gather | bytes 786432 | tf_op jit(solution)/shard_map/all_gather | solution.py:183
  28.0 7.2 %all-to-all-done = bf16[16,16,128]{2,1,0:T(8,128)(2,1)S(1)} async-done(((bf16[16,16,128]{2,1,0:T(8,128)(2,1)}), bf16[16,16,128]{2,1,0:T(8,128)(2,1)S(1)}, u32[]{:S(2)}, u32[]{:S(2)}) %all-to-all-start) | async-done | bytes 65568 | tf_op jit(solution)/shard_map/all_to_all | solution.py:180
  35.2 0.0 collective-permute-done.near_ref
  35.2 2.6 %prefix_state.1 = bf16[16,9,2,128]{3,2,1,0:T(2,128)(2,1)} custom-call(bf16[256,128]{1,0:T(8,128)(2,1)S(1)} %bitcast.20, bf16[2048,128]{1,0:T(8,128)(2,1)S(1)} %pad_maximum_fusion.kv_ref, bf16[2048,128]{1,0:T(8,128)(2,1)S(1)} %collective-permute-done.near_ref, bf16[2,1024,128]{2,1,0:T(8,128)(2,1)S(1)} %bitcast.16, bf16[2,1024,128]{2,1,0:T(8,128)(2,1)S(1)} %bitcast.17), custom_call_target="tpu_custom_call" | custom-call | tf_op jit(solution)/shard_map/prefix_state/pallas_call | solution.py:210
  37.8 4.6 %all-to-all-start.1 = ((bf16[16,9,2,128]{3,2,1,0:T(2,128)(2,1)}), bf16[16,9,2,128]{3,2,1,0:T(2,128)(2,1)S(1)}, u32[]{:S(2)}, u32[]{:S(2)}) async-start(bf16[16,9,2,128]{3,2,1,0:T(2,128)(2,1)} %prefix_state.1), calls=%async_computation.1 | async-start | bytes 147456 | tf_op jit(solution)/shard_map/all_to_all | solution.py:180
  42.4 0.0 copy-done.6
  42.4 2.1 %collective-permute-start.2 = (bf16[80,1024]{1,0:T(8,128)(2,1)S(1)}, bf16[80,1024]{1,0:T(8,128)(2,1)S(1)}, u32[]{:S(2)}, u32[]{:S(2)}) collective-permute-start(bf16[80,1024]{1,0:T(8,128)(2,1)S(1)} %bitcast.31), channel_id=1, source_target_pairs={{0,16},{8,24},{16,0},{24,8},{32,48},{40,56},{48,32},{56,40},{64,80... | collective-permute-start | bytes 491528 | tf_op jit(solution)/shard_map/ppermute | solution.py:177
  45.1 0.0 copy-start.4
  45.2 0.0 copy-start.5
  45.2 0.0 copy-done.1
  45.2 0.0 copy-done
  45.2 0.6 copy-done.4
  45.8 0.0 copy-done.5
  45.8 0.4 suffix_state.1
  46.2 7.9 %all-to-all-done.1.got_ref = bf16[16,9,2,128]{3,2,1,0:T(2,128)(2,1)S(1)} async-done(((bf16[16,9,2,128]{3,2,1,0:T(2,128)(2,1)}), bf16[16,9,2,128]{3,2,1,0:T(2,128)(2,1)S(1)}, u32[]{:S(2)}, u32[]{:S(2)}) %all-to-all-start.1) | async-done | bytes 73760 | tf_op jit(solution)/shard_map/all_to_all | solution.py:180
  54.1 1.1 %combine.1 = bf16[16,16,128]{2,1,0:T(8,128)(2,1)} custom-call(bf16[16,9,2,128]{3,2,1,0:T(2,128)(2,1)S(1)} %all-to-all-done.1.got_ref, f32[16,128]{1,0:T(8,128)S(1)} %get-tuple-element.8.so_ref, f32[16,128]{1,0:T(8,128)S(1)} %get-tuple-element.9.sm_ref, f32[16,128]{1,0:T(8,128)S(1)} %get-tuple-element.10.sl_ref), custom_call_target="tpu_custom_call" | custom-call | tf_op jit(solution)/shard_map/combine/pallas_call | solution.py:224
  55.2 4.0 %all-to-all-start.2 = ((bf16[16,16,128]{2,1,0:T(8,128)(2,1)}), bf16[16,16,128]{2,1,0:T(8,128)(2,1)S(1)}, u32[]{:S(2)}, u32[]{:S(2)}) async-start(bf16[16,16,128]{2,1,0:T(8,128)(2,1)} %combine.1), calls=%async_computation.2 | async-start | bytes 131072 | tf_op jit(solution)/shard_map/all_to_all | solution.py:180
  59.2 3.5 %all-gather.2 = bf16[160,1024]{1,0:T(8,128)(2,1)S(1)} all-gather(bf16[80,1024]{1,0:T(8,128)(2,1)S(1)} %bitcast.32), channel_id=4, replica_groups={{0,8},{16,24},{32,40},{48,56},{64,72},{80,88},{96,104},{112,120},{128,1..., dimensions={0}, use_global_device_ids=true | all-gather | bytes 491520 | tf_op jit(solution)/shard_map/all_gather | solution.py:183
  62.7 0.0 collective-permute-done.2
  62.7 2.0 %all-gather.3 = bf16[160,1024]{1,0:T(8,128)(2,1)S(1)} all-gather(bf16[80,1024]{1,0:T(8,128)(2,1)S(1)} %collective-permute-done.2), channel_id=5, replica_groups={{0,8},{16,24},{32,40},{48,56},{64,72},{80,88},{96,104},{112,120},{128,1..., dimensions={0}, use_global_device_ids=true | all-gather | bytes 491520 | tf_op jit(solution)/shard_map/all_gather | solution.py:183
  64.7 6.1 %all-to-all-done.2.x_ref = bf16[16,16,128]{2,1,0:T(8,128)(2,1)S(1)} async-done(((bf16[16,16,128]{2,1,0:T(8,128)(2,1)}), bf16[16,16,128]{2,1,0:T(8,128)(2,1)S(1)}, u32[]{:S(2)}, u32[]{:S(2)}) %all-to-all-start.2) | async-done | bytes 65568 | tf_op jit(solution)/shard_map/all_to_all | solution.py:180
  70.7 0.4 project.1
  71.2 17.0 %all_to_all.20 = f32[32,4,80]{2,1,0:T(4,128)S(1)} all-to-all(f32[32,4,80]{2,1,0:T(4,128)S(1)} %bitcast.22), channel_id=1, replica_groups={{0,1,2,3,4,5,6,7,8,9,10,11,12,13,14,15,16,17,18,19,20,21,22,23,24,25,26..., dimensions={0} | all-to-all | bytes 81920 | tf_op jit(solution)/shard_map/all_to_all | solution.py:244
  88.2 0.6 finish.1
  (7 shorter events, 0.0 us)
Async XLA Ops:
  0.0 11.8 %copy-start.2 = (bf16[2,1,8,128]{3,2,1,0:T(8,128)(2,1)S(1)}, bf16[2,1,8,128]{3,2,1,0:T(8,128)(2,1)}, u32[]{:S(2)}) copy-start(bf16[2,1,8,128]{3,2,1,0:T(8,128)(2,1)} %param.10) | copy-start | bytes 12292
  1.1 22.5 %collective-permute-start.1 = (bf16[2048,128]{1,0:T(8,128)(2,1)S(1)}, bf16[2048,128]{1,0:T(8,128)(2,1)S(1)}, u32[]{:S(2)}, u32[]{:S(2)}) collective-permute-start(bf16[2048,128]{1,0:T(8,128)(2,1)S(1)} %pad_maximum_fusion.kv_ref), channel_id=1, source_target_pairs={{0,16},{8,24},{16,0},{24,8},{32,48},{40,56},{48,32},{56,40},{64,80... | collective-permute-start | bytes 1572872 | tf_op jit(solution)/shard_map/ppermute | solution.py:177
  5.1 30.1 %collective-permute-start = (bf16[2048,128]{1,0:T(8,128)(2,1)S(1)}, bf16[2048,128]{1,0:T(8,128)(2,1)S(1)}, u32[]{:S(2)}, u32[]{:S(2)}) collective-permute-start(bf16[2048,128]{1,0:T(8,128)(2,1)S(1)} %pad_maximum_fusion.kv_ref), channel_id=1, source_target_pairs={{0,8},{8,0},{16,24},{24,16},{32,40},{40,32},{48,56},{56,48},{64,72... | collective-permute-start | bytes 1572872 | tf_op jit(solution)/shard_map/ppermute | solution.py:177
  12.5 22.7 %all-to-all-start = ((bf16[16,16,128]{2,1,0:T(8,128)(2,1)}), bf16[16,16,128]{2,1,0:T(8,128)(2,1)S(1)}, u32[]{:S(2)}, u32[]{:S(2)}) async-start(bf16[16,16,128]{2,1,0:T(8,128)(2,1)} %broadcast_in_dim.8), calls=%async_computation | async-start | bytes 131072 | tf_op jit(solution)/shard_map/all_to_all | solution.py:180
  35.2 7.2 %copy-start.6 = (bf16[1024,80]{0,1:T(8,128)(2,1)S(1)}, bf16[1024,80]{0,1:T(8,128)(2,1)}, u32[]{:S(2)}) copy-start(bf16[1024,80]{0,1:T(8,128)(2,1)} %param.18) | copy-start | bytes 491524
  35.2 10.0 %copy-start.1 = (bf16[1,512,1,128]{3,1,2,0:T(8,128)(2,1)S(1)}, bf16[1,512,1,128]{3,1,2,0:T(8,128)(2,1)}, u32[]{:S(2)}) copy-start(bf16[1,512,1,128]{3,1,2,0:T(8,128)(2,1)} %param.14) | copy-start | bytes 393220
  37.8 7.4 %copy-start = (bf16[1,512,1,128]{3,1,2,0:T(8,128)(2,1)S(1)}, bf16[1,512,1,128]{3,1,2,0:T(8,128)(2,1)}, u32[]{:S(2)}) copy-start(bf16[1,512,1,128]{3,1,2,0:T(8,128)(2,1)} %param.13) | copy-start | bytes 393220
  37.8 16.3 %all-to-all-start.1 = ((bf16[16,9,2,128]{3,2,1,0:T(2,128)(2,1)}), bf16[16,9,2,128]{3,2,1,0:T(2,128)(2,1)S(1)}, u32[]{:S(2)}, u32[]{:S(2)}) async-start(bf16[16,9,2,128]{3,2,1,0:T(2,128)(2,1)} %prefix_state.1), calls=%async_computation.1 | async-start | bytes 147456 | tf_op jit(solution)/shard_map/all_to_all | solution.py:180
  42.4 20.3 %collective-permute-start.2 = (bf16[80,1024]{1,0:T(8,128)(2,1)S(1)}, bf16[80,1024]{1,0:T(8,128)(2,1)S(1)}, u32[]{:S(2)}, u32[]{:S(2)}) collective-permute-start(bf16[80,1024]{1,0:T(8,128)(2,1)S(1)} %bitcast.31), channel_id=1, source_target_pairs={{0,16},{8,24},{16,0},{24,8},{32,48},{40,56},{48,32},{56,40},{64,80... | collective-permute-start | bytes 491528 | tf_op jit(solution)/shard_map/ppermute | solution.py:177
  45.1 0.7 copy-start.4
  45.2 0.7 copy-start.5
  55.2 15.5 %all-to-all-start.2 = ((bf16[16,16,128]{2,1,0:T(8,128)(2,1)}), bf16[16,16,128]{2,1,0:T(8,128)(2,1)S(1)}, u32[]{:S(2)}, u32[]{:S(2)}) async-start(bf16[16,16,128]{2,1,0:T(8,128)(2,1)} %combine.1), calls=%async_computation.2 | async-start | bytes 131072 | tf_op jit(solution)/shard_map/all_to_all | solution.py:180
  71.2 17.0 %copy-start.3 = (bf16[2,8,80]{2,1,0:T(8,128)(2,1)S(1)}, bf16[2,8,80]{2,1,0:T(8,128)(2,1)}, u32[]{:S(2)}) copy-start(bf16[2,8,80]{2,1,0:T(8,128)(2,1)} %residual_ref.1) | copy-start | bytes 7684

commit v4 on v3

--- a/solution.py
+++ b/solution.py
@@ -12,6 +12,7 @@
 BF16, F32 = jnp.bfloat16, jnp.float32
 SCALE = math.log2(math.e) / math.sqrt(128)
 NT = (((1,), (1,)), ((), ()))
+LAST_Z, LAST_HEAD = 10, 5
 
 
 def split_three(x):
@@ -115,7 +116,7 @@
 def project_kernel(place_ref, x_ref, w_ref, far_ref, out_ref):
     samples, rows, hd = x_ref.shape
     group = w_ref.shape[2] // hd
-    heads = out_ref.shape[1]
+    heads, chunk = out_ref.shape[1:3]
     x = x_ref[...].astype(F32).reshape(samples * rows // group, group, hd)
     x = jnp.swapaxes(x, 0, 1).astype(BF16)
     side = place_ref[0] // 2 * 2
@@ -130,7 +131,9 @@
                     for g in range(group)
                 ],
             )
-            out_ref[at + core] = y.reshape(heads, -1, y.shape[1])
+            for block in range(heads):
+                shard = (block * samples // heads + LAST_Z) % samples * heads // samples
+                out_ref[at + core, (shard - LAST_HEAD) % heads] = y[block * chunk : (block + 1) * chunk]
 
 
 def finish_kernel(terms_ref, residual_ref, out_ref):
@@ -167,10 +170,12 @@
     ctx = lax.axis_size("ctx")
     heads = lax.axis_size("head")
     depth = ctx // 4
-    lines = [[4 * z + j for z in range(depth)] for j in range(4)]
+    lines = [[4 * ((z + LAST_Z) % depth) + j for z in range(depth)] for j in range(4)]
     halves = [[2 * i + core for i in range(ctx // 2)] for core in range(2)]
     pairs = [[2 * i, 2 * i + 1] for i in range(ctx // 2)]
-    planes = [[(4 * z + j) * heads + h for j in range(4) for h in range(heads)] for z in range(depth)]
+    planes = [
+        [(4 * z + j) * heads + (h + LAST_HEAD) % heads for j in range(4) for h in range(heads)] for z in range(depth)
+    ]
     place = lax.axis_index("ctx").astype(jnp.int32)
 
     def swap(x, bit):

time: 89.3 us -> 80.5 us (0.901)
  waiting for transfers between devices: 21.2 us -> 2.3 us
  starting transfers between devices: 32.4 us -> 46.3 us
  blocking collectives: 26.9 us -> 23.2 us
    all_to_all x3, waiting for transfers between devices: 21.2 us -> 2.3 us  [exchange(): return lax.all_to_all(x, 'ctx', 0, 0, axis_index_groups=groups, tiled=True)]
    all_to_all x3, starting transfers between devices: 19.6 us -> 33.5 us  [exchange(): return lax.all_to_all(x, 'ctx', 0, 0, axis_index_groups=groups, tiled=True)]
    all_to_all x1, blocking collectives: 17 us -> 12.4 us  [body(): lax.all_to_all(product, ('ctx', 'head'), 0, 0, axis_index_groups=planes,...]
    all_gather x4, blocking collectives: 9.85 us -> 10.8 us  [both(): return lax.all_gather(x, 'ctx', axis=0, axis_index_groups=pairs)]
  transfers between devices with their start and end apart: 6 -> 6, of which waited for: 3 -> 2; matrix products, arithmetic and copies ran while one was open for 1% -> 1% of each run, Pallas kernels for 2% -> 2%
where the time goes in v4:
time: 80.5 us; the launch traced here: 80 us
  starting transfers between devices  46.3 us (58%)
  blocking collectives  23.2 us (29%)
  Pallas kernels  5.11 us (6%)
  waiting for transfers between devices  2.3 us (3%)
  local copies, waits for them, and re-layouts  1.33 us (2%)
  other arithmetic  1.08 us (1%)
    all_to_all x3, starting transfers between devices, exchange(): return lax.all_to_all(x, 'ctx', 0, 0, axis_index_groups=groups, tiled=True)  33.5 us
    ppermute x3, starting transfers between devices, swap(): return lax.ppermute(x, 'ctx', [(i, i ^ bit) for i in range(ctx)])  12.8 us
    all_to_all x1, blocking collectives, body(): lax.all_to_all(product, ('ctx', 'head'), 0, 0, axis_index_groups=planes,...  12.4 us
    all_gather x4, blocking collectives, both(): return lax.all_gather(x, 'ctx', axis=0, axis_index_groups=pairs)  10.8 us
    pallas_call x1, Pallas kernels, body(): pl.pallas_call(prefix_kernel, out_shape=jax.ShapeDtypeStruct((depth, rows...  2.6 us
    all_to_all x3, waiting for transfers between devices, exchange(): return lax.all_to_all(x, 'ctx', 0, 0, axis_index_groups=groups, tiled=True)  2.3 us
  transfers between devices with their start and end apart: 6, of which 2 were waited for; matrix products, arithmetic and copies ran while one was open for 1% of the time, Pallas kernels for 2%

profile of v4, /device:TPU:1, one launch (start us, length us, event | category | flops | bytes accessed | tf_op | source)
XLA Modules:
  0.0 80.0 jit_solution(10239065952270038491)
XLA Ops:
  0.0 1.1 %pad_maximum_fusion.kv_ref = bf16[2048,128]{1,0:T(8,128)(2,1)S(1)} fusion(bf16[1024,128]{1,0:T(8,128)(2,1)} %bitcast.29, bf16[1024,128]{1,0:T(8,128)(2,1)} %bitcast.30), kind=kLoop, calls=%fused_computation | loop fusion | flops 1048576 | bytes 1048576 | tf_op jit(solution)/shard_map/concatenate | solution.py:191
  1.1 4.0 %collective-permute-start.1 = (bf16[2048,128]{1,0:T(8,128)(2,1)S(1)}, bf16[2048,128]{1,0:T(8,128)(2,1)S(1)}, u32[]{:S(2)}, u32[]{:S(2)}) collective-permute-start(bf16[2048,128]{1,0:T(8,128)(2,1)S(1)} %pad_maximum_fusion.kv_ref), channel_id=1, source_target_pairs={{0,16},{8,24},{16,0},{24,8},{32,48},{40,56},{48,32},{56,40},{64,80... | collective-permute-start | bytes 1572872 | tf_op jit(solution)/shard_map/ppermute | solution.py:182
  5.1 6.7 %collective-permute-start = (bf16[2048,128]{1,0:T(8,128)(2,1)S(1)}, bf16[2048,128]{1,0:T(8,128)(2,1)S(1)}, u32[]{:S(2)}, u32[]{:S(2)}) collective-permute-start(bf16[2048,128]{1,0:T(8,128)(2,1)S(1)} %pad_maximum_fusion.kv_ref), channel_id=1, source_target_pairs={{0,8},{8,0},{16,24},{24,16},{32,40},{40,32},{48,56},{56,48},{64,72... | collective-permute-start | bytes 1572872 | tf_op jit(solution)/shard_map/ppermute | solution.py:182
  11.8 0.0 copy-done.2
  11.8 0.6 broadcast_in_dim.8
  12.5 12.7 %all-to-all-start = ((bf16[16,16,128]{2,1,0:T(8,128)(2,1)}), bf16[16,16,128]{2,1,0:T(8,128)(2,1)S(1)}, u32[]{:S(2)}, u32[]{:S(2)}) async-start(bf16[16,16,128]{2,1,0:T(8,128)(2,1)} %broadcast_in_dim.8), calls=%async_computation | async-start | bytes 131072 | tf_op jit(solution)/shard_map/all_to_all | solution.py:185
  25.1 0.0 collective-permute-done.1
  25.2 2.4 %all-gather = bf16[2048,128]{1,0:T(8,128)(2,1)S(1)} all-gather(bf16[1024,128]{1,0:T(8,128)(2,1)S(1)} %get-tuple-element.12), channel_id=2, replica_groups={{0,8},{16,24},{32,40},{48,56},{64,72},{80,88},{96,104},{112,120},{128,1..., dimensions={0}, use_global_device_ids=true | all-gather | bytes 786432 | tf_op jit(solution)/shard_map/all_gather | solution.py:188
  27.6 2.2 %all-gather.1 = bf16[2048,128]{1,0:T(8,128)(2,1)S(1)} all-gather(bf16[1024,128]{1,0:T(8,128)(2,1)S(1)} %get-tuple-element.11), channel_id=3, replica_groups={{0,8},{16,24},{32,40},{48,56},{64,72},{80,88},{96,104},{112,120},{128,1..., dimensions={0}, use_global_device_ids=true | all-gather | bytes 786432 | tf_op jit(solution)/shard_map/all_gather | solution.py:188
  29.7 1.1 %all-to-all-done = bf16[16,16,128]{2,1,0:T(8,128)(2,1)S(1)} async-done(((bf16[16,16,128]{2,1,0:T(8,128)(2,1)}), bf16[16,16,128]{2,1,0:T(8,128)(2,1)S(1)}, u32[]{:S(2)}, u32[]{:S(2)}) %all-to-all-start) | async-done | bytes 65568 | tf_op jit(solution)/shard_map/all_to_all | solution.py:185
  30.8 0.0 collective-permute-done.near_ref
  30.8 2.6 %prefix_state.1 = bf16[16,9,2,128]{3,2,1,0:T(2,128)(2,1)} custom-call(bf16[256,128]{1,0:T(8,128)(2,1)S(1)} %bitcast.20, bf16[2048,128]{1,0:T(8,128)(2,1)S(1)} %pad_maximum_fusion.kv_ref, bf16[2048,128]{1,0:T(8,128)(2,1)S(1)} %collective-permute-done.near_ref, bf16[2,1024,128]{2,1,0:T(8,128)(2,1)S(1)} %bitcast.16, bf16[2,1024,128]{2,1,0:T(8,128)(2,1)S(1)} %bitcast.17), custom_call_target="tpu_custom_call" | custom-call | tf_op jit(solution)/shard_map/prefix_state/pallas_call | solution.py:215
  33.4 10.6 %all-to-all-start.1 = ((bf16[16,9,2,128]{3,2,1,0:T(2,128)(2,1)}), bf16[16,9,2,128]{3,2,1,0:T(2,128)(2,1)S(1)}, u32[]{:S(2)}, u32[]{:S(2)}) async-start(bf16[16,9,2,128]{3,2,1,0:T(2,128)(2,1)} %prefix_state.1), calls=%async_computation.1 | async-start | bytes 147456 | tf_op jit(solution)/shard_map/all_to_all | solution.py:185
  44.0 2.1 %collective-permute-start.2 = (bf16[80,1024]{1,0:T(8,128)(2,1)S(1)}, bf16[80,1024]{1,0:T(8,128)(2,1)S(1)}, u32[]{:S(2)}, u32[]{:S(2)}) collective-permute-start(bf16[80,1024]{1,0:T(8,128)(2,1)S(1)} %bitcast.31), channel_id=1, source_target_pairs={{0,16},{8,24},{16,0},{24,8},{32,48},{40,56},{48,32},{56,40},{64,80... | collective-permute-start | bytes 491528 | tf_op jit(solution)/shard_map/ppermute | solution.py:182
  46.7 0.0 copy-start.4
  46.7 0.0 copy-start.5
  46.7 0.0 copy-done.1
  46.7 0.0 copy-done
  46.8 0.6 copy-done.4
  47.4 0.0 copy-done.5
  47.4 0.4 suffix_state.1
  47.7 1.2 %all-to-all-done.1.got_ref = bf16[16,9,2,128]{3,2,1,0:T(2,128)(2,1)S(1)} async-done(((bf16[16,9,2,128]{3,2,1,0:T(2,128)(2,1)}), bf16[16,9,2,128]{3,2,1,0:T(2,128)(2,1)S(1)}, u32[]{:S(2)}, u32[]{:S(2)}) %all-to-all-start.1) | async-done | bytes 73760 | tf_op jit(solution)/shard_map/all_to_all | solution.py:185
  49.0 1.1 %combine.1 = bf16[16,16,128]{2,1,0:T(8,128)(2,1)} custom-call(bf16[16,9,2,128]{3,2,1,0:T(2,128)(2,1)S(1)} %all-to-all-done.1.got_ref, f32[16,128]{1,0:T(8,128)S(1)} %get-tuple-element.8.so_ref, f32[16,128]{1,0:T(8,128)S(1)} %get-tuple-element.9.sm_ref, f32[16,128]{1,0:T(8,128)S(1)} %get-tuple-element.10.sl_ref), custom_call_target="tpu_custom_call" | custom-call | tf_op jit(solution)/shard_map/combine/pallas_call | solution.py:229
  50.1 10.2 %all-to-all-start.2 = ((bf16[16,16,128]{2,1,0:T(8,128)(2,1)}), bf16[16,16,128]{2,1,0:T(8,128)(2,1)S(1)}, u32[]{:S(2)}, u32[]{:S(2)}) async-start(bf16[16,16,128]{2,1,0:T(8,128)(2,1)} %combine.1), calls=%async_computation.2 | async-start | bytes 131072 | tf_op jit(solution)/shard_map/all_to_all | solution.py:185
  60.3 4.2 %all-gather.2 = bf16[160,1024]{1,0:T(8,128)(2,1)S(1)} all-gather(bf16[80,1024]{1,0:T(8,128)(2,1)S(1)} %bitcast.32), channel_id=4, replica_groups={{0,8},{16,24},{32,40},{48,56},{64,72},{80,88},{96,104},{112,120},{128,1..., dimensions={0}, use_global_device_ids=true | all-gather | bytes 491520 | tf_op jit(solution)/shard_map/all_gather | solution.py:188
  64.5 0.0 collective-permute-done.2
  64.5 2.0 %all-gather.3 = bf16[160,1024]{1,0:T(8,128)(2,1)S(1)} all-gather(bf16[80,1024]{1,0:T(8,128)(2,1)S(1)} %collective-permute-done.2), channel_id=5, replica_groups={{0,8},{16,24},{32,40},{48,56},{64,72},{80,88},{96,104},{112,120},{128,1..., dimensions={0}, use_global_device_ids=true | all-gather | bytes 491520 | tf_op jit(solution)/shard_map/all_gather | solution.py:188
  66.5 0.0 all-to-all-done.2.x_ref
  66.5 0.4 project.1
  67.0 12.4 %all_to_all.20 = f32[32,4,80]{2,1,0:T(4,128)S(1)} all-to-all(f32[32,4,80]{2,1,0:T(4,128)S(1)} %bitcast.22), channel_id=1, replica_groups={{5,6,7,0,1,2,3,4,13,14,15,8,9,10,11,12,21,22,23,16,17,18,19,20,29,30,31..., dimensions={0} | all-to-all | bytes 81920 | tf_op jit(solution)/shard_map/all_to_all | solution.py:249
  79.4 0.0 copy-done.3
  79.4 0.6 finish.1
  (7 shorter events, 0.0 us)
Async XLA Ops:
  0.0 11.8 %copy-start.2 = (bf16[2,1,8,128]{3,2,1,0:T(8,128)(2,1)S(1)}, bf16[2,1,8,128]{3,2,1,0:T(8,128)(2,1)}, u32[]{:S(2)}) copy-start(bf16[2,1,8,128]{3,2,1,0:T(8,128)(2,1)} %param.10) | copy-start | bytes 12292
  1.1 24.1 %collective-permute-start.1 = (bf16[2048,128]{1,0:T(8,128)(2,1)S(1)}, bf16[2048,128]{1,0:T(8,128)(2,1)S(1)}, u32[]{:S(2)}, u32[]{:S(2)}) collective-permute-start(bf16[2048,128]{1,0:T(8,128)(2,1)S(1)} %pad_maximum_fusion.kv_ref), channel_id=1, source_target_pairs={{0,16},{8,24},{16,0},{24,8},{32,48},{40,56},{48,32},{56,40},{64,80... | collective-permute-start | bytes 1572872 | tf_op jit(solution)/shard_map/ppermute | solution.py:182
  5.1 25.7 %collective-permute-start = (bf16[2048,128]{1,0:T(8,128)(2,1)S(1)}, bf16[2048,128]{1,0:T(8,128)(2,1)S(1)}, u32[]{:S(2)}, u32[]{:S(2)}) collective-permute-start(bf16[2048,128]{1,0:T(8,128)(2,1)S(1)} %pad_maximum_fusion.kv_ref), channel_id=1, source_target_pairs={{0,8},{8,0},{16,24},{24,16},{32,40},{40,32},{48,56},{56,48},{64,72... | collective-permute-start | bytes 1572872 | tf_op jit(solution)/shard_map/ppermute | solution.py:182
  12.5 18.3 %all-to-all-start = ((bf16[16,16,128]{2,1,0:T(8,128)(2,1)}), bf16[16,16,128]{2,1,0:T(8,128)(2,1)S(1)}, u32[]{:S(2)}, u32[]{:S(2)}) async-start(bf16[16,16,128]{2,1,0:T(8,128)(2,1)} %broadcast_in_dim.8), calls=%async_computation | async-start | bytes 131072 | tf_op jit(solution)/shard_map/all_to_all | solution.py:185
  30.8 13.2 %copy-start.6 = (bf16[1024,80]{0,1:T(8,128)(2,1)S(1)}, bf16[1024,80]{0,1:T(8,128)(2,1)}, u32[]{:S(2)}) copy-start(bf16[1024,80]{0,1:T(8,128)(2,1)} %param.18) | copy-start | bytes 491524
  30.8 15.9 %copy-start.1 = (bf16[1,512,1,128]{3,1,2,0:T(8,128)(2,1)S(1)}, bf16[1,512,1,128]{3,1,2,0:T(8,128)(2,1)}, u32[]{:S(2)}) copy-start(bf16[1,512,1,128]{3,1,2,0:T(8,128)(2,1)} %param.14) | copy-start | bytes 393220
  33.4 13.3 %copy-start = (bf16[1,512,1,128]{3,1,2,0:T(8,128)(2,1)S(1)}, bf16[1,512,1,128]{3,1,2,0:T(8,128)(2,1)}, u32[]{:S(2)}) copy-start(bf16[1,512,1,128]{3,1,2,0:T(8,128)(2,1)} %param.13) | copy-start | bytes 393220
  33.4 15.6 %all-to-all-start.1 = ((bf16[16,9,2,128]{3,2,1,0:T(2,128)(2,1)}), bf16[16,9,2,128]{3,2,1,0:T(2,128)(2,1)S(1)}, u32[]{:S(2)}, u32[]{:S(2)}) async-start(bf16[16,9,2,128]{3,2,1,0:T(2,128)(2,1)} %prefix_state.1), calls=%async_computation.1 | async-start | bytes 147456 | tf_op jit(solution)/shard_map/all_to_all | solution.py:185
  44.0 20.5 %collective-permute-start.2 = (bf16[80,1024]{1,0:T(8,128)(2,1)S(1)}, bf16[80,1024]{1,0:T(8,128)(2,1)S(1)}, u32[]{:S(2)}, u32[]{:S(2)}) collective-permute-start(bf16[80,1024]{1,0:T(8,128)(2,1)S(1)} %bitcast.31), channel_id=1, source_target_pairs={{0,16},{8,24},{16,0},{24,8},{32,48},{40,56},{48,32},{56,40},{64,80... | collective-permute-start | bytes 491528 | tf_op jit(solution)/shard_map/ppermute | solution.py:182
  46.7 0.7 copy-start.4
  46.7 0.7 copy-start.5
  50.1 16.5 %all-to-all-start.2 = ((bf16[16,16,128]{2,1,0:T(8,128)(2,1)}), bf16[16,16,128]{2,1,0:T(8,128)(2,1)S(1)}, u32[]{:S(2)}, u32[]{:S(2)}) async-start(bf16[16,16,128]{2,1,0:T(8,128)(2,1)} %combine.1), calls=%async_computation.2 | async-start | bytes 131072 | tf_op jit(solution)/shard_map/all_to_all | solution.py:185
  67.0 12.4 %copy-start.3 = (bf16[2,8,80]{2,1,0:T(8,128)(2,1)S(1)}, bf16[2,8,80]{2,1,0:T(8,128)(2,1)}, u32[]{:S(2)}) copy-start(bf16[2,8,80]{2,1,0:T(8,128)(2,1)} %residual_ref.1) | copy-start | bytes 7684

commit v5 on v3

--- a/solution.py
+++ b/solution.py
@@ -12,6 +12,8 @@
 BF16, F32 = jnp.bfloat16, jnp.float32
 SCALE = math.log2(math.e) / math.sqrt(128)
 NT = (((1,), (1,)), ((), ()))
+LINE_ORDER = [10, 9, 8, 7, 6, 5, 4, 3, 2, 1, 0, 15, 14, 13, 12, 11]
+SIDE_ORDER, HEAD_ORDER = [1, 2, 3, 0], [5, 6, 7, 0, 1, 2, 3, 4]
 
 
 def split_three(x):
@@ -37,7 +39,7 @@
 
 
 def prefix_kernel(q_ref, kv_ref, near_ref, fk_ref, fv_ref, out_ref):
-    key_block, row_block = 256, 256
+    key_block, row_block = 256, 128
     depth = kv_ref.shape[0] // 2
     starts = range(0, depth, key_block)
     shards = [
@@ -46,12 +48,17 @@
         (fk_ref.at[0], fv_ref.at[0]),
         (fk_ref.at[1], fv_ref.at[1]),
     ]
-    for at in range(q_ref.shape[0] // row_block):
-        q = q_ref[at * row_block : (at + 1) * row_block, :]
-        scores = [
-            lax.dot_general(q, k[i : i + key_block, :], NT, preferred_element_type=F32) for k, _ in shards for i in starts
+    spans = [slice(at, at + row_block) for at in range(0, q_ref.shape[0], row_block)]
+    values = [v[i : i + key_block, :] for _, v in shards for i in starts]
+    all_scores = [
+        [
+            lax.dot_general(q_ref[span, :], k[i : i + key_block, :], NT, preferred_element_type=F32)
+            for k, _ in shards
+            for i in starts
         ]
-        values = [v[i : i + key_block, :] for _, v in shards for i in starts]
+        for span in spans
+    ]
+    for span, scores in zip(spans, all_scores):
         highest = functools.reduce(jnp.maximum, scores).max(1, keepdims=True)
         totals, weighted = [], []
         for s, v in zip(scores, values):
@@ -60,7 +67,7 @@
             weighted.append(jnp.dot(p.astype(BF16), v, preferred_element_type=F32))
         total = functools.reduce(jnp.add, totals).sum(1, keepdims=True)
         weighted = functools.reduce(jnp.add, weighted)
-        first, count = at * row_block // 16, row_block // 16
+        first, count = span.start // 16, row_block // 16
         out_ref[first : first + count, 0:8] = weighted.astype(BF16).reshape(count, 8, 2, 128)
         lane = lax.broadcasted_iota(jnp.int32, (row_block, 128), 1)
         stats = jnp.zeros((row_block, 128), F32)
@@ -115,8 +122,9 @@
 def project_kernel(place_ref, x_ref, w_ref, far_ref, out_ref):
     samples, rows, hd = x_ref.shape
     group = w_ref.shape[2] // hd
-    heads = out_ref.shape[1]
-    x = x_ref[...].astype(F32).reshape(samples * rows // group, group, hd)
+    heads, chunk = out_ref.shape[1:3]
+    steps = rows // group
+    x = x_ref[...].astype(F32).reshape(samples * steps, group, hd)
     x = jnp.swapaxes(x, 0, 1).astype(BF16)
     side = place_ref[0] // 2 * 2
     for ref, at in ((w_ref, side), (far_ref, 2 - side)):
@@ -130,13 +138,19 @@
                     for g in range(group)
                 ],
             )
-            out_ref[at + core] = y.reshape(heads, -1, y.shape[1])
+            to = functools.reduce(jnp.add, [jnp.where(at + core == d, p, 0) for p, d in enumerate(SIDE_ORDER)])
+            for member, z in enumerate(LINE_ORDER):
+                shard, slot = divmod(z * heads, samples)
+                first = slot * chunk // samples
+                out_ref[to, HEAD_ORDER.index(shard), first : first + steps] = y[member * steps : (member + 1) * steps]
 
 
 def finish_kernel(terms_ref, residual_ref, out_ref):
     planes, heads = terms_ref.shape[:2]
     steps = residual_ref.shape[0]
-    sums = [functools.reduce(jnp.add, [terms_ref[d, h] for h in range(heads)]) for d in range(planes)]
+    sums = [
+        functools.reduce(jnp.add, [terms_ref[SIDE_ORDER.index(d), h] for h in range(heads)]) for d in range(planes)
+    ]
     for t in range(steps):
         rows = [sums[d][z * steps + t][None] for z in range(sums[0].shape[0] // steps) for d in range(planes)]
         out_ref[t] = (jnp.concatenate(rows, 0) + residual_ref[t].astype(F32)).astype(BF16)
@@ -167,10 +181,10 @@
     ctx = lax.axis_size("ctx")
     heads = lax.axis_size("head")
     depth = ctx // 4
-    lines = [[4 * z + j for z in range(depth)] for j in range(4)]
+    lines = [[4 * z + j for z in LINE_ORDER] for j in range(4)]
     halves = [[2 * i + core for i in range(ctx // 2)] for core in range(2)]
     pairs = [[2 * i, 2 * i + 1] for i in range(ctx // 2)]
-    planes = [[(4 * z + j) * heads + h for j in range(4) for h in range(heads)] for z in range(depth)]
+    planes = [[(4 * z + j) * heads + h for j in SIDE_ORDER for h in HEAD_ORDER] for z in range(depth)]
     place = lax.axis_index("ctx").astype(jnp.int32)
 
     def swap(x, bit):

time: 89.3 us -> 79.5 us (0.89)
  waiting for transfers between devices: 21.2 us -> 2.66 us
  starting transfers between devices: 32.4 us -> 46.3 us
  blocking collectives: 26.9 us -> 21.9 us
    all_to_all x3, waiting for transfers between devices: 21.2 us -> 2.65 us  [exchange(): return lax.all_to_all(x, 'ctx', 0, 0, axis_index_groups=groups, tiled=True)]
    all_to_all x3, starting transfers between devices: 19.6 us -> 33.5 us  [exchange(): return lax.all_to_all(x, 'ctx', 0, 0, axis_index_groups=groups, tiled=True)]
    all_to_all x1, blocking collectives: 17 us -> 12 us  [body(): lax.all_to_all(product, ('ctx', 'head'), 0, 0, axis_index_groups=planes,...]
  transfers between devices with their start and end apart: 6 -> 6, of which waited for: 3 -> 2; matrix products, arithmetic and copies ran while one was open for 1% -> 1% of each run, Pallas kernels for 2% -> 2%
where the time goes in v5:
time: 79.5 us; the launch traced here: 79 us
  starting transfers between devices  46.3 us (58%)
  blocking collectives  21.9 us (28%)
  Pallas kernels  4.99 us (6%)
  waiting for transfers between devices  2.66 us (3%)
  local copies, waits for them, and re-layouts  1.33 us (2%)
  other arithmetic  1.08 us (1%)
    all_to_all x3, starting transfers between devices, exchange(): return lax.all_to_all(x, 'ctx', 0, 0, axis_index_groups=groups, tiled=True)  33.5 us
    ppermute x3, starting transfers between devices, swap(): return lax.ppermute(x, 'ctx', [(i, i ^ bit) for i in range(ctx)])  12.8 us
    all_to_all x1, blocking collectives, body(): lax.all_to_all(product, ('ctx', 'head'), 0, 0, axis_index_groups=planes,...  12 us
    all_gather x4, blocking collectives, both(): return lax.all_gather(x, 'ctx', axis=0, axis_index_groups=pairs)  9.95 us
    all_to_all x3, waiting for transfers between devices, exchange(): return lax.all_to_all(x, 'ctx', 0, 0, axis_index_groups=groups, tiled=True)  2.65 us
    pallas_call x1, Pallas kernels, body(): pl.pallas_call(prefix_kernel, out_shape=jax.ShapeDtypeStruct((depth, rows...  2.46 us
  transfers between devices with their start and end apart: 6, of which 2 were waited for; matrix products, arithmetic and copies ran while one was open for 1% of the time, Pallas kernels for 2%

profile of v5, /device:TPU:1, one launch (start us, length us, event | category | flops | bytes accessed | tf_op | source)
XLA Modules:
  0.0 79.0 jit_solution(11460132071684819949)
XLA Ops:
  0.0 1.1 %pad_maximum_fusion.kv_ref = bf16[2048,128]{1,0:T(8,128)(2,1)S(1)} fusion(bf16[1024,128]{1,0:T(8,128)(2,1)} %bitcast.29, bf16[1024,128]{1,0:T(8,128)(2,1)} %bitcast.30), kind=kLoop, calls=%fused_computation | loop fusion | flops 1048576 | bytes 1048576 | tf_op jit(solution)/shard_map/concatenate | solution.py:200
  1.1 4.0 %collective-permute-start.1 = (bf16[2048,128]{1,0:T(8,128)(2,1)S(1)}, bf16[2048,128]{1,0:T(8,128)(2,1)S(1)}, u32[]{:S(2)}, u32[]{:S(2)}) collective-permute-start(bf16[2048,128]{1,0:T(8,128)(2,1)S(1)} %pad_maximum_fusion.kv_ref), channel_id=1, source_target_pairs={{0,16},{8,24},{16,0},{24,8},{32,48},{40,56},{48,32},{56,40},{64,80... | collective-permute-start | bytes 1572872 | tf_op jit(solution)/shard_map/ppermute | solution.py:191
  5.1 6.7 %collective-permute-start = (bf16[2048,128]{1,0:T(8,128)(2,1)S(1)}, bf16[2048,128]{1,0:T(8,128)(2,1)S(1)}, u32[]{:S(2)}, u32[]{:S(2)}) collective-permute-start(bf16[2048,128]{1,0:T(8,128)(2,1)S(1)} %pad_maximum_fusion.kv_ref), channel_id=1, source_target_pairs={{0,8},{8,0},{16,24},{24,16},{32,40},{40,32},{48,56},{56,48},{64,72... | collective-permute-start | bytes 1572872 | tf_op jit(solution)/shard_map/ppermute | solution.py:191
  11.8 0.0 copy-done.2
  11.8 0.6 broadcast_in_dim.8
  12.5 12.7 %all-to-all-start = ((bf16[16,16,128]{2,1,0:T(8,128)(2,1)}), bf16[16,16,128]{2,1,0:T(8,128)(2,1)S(1)}, u32[]{:S(2)}, u32[]{:S(2)}) async-start(bf16[16,16,128]{2,1,0:T(8,128)(2,1)} %broadcast_in_dim.8), calls=%async_computation | async-start | bytes 131072 | tf_op jit(solution)/shard_map/all_to_all | solution.py:194
  25.1 0.0 collective-permute-done.1
  25.2 2.4 %all-gather = bf16[2048,128]{1,0:T(8,128)(2,1)S(1)} all-gather(bf16[1024,128]{1,0:T(8,128)(2,1)S(1)} %get-tuple-element.12), channel_id=2, replica_groups={{0,8},{16,24},{32,40},{48,56},{64,72},{80,88},{96,104},{112,120},{128,1..., dimensions={0}, use_global_device_ids=true | all-gather | bytes 786432 | tf_op jit(solution)/shard_map/all_gather | solution.py:197
  27.6 2.2 %all-gather.1 = bf16[2048,128]{1,0:T(8,128)(2,1)S(1)} all-gather(bf16[1024,128]{1,0:T(8,128)(2,1)S(1)} %get-tuple-element.11), channel_id=3, replica_groups={{0,8},{16,24},{32,40},{48,56},{64,72},{80,88},{96,104},{112,120},{128,1..., dimensions={0}, use_global_device_ids=true | all-gather | bytes 786432 | tf_op jit(solution)/shard_map/all_gather | solution.py:197
  29.7 0.9 %all-to-all-done = bf16[16,16,128]{2,1,0:T(8,128)(2,1)S(1)} async-done(((bf16[16,16,128]{2,1,0:T(8,128)(2,1)}), bf16[16,16,128]{2,1,0:T(8,128)(2,1)S(1)}, u32[]{:S(2)}, u32[]{:S(2)}) %all-to-all-start) | async-done | bytes 65568 | tf_op jit(solution)/shard_map/all_to_all | solution.py:194
  30.6 0.0 collective-permute-done.near_ref
  30.6 2.5 %prefix_state.1 = bf16[16,9,2,128]{3,2,1,0:T(2,128)(2,1)} custom-call(bf16[256,128]{1,0:T(8,128)(2,1)S(1)} %bitcast.20, bf16[2048,128]{1,0:T(8,128)(2,1)S(1)} %pad_maximum_fusion.kv_ref, bf16[2048,128]{1,0:T(8,128)(2,1)S(1)} %collective-permute-done.near_ref, bf16[2,1024,128]{2,1,0:T(8,128)(2,1)S(1)} %bitcast.16, bf16[2,1024,128]{2,1,0:T(8,128)(2,1)S(1)} %bitcast.17), custom_call_target="tpu_custom_call" | custom-call | tf_op jit(solution)/shard_map/prefix_state/pallas_call | solution.py:224
  33.1 10.7 %all-to-all-start.1 = ((bf16[16,9,2,128]{3,2,1,0:T(2,128)(2,1)}), bf16[16,9,2,128]{3,2,1,0:T(2,128)(2,1)S(1)}, u32[]{:S(2)}, u32[]{:S(2)}) async-start(bf16[16,9,2,128]{3,2,1,0:T(2,128)(2,1)} %prefix_state.1), calls=%async_computation.1 | async-start | bytes 147456 | tf_op jit(solution)/shard_map/all_to_all | solution.py:194
  43.8 0.0 copy-done.6
  43.8 2.1 %collective-permute-start.2 = (bf16[80,1024]{1,0:T(8,128)(2,1)S(1)}, bf16[80,1024]{1,0:T(8,128)(2,1)S(1)}, u32[]{:S(2)}, u32[]{:S(2)}) collective-permute-start(bf16[80,1024]{1,0:T(8,128)(2,1)S(1)} %bitcast.31), channel_id=1, source_target_pairs={{0,16},{8,24},{16,0},{24,8},{32,48},{40,56},{48,32},{56,40},{64,80... | collective-permute-start | bytes 491528 | tf_op jit(solution)/shard_map/ppermute | solution.py:191
  46.6 0.0 copy-start.4
  46.6 0.0 copy-start.5
  46.6 0.0 copy-done.1
  46.6 0.6 copy-done.4
  47.2 0.0 copy-done.5
  47.2 0.4 suffix_state.1
  47.6 1.8 %all-to-all-done.1.got_ref = bf16[16,9,2,128]{3,2,1,0:T(2,128)(2,1)S(1)} async-done(((bf16[16,9,2,128]{3,2,1,0:T(2,128)(2,1)}), bf16[16,9,2,128]{3,2,1,0:T(2,128)(2,1)S(1)}, u32[]{:S(2)}, u32[]{:S(2)}) %all-to-all-start.1) | async-done | bytes 73760 | tf_op jit(solution)/shard_map/all_to_all | solution.py:194
  49.4 1.1 %combine.1 = bf16[16,16,128]{2,1,0:T(8,128)(2,1)} custom-call(bf16[16,9,2,128]{3,2,1,0:T(2,128)(2,1)S(1)} %all-to-all-done.1.got_ref, f32[16,128]{1,0:T(8,128)S(1)} %get-tuple-element.8.so_ref, f32[16,128]{1,0:T(8,128)S(1)} %get-tuple-element.9.sm_ref, f32[16,128]{1,0:T(8,128)S(1)} %get-tuple-element.10.sl_ref), custom_call_target="tpu_custom_call" | custom-call | tf_op jit(solution)/shard_map/combine/pallas_call | solution.py:238
  50.5 10.1 %all-to-all-start.2 = ((bf16[16,16,128]{2,1,0:T(8,128)(2,1)}), bf16[16,16,128]{2,1,0:T(8,128)(2,1)S(1)}, u32[]{:S(2)}, u32[]{:S(2)}) async-start(bf16[16,16,128]{2,1,0:T(8,128)(2,1)} %combine.1), calls=%async_computation.2 | async-start | bytes 131072 | tf_op jit(solution)/shard_map/all_to_all | solution.py:194
  60.5 3.4 %all-gather.2 = bf16[160,1024]{1,0:T(8,128)(2,1)S(1)} all-gather(bf16[80,1024]{1,0:T(8,128)(2,1)S(1)} %bitcast.32), channel_id=4, replica_groups={{0,8},{16,24},{32,40},{48,56},{64,72},{80,88},{96,104},{112,120},{128,1..., dimensions={0}, use_global_device_ids=true | all-gather | bytes 491520 | tf_op jit(solution)/shard_map/all_gather | solution.py:197
  63.9 0.0 collective-permute-done.2
  63.9 2.0 %all-gather.3 = bf16[160,1024]{1,0:T(8,128)(2,1)S(1)} all-gather(bf16[80,1024]{1,0:T(8,128)(2,1)S(1)} %collective-permute-done.2), channel_id=5, replica_groups={{0,8},{16,24},{32,40},{48,56},{64,72},{80,88},{96,104},{112,120},{128,1..., dimensions={0}, use_global_device_ids=true | all-gather | bytes 491520 | tf_op jit(solution)/shard_map/all_gather | solution.py:197
  65.9 0.0 all-to-all-done.2.x_ref
  65.9 0.5 project.1
  66.4 0.0 copy-start.3
  66.4 12.0 %all_to_all.20 = f32[32,4,80]{2,1,0:T(4,128)S(1)} all-to-all(f32[32,4,80]{2,1,0:T(4,128)S(1)} %bitcast.22), channel_id=1, replica_groups={{13,14,15,8,9,10,11,12,21,22,23,16,17,18,19,20,29,30,31,24,25,26,27,28,..., dimensions={0} | all-to-all | bytes 81920 | tf_op jit(solution)/shard_map/all_to_all | solution.py:258
  78.4 0.6 finish.1
  (7 shorter events, 0.0 us)
Async XLA Ops:
  0.0 11.8 %copy-start.2 = (bf16[2,1,8,128]{3,2,1,0:T(8,128)(2,1)S(1)}, bf16[2,1,8,128]{3,2,1,0:T(8,128)(2,1)}, u32[]{:S(2)}) copy-start(bf16[2,1,8,128]{3,2,1,0:T(8,128)(2,1)} %param.10) | copy-start | bytes 12292
  1.1 24.1 %collective-permute-start.1 = (bf16[2048,128]{1,0:T(8,128)(2,1)S(1)}, bf16[2048,128]{1,0:T(8,128)(2,1)S(1)}, u32[]{:S(2)}, u32[]{:S(2)}) collective-permute-start(bf16[2048,128]{1,0:T(8,128)(2,1)S(1)} %pad_maximum_fusion.kv_ref), channel_id=1, source_target_pairs={{0,16},{8,24},{16,0},{24,8},{32,48},{40,56},{48,32},{56,40},{64,80... | collective-permute-start | bytes 1572872 | tf_op jit(solution)/shard_map/ppermute | solution.py:191
  5.1 25.5 %collective-permute-start = (bf16[2048,128]{1,0:T(8,128)(2,1)S(1)}, bf16[2048,128]{1,0:T(8,128)(2,1)S(1)}, u32[]{:S(2)}, u32[]{:S(2)}) collective-permute-start(bf16[2048,128]{1,0:T(8,128)(2,1)S(1)} %pad_maximum_fusion.kv_ref), channel_id=1, source_target_pairs={{0,8},{8,0},{16,24},{24,16},{32,40},{40,32},{48,56},{56,48},{64,72... | collective-permute-start | bytes 1572872 | tf_op jit(solution)/shard_map/ppermute | solution.py:191
  12.5 18.2 %all-to-all-start = ((bf16[16,16,128]{2,1,0:T(8,128)(2,1)}), bf16[16,16,128]{2,1,0:T(8,128)(2,1)S(1)}, u32[]{:S(2)}, u32[]{:S(2)}) async-start(bf16[16,16,128]{2,1,0:T(8,128)(2,1)} %broadcast_in_dim.8), calls=%async_computation | async-start | bytes 131072 | tf_op jit(solution)/shard_map/all_to_all | solution.py:194
  30.6 13.2 %copy-start.6 = (bf16[1024,80]{0,1:T(8,128)(2,1)S(1)}, bf16[1024,80]{0,1:T(8,128)(2,1)}, u32[]{:S(2)}) copy-start(bf16[1024,80]{0,1:T(8,128)(2,1)} %param.18) | copy-start | bytes 491524
  30.6 15.9 %copy-start.1 = (bf16[1,512,1,128]{3,1,2,0:T(8,128)(2,1)S(1)}, bf16[1,512,1,128]{3,1,2,0:T(8,128)(2,1)}, u32[]{:S(2)}) copy-start(bf16[1,512,1,128]{3,1,2,0:T(8,128)(2,1)} %param.14) | copy-start | bytes 393220
  33.1 13.5 %copy-start = (bf16[1,512,1,128]{3,1,2,0:T(8,128)(2,1)S(1)}, bf16[1,512,1,128]{3,1,2,0:T(8,128)(2,1)}, u32[]{:S(2)}) copy-start(bf16[1,512,1,128]{3,1,2,0:T(8,128)(2,1)} %param.13) | copy-start | bytes 393220
  33.1 16.2 %all-to-all-start.1 = ((bf16[16,9,2,128]{3,2,1,0:T(2,128)(2,1)}), bf16[16,9,2,128]{3,2,1,0:T(2,128)(2,1)S(1)}, u32[]{:S(2)}, u32[]{:S(2)}) async-start(bf16[16,9,2,128]{3,2,1,0:T(2,128)(2,1)} %prefix_state.1), calls=%async_computation.1 | async-start | bytes 147456 | tf_op jit(solution)/shard_map/all_to_all | solution.py:194
  43.8 20.1 %collective-permute-start.2 = (bf16[80,1024]{1,0:T(8,128)(2,1)S(1)}, bf16[80,1024]{1,0:T(8,128)(2,1)S(1)}, u32[]{:S(2)}, u32[]{:S(2)}) collective-permute-start(bf16[80,1024]{1,0:T(8,128)(2,1)S(1)} %bitcast.31), channel_id=1, source_target_pairs={{0,16},{8,24},{16,0},{24,8},{32,48},{40,56},{48,32},{56,40},{64,80... | collective-permute-start | bytes 491528 | tf_op jit(solution)/shard_map/ppermute | solution.py:191
  46.6 0.7 copy-start.4
  46.6 0.7 copy-start.5
  50.5 15.5 %all-to-all-start.2 = ((bf16[16,16,128]{2,1,0:T(8,128)(2,1)}), bf16[16,16,128]{2,1,0:T(8,128)(2,1)S(1)}, u32[]{:S(2)}, u32[]{:S(2)}) async-start(bf16[16,16,128]{2,1,0:T(8,128)(2,1)} %combine.1), calls=%async_computation.2 | async-start | bytes 131072 | tf_op jit(solution)/shard_map/all_to_all | solution.py:194
  66.4 12.0 %copy-start.3 = (bf16[2,8,80]{2,1,0:T(8,128)(2,1)S(1)}, bf16[2,8,80]{2,1,0:T(8,128)(2,1)}, u32[]{:S(2)}) copy-start(bf16[2,8,80]{2,1,0:T(8,128)(2,1)} %residual_ref.1) | copy-start | bytes 7684

commit v6 on v5

--- a/solution.py
+++ b/solution.py
@@ -12,7 +12,7 @@
 BF16, F32 = jnp.bfloat16, jnp.float32
 SCALE = math.log2(math.e) / math.sqrt(128)
 NT = (((1,), (1,)), ((), ()))
-LINE_ORDER = [10, 9, 8, 7, 6, 5, 4, 3, 2, 1, 0, 15, 14, 13, 12, 11]
+LINE_ORDER = [11, 10, 12, 9, 13, 8, 14, 7, 15, 6, 0, 5, 1, 4, 2, 3]
 SIDE_ORDER, HEAD_ORDER = [1, 2, 3, 0], [5, 6, 7, 0, 1, 2, 3, 4]
 
 
@@ -142,14 +142,14 @@
             for member, z in enumerate(LINE_ORDER):
                 shard, slot = divmod(z * heads, samples)
                 first = slot * chunk // samples
-                out_ref[to, HEAD_ORDER.index(shard), first : first + steps] = y[member * steps : (member + 1) * steps]
+                out_ref[to, HEAD_ORDER.index(shard), first : first + steps] = y[member * steps : (member + 1) * steps].astype(BF16)
 
 
 def finish_kernel(terms_ref, residual_ref, out_ref):
     planes, heads = terms_ref.shape[:2]
     steps = residual_ref.shape[0]
     sums = [
-        functools.reduce(jnp.add, [terms_ref[SIDE_ORDER.index(d), h] for h in range(heads)]) for d in range(planes)
+        functools.reduce(jnp.add, [terms_ref[SIDE_ORDER.index(d), h].astype(F32) for h in range(heads)]) for d in range(planes)
     ]
     for t in range(steps):
         rows = [sums[d][z * steps + t][None] for z in range(sums[0].shape[0] // steps) for d in range(planes)]
@@ -248,7 +248,7 @@
     columns = weight.shape[0]
     product = pl.pallas_call(
         project_kernel,
-        out_shape=jax.ShapeDtypeStruct((4, heads, depth * steps // heads, columns), F32),
+        out_shape=jax.ShapeDtypeStruct((4, heads, depth * steps // heads, columns), BF16),
         in_specs=[SMEM] + vmem(3),
         out_specs=vmem(1)[0],
         compiler_params=PARAMS,

time: 79.5 us -> 79.4 us (level)
  starting transfers between devices: 46.3 us -> 43.8 us
  waiting for transfers between devices: 2.66 us -> 4.22 us
  blocking collectives: 21.9 us -> 22.7 us
    all_to_all x3, starting transfers between devices: 33.5 us -> 31 us  [exchange(): return lax.all_to_all(x, 'ctx', 0, 0, axis_index_groups=groups, tiled=True)]
    all_to_all x3, waiting for transfers between devices: 2.65 us -> 4.21 us  [exchange(): return lax.all_to_all(x, 'ctx', 0, 0, axis_index_groups=groups, tiled=True)]
where the time goes in v6:
time: 79.4 us; the launch traced here: 78.9 us
  starting transfers between devices  43.8 us (55%)
  blocking collectives  22.7 us (29%)
  Pallas kernels  4.98 us (6%)
  waiting for transfers between devices  4.22 us (5%)
  local copies, waits for them, and re-layouts  1.33 us (2%)
  other arithmetic  1.08 us (1%)
    all_to_all x3, starting transfers between devices, exchange(): return lax.all_to_all(x, 'ctx', 0, 0, axis_index_groups=groups, tiled=True)  31 us
    ppermute x3, starting transfers between devices, swap(): return lax.ppermute(x, 'ctx', [(i, i ^ bit) for i in range(ctx)])  12.8 us
    all_to_all x1, blocking collectives, body(): lax.all_to_all(product, ('ctx', 'head'), 0, 0, axis_index_groups=planes,...  12.4 us
    all_gather x4, blocking collectives, both(): return lax.all_gather(x, 'ctx', axis=0, axis_index_groups=pairs)  10.3 us
    all_to_all x3, waiting for transfers between devices, exchange(): return lax.all_to_all(x, 'ctx', 0, 0, axis_index_groups=groups, tiled=True)  4.21 us
    pallas_call x1, Pallas kernels, body(): pl.pallas_call(prefix_kernel, out_shape=jax.ShapeDtypeStruct((depth, rows...  2.45 us
  transfers between devices with their start and end apart: 6, of which 2 were waited for; matrix products, arithmetic and copies ran while one was open for 1% of the time, Pallas kernels for 2%

profile of v6, /device:TPU:1, one launch (start us, length us, event | category | flops | bytes accessed | tf_op | source)
XLA Modules:
  0.0 78.9 jit_solution(14128276262658681002)
XLA Ops:
  0.0 1.1 %pad_maximum_fusion.kv_ref = bf16[2048,128]{1,0:T(8,128)(2,1)S(1)} fusion(bf16[1024,128]{1,0:T(8,128)(2,1)} %bitcast.29, bf16[1024,128]{1,0:T(8,128)(2,1)} %bitcast.30), kind=kLoop, calls=%fused_computation | loop fusion | flops 1048576 | bytes 1048576 | tf_op jit(solution)/shard_map/concatenate | solution.py:200
  1.1 4.0 %collective-permute-start.1 = (bf16[2048,128]{1,0:T(8,128)(2,1)S(1)}, bf16[2048,128]{1,0:T(8,128)(2,1)S(1)}, u32[]{:S(2)}, u32[]{:S(2)}) collective-permute-start(bf16[2048,128]{1,0:T(8,128)(2,1)S(1)} %pad_maximum_fusion.kv_ref), channel_id=1, source_target_pairs={{0,16},{8,24},{16,0},{24,8},{32,48},{40,56},{48,32},{56,40},{64,80... | collective-permute-start | bytes 1572872 | tf_op jit(solution)/shard_map/ppermute | solution.py:191
  5.1 6.7 %collective-permute-start = (bf16[2048,128]{1,0:T(8,128)(2,1)S(1)}, bf16[2048,128]{1,0:T(8,128)(2,1)S(1)}, u32[]{:S(2)}, u32[]{:S(2)}) collective-permute-start(bf16[2048,128]{1,0:T(8,128)(2,1)S(1)} %pad_maximum_fusion.kv_ref), channel_id=1, source_target_pairs={{0,8},{8,0},{16,24},{24,16},{32,40},{40,32},{48,56},{56,48},{64,72... | collective-permute-start | bytes 1572872 | tf_op jit(solution)/shard_map/ppermute | solution.py:191
  11.8 0.0 copy-done.2
  11.8 0.6 broadcast_in_dim.8
  12.5 11.8 %all-to-all-start = ((bf16[16,16,128]{2,1,0:T(8,128)(2,1)}), bf16[16,16,128]{2,1,0:T(8,128)(2,1)S(1)}, u32[]{:S(2)}, u32[]{:S(2)}) async-start(bf16[16,16,128]{2,1,0:T(8,128)(2,1)} %broadcast_in_dim.8), calls=%async_computation | async-start | bytes 131072 | tf_op jit(solution)/shard_map/all_to_all | solution.py:194
  24.2 0.0 collective-permute-done.1
  24.3 2.4 %all-gather = bf16[2048,128]{1,0:T(8,128)(2,1)S(1)} all-gather(bf16[1024,128]{1,0:T(8,128)(2,1)S(1)} %get-tuple-element.12), channel_id=2, replica_groups={{0,8},{16,24},{32,40},{48,56},{64,72},{80,88},{96,104},{112,120},{128,1..., dimensions={0}, use_global_device_ids=true | all-gather | bytes 786432 | tf_op jit(solution)/shard_map/all_gather | solution.py:197
  26.7 2.2 %all-gather.1 = bf16[2048,128]{1,0:T(8,128)(2,1)S(1)} all-gather(bf16[1024,128]{1,0:T(8,128)(2,1)S(1)} %get-tuple-element.11), channel_id=3, replica_groups={{0,8},{16,24},{32,40},{48,56},{64,72},{80,88},{96,104},{112,120},{128,1..., dimensions={0}, use_global_device_ids=true | all-gather | bytes 786432 | tf_op jit(solution)/shard_map/all_gather | solution.py:197
  28.8 1.5 %all-to-all-done = bf16[16,16,128]{2,1,0:T(8,128)(2,1)S(1)} async-done(((bf16[16,16,128]{2,1,0:T(8,128)(2,1)}), bf16[16,16,128]{2,1,0:T(8,128)(2,1)S(1)}, u32[]{:S(2)}, u32[]{:S(2)}) %all-to-all-start) | async-done | bytes 65568 | tf_op jit(solution)/shard_map/all_to_all | solution.py:194
  30.4 0.0 collective-permute-done.near_ref
  30.4 2.4 %prefix_state.1 = bf16[16,9,2,128]{3,2,1,0:T(2,128)(2,1)} custom-call(bf16[256,128]{1,0:T(8,128)(2,1)S(1)} %bitcast.20, bf16[2048,128]{1,0:T(8,128)(2,1)S(1)} %pad_maximum_fusion.kv_ref, bf16[2048,128]{1,0:T(8,128)(2,1)S(1)} %collective-permute-done.near_ref, bf16[2,1024,128]{2,1,0:T(8,128)(2,1)S(1)} %bitcast.16, bf16[2,1024,128]{2,1,0:T(8,128)(2,1)S(1)} %bitcast.17), custom_call_target="tpu_custom_call" | custom-call | tf_op jit(solution)/shard_map/prefix_state/pallas_call | solution.py:224
  32.8 10.1 %all-to-all-start.1 = ((bf16[16,9,2,128]{3,2,1,0:T(2,128)(2,1)}), bf16[16,9,2,128]{3,2,1,0:T(2,128)(2,1)S(1)}, u32[]{:S(2)}, u32[]{:S(2)}) async-start(bf16[16,9,2,128]{3,2,1,0:T(2,128)(2,1)} %prefix_state.1), calls=%async_computation.1 | async-start | bytes 147456 | tf_op jit(solution)/shard_map/all_to_all | solution.py:194
  42.9 0.0 copy-done.6
  42.9 2.1 %collective-permute-start.2 = (bf16[80,1024]{1,0:T(8,128)(2,1)S(1)}, bf16[80,1024]{1,0:T(8,128)(2,1)S(1)}, u32[]{:S(2)}, u32[]{:S(2)}) collective-permute-start(bf16[80,1024]{1,0:T(8,128)(2,1)S(1)} %bitcast.31), channel_id=1, source_target_pairs={{0,16},{8,24},{16,0},{24,8},{32,48},{40,56},{48,32},{56,40},{64,80... | collective-permute-start | bytes 491528 | tf_op jit(solution)/shard_map/ppermute | solution.py:191
  45.7 0.0 copy-start.4
  45.7 0.0 copy-start.5
  45.7 0.0 copy-done.1
  45.7 0.0 copy-done
  45.7 0.6 copy-done.4
  46.3 0.0 copy-done.5
  46.3 0.4 suffix_state.1
  46.7 2.6 %all-to-all-done.1.got_ref = bf16[16,9,2,128]{3,2,1,0:T(2,128)(2,1)S(1)} async-done(((bf16[16,9,2,128]{3,2,1,0:T(2,128)(2,1)}), bf16[16,9,2,128]{3,2,1,0:T(2,128)(2,1)S(1)}, u32[]{:S(2)}, u32[]{:S(2)}) %all-to-all-start.1) | async-done | bytes 73760 | tf_op jit(solution)/shard_map/all_to_all | solution.py:194
  49.3 1.1 %combine.1 = bf16[16,16,128]{2,1,0:T(8,128)(2,1)} custom-call(bf16[16,9,2,128]{3,2,1,0:T(2,128)(2,1)S(1)} %all-to-all-done.1.got_ref, f32[16,128]{1,0:T(8,128)S(1)} %get-tuple-element.8.so_ref, f32[16,128]{1,0:T(8,128)S(1)} %get-tuple-element.9.sm_ref, f32[16,128]{1,0:T(8,128)S(1)} %get-tuple-element.10.sl_ref), custom_call_target="tpu_custom_call" | custom-call | tf_op jit(solution)/shard_map/combine/pallas_call | solution.py:238
  50.4 9.2 %all-to-all-start.2 = ((bf16[16,16,128]{2,1,0:T(8,128)(2,1)}), bf16[16,16,128]{2,1,0:T(8,128)(2,1)S(1)}, u32[]{:S(2)}, u32[]{:S(2)}) async-start(bf16[16,16,128]{2,1,0:T(8,128)(2,1)} %combine.1), calls=%async_computation.2 | async-start | bytes 131072 | tf_op jit(solution)/shard_map/all_to_all | solution.py:194
  59.6 3.7 %all-gather.2 = bf16[160,1024]{1,0:T(8,128)(2,1)S(1)} all-gather(bf16[80,1024]{1,0:T(8,128)(2,1)S(1)} %bitcast.32), channel_id=4, replica_groups={{0,8},{16,24},{32,40},{48,56},{64,72},{80,88},{96,104},{112,120},{128,1..., dimensions={0}, use_global_device_ids=true | all-gather | bytes 491520 | tf_op jit(solution)/shard_map/all_gather | solution.py:197
  63.3 0.0 collective-permute-done.2
  63.3 2.0 %all-gather.3 = bf16[160,1024]{1,0:T(8,128)(2,1)S(1)} all-gather(bf16[80,1024]{1,0:T(8,128)(2,1)S(1)} %collective-permute-done.2), channel_id=5, replica_groups={{0,8},{16,24},{32,40},{48,56},{64,72},{80,88},{96,104},{112,120},{128,1..., dimensions={0}, use_global_device_ids=true | all-gather | bytes 491520 | tf_op jit(solution)/shard_map/all_gather | solution.py:197
  65.3 0.0 all-to-all-done.2.x_ref
  65.4 0.5 project.1
  65.9 12.4 %all_to_all.20 = bf16[32,4,80]{2,1,0:T(4,128)(2,1)S(1)} all-to-all(bf16[32,4,80]{2,1,0:T(4,128)(2,1)S(1)} %bitcast.21), channel_id=1, replica_groups={{13,14,15,8,9,10,11,12,21,22,23,16,17,18,19,20,29,30,31,24,25,26,27,28,..., dimensions={0} | all-to-all | bytes 40960 | tf_op jit(solution)/shard_map/all_to_all | solution.py:258
  78.2 0.6 finish.1
  (7 shorter events, 0.0 us)
Async XLA Ops:
  0.0 11.8 %copy-start.2 = (bf16[2,1,8,128]{3,2,1,0:T(8,128)(2,1)S(1)}, bf16[2,1,8,128]{3,2,1,0:T(8,128)(2,1)}, u32[]{:S(2)}) copy-start(bf16[2,1,8,128]{3,2,1,0:T(8,128)(2,1)} %param.10) | copy-start | bytes 12292
  1.1 23.2 %collective-permute-start.1 = (bf16[2048,128]{1,0:T(8,128)(2,1)S(1)}, bf16[2048,128]{1,0:T(8,128)(2,1)S(1)}, u32[]{:S(2)}, u32[]{:S(2)}) collective-permute-start(bf16[2048,128]{1,0:T(8,128)(2,1)S(1)} %pad_maximum_fusion.kv_ref), channel_id=1, source_target_pairs={{0,16},{8,24},{16,0},{24,8},{32,48},{40,56},{48,32},{56,40},{64,80... | collective-permute-start | bytes 1572872 | tf_op jit(solution)/shard_map/ppermute | solution.py:191
  5.1 25.3 %collective-permute-start = (bf16[2048,128]{1,0:T(8,128)(2,1)S(1)}, bf16[2048,128]{1,0:T(8,128)(2,1)S(1)}, u32[]{:S(2)}, u32[]{:S(2)}) collective-permute-start(bf16[2048,128]{1,0:T(8,128)(2,1)S(1)} %pad_maximum_fusion.kv_ref), channel_id=1, source_target_pairs={{0,8},{8,0},{16,24},{24,16},{32,40},{40,32},{48,56},{56,48},{64,72... | collective-permute-start | bytes 1572872 | tf_op jit(solution)/shard_map/ppermute | solution.py:191
  12.5 17.9 %all-to-all-start = ((bf16[16,16,128]{2,1,0:T(8,128)(2,1)}), bf16[16,16,128]{2,1,0:T(8,128)(2,1)S(1)}, u32[]{:S(2)}, u32[]{:S(2)}) async-start(bf16[16,16,128]{2,1,0:T(8,128)(2,1)} %broadcast_in_dim.8), calls=%async_computation | async-start | bytes 131072 | tf_op jit(solution)/shard_map/all_to_all | solution.py:194
  30.4 12.5 %copy-start.6 = (bf16[1024,80]{0,1:T(8,128)(2,1)S(1)}, bf16[1024,80]{0,1:T(8,128)(2,1)}, u32[]{:S(2)}) copy-start(bf16[1024,80]{0,1:T(8,128)(2,1)} %param.18) | copy-start | bytes 491524
  30.4 15.3 %copy-start.1 = (bf16[1,512,1,128]{3,1,2,0:T(8,128)(2,1)S(1)}, bf16[1,512,1,128]{3,1,2,0:T(8,128)(2,1)}, u32[]{:S(2)}) copy-start(bf16[1,512,1,128]{3,1,2,0:T(8,128)(2,1)} %param.14) | copy-start | bytes 393220
  32.8 12.9 %copy-start = (bf16[1,512,1,128]{3,1,2,0:T(8,128)(2,1)S(1)}, bf16[1,512,1,128]{3,1,2,0:T(8,128)(2,1)}, u32[]{:S(2)}) copy-start(bf16[1,512,1,128]{3,1,2,0:T(8,128)(2,1)} %param.13) | copy-start | bytes 393220
  32.8 16.5 %all-to-all-start.1 = ((bf16[16,9,2,128]{3,2,1,0:T(2,128)(2,1)}), bf16[16,9,2,128]{3,2,1,0:T(2,128)(2,1)S(1)}, u32[]{:S(2)}, u32[]{:S(2)}) async-start(bf16[16,9,2,128]{3,2,1,0:T(2,128)(2,1)} %prefix_state.1), calls=%async_computation.1 | async-start | bytes 147456 | tf_op jit(solution)/shard_map/all_to_all | solution.py:194
  42.9 20.4 %collective-permute-start.2 = (bf16[80,1024]{1,0:T(8,128)(2,1)S(1)}, bf16[80,1024]{1,0:T(8,128)(2,1)S(1)}, u32[]{:S(2)}, u32[]{:S(2)}) collective-permute-start(bf16[80,1024]{1,0:T(8,128)(2,1)S(1)} %bitcast.31), channel_id=1, source_target_pairs={{0,16},{8,24},{16,0},{24,8},{32,48},{40,56},{48,32},{56,40},{64,80... | collective-permute-start | bytes 491528 | tf_op jit(solution)/shard_map/ppermute | solution.py:191
  45.7 0.7 copy-start.4
  45.7 0.7 copy-start.5
  50.4 14.9 %all-to-all-start.2 = ((bf16[16,16,128]{2,1,0:T(8,128)(2,1)}), bf16[16,16,128]{2,1,0:T(8,128)(2,1)S(1)}, u32[]{:S(2)}, u32[]{:S(2)}) async-start(bf16[16,16,128]{2,1,0:T(8,128)(2,1)} %combine.1), calls=%async_computation.2 | async-start | bytes 131072 | tf_op jit(solution)/shard_map/all_to_all | solution.py:194
  65.4 12.9 %copy-start.3 = (bf16[2,8,80]{2,1,0:T(8,128)(2,1)S(1)}, bf16[2,8,80]{2,1,0:T(8,128)(2,1)}, u32[]{:S(2)}) copy-start(bf16[2,8,80]{2,1,0:T(8,128)(2,1)} %residual_ref.1) | copy-start | bytes 7684

commit v7 on v5

--- a/solution.py
+++ b/solution.py
@@ -12,6 +12,7 @@
 BF16, F32 = jnp.bfloat16, jnp.float32
 SCALE = math.log2(math.e) / math.sqrt(128)
 NT = (((1,), (1,)), ((), ()))
+EARLY_Z = 5
 LINE_ORDER = [10, 9, 8, 7, 6, 5, 4, 3, 2, 1, 0, 15, 14, 13, 12, 11]
 SIDE_ORDER, HEAD_ORDER = [1, 2, 3, 0], [5, 6, 7, 0, 1, 2, 3, 4]
 
@@ -38,26 +39,70 @@
     return rows
 
 
-def prefix_kernel(q_ref, kv_ref, near_ref, fk_ref, fv_ref, out_ref):
+def hand_on_kernel(_, out_ref):
+    out_ref[...] = jnp.zeros_like(out_ref)
+
+
+def untouched_kernel(_, out_ref):
+    pass
+
+
+def prefix_kernel(
+    early_ref, q_ref, kv_ref, early_near_ref, late_near_ref, fk_ref, fv_ref, out_ref, near_ref, sems
+):
+    depth = kv_ref.shape[0] // 2
+    k_ref, v_ref = kv_ref.at[0:depth], kv_ref.at[depth : 2 * depth]
+
+    def moves(source):
+        return [
+            pltpu.make_async_copy(source.at[part], near_ref.at[part], sems.at[i])
+            for i, part in enumerate((pl.ds(0, depth), pl.ds(depth, depth)))
+        ]
+
+    @pl.when(early_ref[0] > 0)
+    def _():
+        for move in moves(early_near_ref):
+            move.start()
+
+    @pl.when(early_ref[0] <= 0)
+    def _():
+        for move in moves(late_near_ref):
+            move.start()
+
+    def arrived():
+        @pl.when(early_ref[0] > 0)
+        def _():
+            for move in moves(early_near_ref):
+                move.wait()
+
+        @pl.when(early_ref[0] <= 0)
+        def _():
+            for move in moves(late_near_ref):
+                move.wait()
+
+    prefix_state(q_ref, k_ref, v_ref, near_ref, fk_ref, fv_ref, out_ref, arrived)
+
+
+def prefix_state(q_ref, k_ref, v_ref, near_ref, fk_ref, fv_ref, out_ref, arrived):
     key_block, row_block = 256, 128
-    depth = kv_ref.shape[0] // 2
+    depth = k_ref.shape[0]
     starts = range(0, depth, key_block)
     shards = [
-        (kv_ref.at[0:depth], kv_ref.at[depth : 2 * depth]),
-        (near_ref.at[0:depth], near_ref.at[depth : 2 * depth]),
+        (k_ref, v_ref),
         (fk_ref.at[0], fv_ref.at[0]),
         (fk_ref.at[1], fv_ref.at[1]),
+        (near_ref.at[0:depth], near_ref.at[depth : 2 * depth]),
     ]
     spans = [slice(at, at + row_block) for at in range(0, q_ref.shape[0], row_block)]
+    def score(span, k):
+        return [
+            lax.dot_general(q_ref[span, :], k[i : i + key_block, :], NT, preferred_element_type=F32) for i in starts
+        ]
+
+    held = [[s for k, _ in shards[:-1] for s in score(span, k)] for span in spans]
+    arrived()
+    all_scores = [scores + score(span, shards[-1][0]) for span, scores in zip(spans, held)]
     values = [v[i : i + key_block, :] for _, v in shards for i in starts]
-    all_scores = [
-        [
-            lax.dot_general(q_ref[span, :], k[i : i + key_block, :], NT, preferred_element_type=F32)
-            for k, _ in shards
-            for i in starts
-        ]
-        for span in spans
-    ]
     for span, scores in zip(spans, all_scores):
         highest = functools.reduce(jnp.maximum, scores).max(1, keepdims=True)
         totals, weighted = [], []
@@ -190,6 +235,28 @@
     def swap(x, bit):
         return lax.ppermute(x, "ctx", [(i, i ^ bit) for i in range(ctx)])
 
+    def early_swap(x):
+        near = swap(x, 1)
+        after = pl.pallas_call(
+            hand_on_kernel,
+            out_shape=jax.ShapeDtypeStruct((rows, hd), BF16),
+            in_specs=[pl.BlockSpec(memory_space=pl.ANY)],
+            out_specs=vmem(1)[0],
+            compiler_params=PARAMS,
+            name="hand_on",
+        )(near)
+        return near, after
+
+    def untouched(x):
+        return pl.pallas_call(
+            untouched_kernel,
+            out_shape=jax.ShapeDtypeStruct(x.shape, x.dtype),
+            in_specs=[pl.BlockSpec(memory_space=pl.ANY)],
+            out_specs=pl.BlockSpec(memory_space=pl.ANY),
+            compiler_params=PARAMS,
+            name="untouched",
+        )(x)
+
     def exchange(x, groups):
         return lax.all_to_all(x, "ctx", 0, 0, axis_index_groups=groups, tiled=True)
 
@@ -199,9 +266,11 @@
     query_rows = queries.reshape(rows, hd)
     kv = jnp.concatenate([prefix_keys.reshape(-1, hd), prefix_values.reshape(-1, hd)], 0)
     far = swap(kv, 2)
-    near = swap(kv, 1)
-    copies = jnp.broadcast_to(query_rows[None], (depth, rows, hd))
+    early = place // 4 < EARLY_Z
+    early_near, nothing = lax.cond(early, early_swap, lambda x: (untouched(x), jnp.zeros((rows, hd), BF16)), kv)
+    copies = jnp.broadcast_to((query_rows + nothing)[None], (depth, rows, hd))
     line_queries = exchange(copies, lines).reshape(depth * rows, hd)
+    late_near = lax.cond(early, lambda x: untouched(x), lambda x: swap(x, 1), kv)
     half = kv.shape[0] // 2
     far_keys, far_values = both(far[:half]), both(far[half:])
 
@@ -224,11 +293,12 @@
     partial = pl.pallas_call(
         prefix_kernel,
         out_shape=jax.ShapeDtypeStruct((depth, rows // 2 + 1, 2, hd), BF16),
-        in_specs=vmem(5),
+        in_specs=[SMEM] + vmem(2) + [pl.BlockSpec(memory_space=pl.ANY)] * 2 + vmem(2),
         out_specs=vmem(1)[0],
+        scratch_shapes=[pltpu.VMEM(kv.shape, BF16), pltpu.SemaphoreType.DMA((2,))],
         compiler_params=PARAMS,
         name="prefix_state",
-    )(line_queries, kv, near, far_keys, far_values)
+    )(early.astype(jnp.int32).reshape(1), line_queries, kv, early_near, late_near, far_keys, far_values)
     received = exchange(partial, lines)
 
     weight = out_weight.T

time: 79.5 us -> 79.4 us (level)
  blocking collectives: 21.9 us -> 21 us
  Pallas kernels: 4.99 us -> 5.86 us
    all_to_all x3, waiting for transfers between devices: 2.65 us -> 0.21 us  [exchange(): return lax.all_to_all(x, 'ctx', 0, 0, axis_index_groups=groups, tiled=True)]
    ppermute x3, waiting for transfers between devices: 0.01 us -> 1.65 us  [swap(): return lax.ppermute(x, 'ctx', [(i, i ^ bit) for i in range(ctx)])]
    ppermute x3, starting transfers between devices: 12.8 us -> 14.4 us  [swap(): return lax.ppermute(x, 'ctx', [(i, i ^ bit) for i in range(ctx)])]
    all_to_all x1, blocking collectives: 12 us -> 10.7 us  [body(): lax.all_to_all(product, ('ctx', 'head'), 0, 0, axis_index_groups=planes,...]
    all_to_all x3, starting transfers between devices: 33.5 us -> 32.6 us  [exchange(): return lax.all_to_all(x, 'ctx', 0, 0, axis_index_groups=groups, tiled=True)]
    pallas_call x1, Pallas kernels: 2.46 us -> 3.35 us  [body(): pl.pallas_call(prefix_kernel, out_shape=jax.ShapeDtypeStruct((depth, rows...]
where the time goes in v7:
time: 79.4 us; the launch traced here: 78.9 us
  starting transfers between devices  46.9 us (59%)
  blocking collectives  21 us (26%)
  Pallas kernels  5.86 us (7%)
  waiting for transfers between devices  1.87 us (2%)
  local copies, waits for them, and re-layouts  1.34 us (2%)
  other arithmetic  1.07 us (1%)
    all_to_all x3, starting transfers between devices, exchange(): return lax.all_to_all(x, 'ctx', 0, 0, axis_index_groups=groups, tiled=True)  32.6 us
    ppermute x3, starting transfers between devices, swap(): return lax.ppermute(x, 'ctx', [(i, i ^ bit) for i in range(ctx)])  14.4 us
    all_to_all x1, blocking collectives, body(): lax.all_to_all(product, ('ctx', 'head'), 0, 0, axis_index_groups=planes,...  10.7 us
    all_gather x4, blocking collectives, both(): return lax.all_gather(x, 'ctx', axis=0, axis_index_groups=pairs)  10.4 us
    pallas_call x1, Pallas kernels, body(): pl.pallas_call(prefix_kernel, out_shape=jax.ShapeDtypeStruct((depth, rows...  3.35 us
    ppermute x3, waiting for transfers between devices, swap(): return lax.ppermute(x, 'ctx', [(i, i ^ bit) for i in range(ctx)])  1.65 us
  transfers between devices with their start and end apart: 6, of which 2 were waited for; matrix products, arithmetic and copies ran while one was open for 1% of the time, Pallas kernels for 2%

profile of v7, /device:TPU:1, one launch (start us, length us, event | category | flops | bytes accessed | tf_op | source)
XLA Modules:
  0.0 78.9 jit_solution(1492154806998328235)
XLA Ops:
  0.0 1.1 %pad_maximum_fusion.kv_ref = bf16[2048,128]{1,0:T(8,128)(2,1)S(1)} fusion(bf16[1024,128]{1,0:T(8,128)(2,1)} %bitcast.30, bf16[1024,128]{1,0:T(8,128)(2,1)} %bitcast.31), kind=kLoop, calls=%fused_computation | loop fusion | flops 1048576 | bytes 1048576 | tf_op jit(solution)/shard_map/concatenate | solution.py:267
  1.1 4.0 %collective-permute-start.2 = (bf16[2048,128]{1,0:T(8,128)(2,1)S(1)}, bf16[2048,128]{1,0:T(8,128)(2,1)S(1)}, u32[]{:S(2)}, u32[]{:S(2)}) collective-permute-start(bf16[2048,128]{1,0:T(8,128)(2,1)S(1)} %pad_maximum_fusion.kv_ref), channel_id=1, source_target_pairs={{0,16},{8,24},{16,0},{24,8},{32,48},{40,56},{48,32},{56,40},{64,80... | collective-permute-start | bytes 1572872 | tf_op jit(solution)/shard_map/ppermute | solution.py:236
  5.1 0.0 copy-start.2
  5.1 8.4 %conditional.2 = (bf16[2048,128]{1,0:T(8,128)(2,1)}, bf16[16,128]{1,0:T(8,128)(2,1)S(1)}) conditional(s32[]{:T(128)} %convert_element_type.2, bf16[2048,128]{1,0:T(8,128)(2,1)S(1)} %pad_maximum_fusion.kv_ref, bf16[2048,128]{1,0:T(8,128)(2,1)S(1)} %pad_maximum_fusion.kv_ref), branch_computations={%region_0.1_spmd, %region_1.2_spmd} | conditional | bytes 2097208 | solution.py:270
  5.2 6.7 %collective-permute-start = (bf16[2048,128]{1,0:T(8,128)(2,1)S(1)}, bf16[2048,128]{1,0:T(8,128)(2,1)}, u32[]{:S(2)}, u32[]{:S(2)}) collective-permute-start(bf16[2048,128]{1,0:T(8,128)(2,1)S(1)} %param.1), channel_id=1, source_target_pairs={{0,8},{8,0},{16,24},{24,16},{32,40},{40,32},{48,56},{56,48},{64,72... | collective-permute-start | bytes 1572872 | tf_op jit(solution)/shard_map/cond/branch_1_fun/ppermute | solution.py:236
  11.8 1.6 %collective-permute-done._ = bf16[2048,128]{1,0:T(8,128)(2,1)} collective-permute-done((bf16[2048,128]{1,0:T(8,128)(2,1)S(1)}, bf16[2048,128]{1,0:T(8,128)(2,1)}, u32[]{:S(2)}, u32[]{:S(2)}) %collective-permute-start) | collective-permute-done | bytes 524320 | tf_op jit(solution)/shard_map/cond/branch_1_fun/ppermute | solution.py:236
  13.5 0.6 broadcast_in_dim.2
  14.1 9.7 %all-to-all-start = ((bf16[16,16,128]{2,1,0:T(8,128)(2,1)}), bf16[16,16,128]{2,1,0:T(8,128)(2,1)S(1)}, u32[]{:S(2)}, u32[]{:S(2)}) async-start(bf16[16,16,128]{2,1,0:T(8,128)(2,1)} %broadcast_in_dim.2), calls=%async_computation | async-start | bytes 131072 | tf_op jit(solution)/shard_map/all_to_all | solution.py:261
  23.8 0.0 collective-permute-done.2
  23.9 2.7 %all-gather = bf16[2048,128]{1,0:T(8,128)(2,1)S(1)} all-gather(bf16[1024,128]{1,0:T(8,128)(2,1)S(1)} %get-tuple-element.23), channel_id=2, replica_groups={{0,8},{16,24},{32,40},{48,56},{64,72},{80,88},{96,104},{112,120},{128,1..., dimensions={0}, use_global_device_ids=true | all-gather | bytes 786432 | tf_op jit(solution)/shard_map/all_gather | solution.py:264
  26.6 2.2 %all-gather.1 = bf16[2048,128]{1,0:T(8,128)(2,1)S(1)} all-gather(bf16[1024,128]{1,0:T(8,128)(2,1)S(1)} %get-tuple-element.22), channel_id=3, replica_groups={{0,8},{16,24},{32,40},{48,56},{64,72},{80,88},{96,104},{112,120},{128,1..., dimensions={0}, use_global_device_ids=true | all-gather | bytes 786432 | tf_op jit(solution)/shard_map/all_gather | solution.py:264
  28.8 0.0 all-to-all-done
  28.8 3.3 %prefix_state.1 = bf16[16,9,2,128]{3,2,1,0:T(2,128)(2,1)} custom-call(s32[1]{0:T(128)} %bitcast.1.early_ref, bf16[256,128]{1,0:T(8,128)(2,1)S(1)} %bitcast.22, bf16[2048,128]{1,0:T(8,128)(2,1)S(1)} %pad_maximum_fusion.kv_ref, bf16[2048,128]{1,0:T(8,128)(2,1)} %get-tuple-element.18.early_near_ref, bf16[2048,128]{1,0:T(8,128)(2,1)S(1)} %get-tuple-element.28.late_near_ref, ...), custom_call_target="tpu_custom_call" | custom-call | tf_op jit(solution)/shard_map/prefix_state/pallas_call | solution.py:293
  32.2 0.0 copy-start
  32.2 11.6 %all-to-all-start.1 = ((bf16[16,9,2,128]{3,2,1,0:T(2,128)(2,1)}), bf16[16,9,2,128]{3,2,1,0:T(2,128)(2,1)S(1)}, u32[]{:S(2)}, u32[]{:S(2)}) async-start(bf16[16,9,2,128]{3,2,1,0:T(2,128)(2,1)} %prefix_state.1), calls=%async_computation.1 | async-start | bytes 147456 | tf_op jit(solution)/shard_map/all_to_all | solution.py:261
  43.8 3.6 %collective-permute-start.3 = (bf16[80,1024]{1,0:T(8,128)(2,1)S(1)}, bf16[80,1024]{1,0:T(8,128)(2,1)S(1)}, u32[]{:S(2)}, u32[]{:S(2)}) collective-permute-start(bf16[80,1024]{1,0:T(8,128)(2,1)S(1)} %bitcast.32), channel_id=1, source_target_pairs={{0,16},{8,24},{16,0},{24,8},{32,48},{40,56},{48,32},{56,40},{64,80... | collective-permute-start | bytes 491528 | tf_op jit(solution)/shard_map/ppermute | solution.py:236
  48.1 0.0 copy-start.4
  48.1 0.0 copy-start.5
  48.1 0.6 copy-done.4
  48.7 0.0 copy-done.5
  48.8 0.4 suffix_state.1
  49.1 0.2 all-to-all-done.1.got_ref
  49.3 1.1 %combine.1 = bf16[16,16,128]{2,1,0:T(8,128)(2,1)} custom-call(bf16[16,9,2,128]{3,2,1,0:T(2,128)(2,1)S(1)} %all-to-all-done.1.got_ref, f32[16,128]{1,0:T(8,128)S(1)} %get-tuple-element.19.so_ref, f32[16,128]{1,0:T(8,128)S(1)} %get-tuple-element.20.sm_ref, f32[16,128]{1,0:T(8,128)S(1)} %get-tuple-element.21.sl_ref), custom_call_target="tpu_custom_call" | custom-call | tf_op jit(solution)/shard_map/combine/pallas_call | solution.py:308
  50.4 11.3 %all-to-all-start.2 = ((bf16[16,16,128]{2,1,0:T(8,128)(2,1)}), bf16[16,16,128]{2,1,0:T(8,128)(2,1)S(1)}, u32[]{:S(2)}, u32[]{:S(2)}) async-start(bf16[16,16,128]{2,1,0:T(8,128)(2,1)} %combine.1), calls=%async_computation.2 | async-start | bytes 131072 | tf_op jit(solution)/shard_map/all_to_all | solution.py:261
  61.7 3.4 %all-gather.2 = bf16[160,1024]{1,0:T(8,128)(2,1)S(1)} all-gather(bf16[80,1024]{1,0:T(8,128)(2,1)S(1)} %bitcast.33), channel_id=4, replica_groups={{0,8},{16,24},{32,40},{48,56},{64,72},{80,88},{96,104},{112,120},{128,1..., dimensions={0}, use_global_device_ids=true | all-gather | bytes 491520 | tf_op jit(solution)/shard_map/all_gather | solution.py:264
  65.1 0.0 collective-permute-done.3
  65.1 2.0 %all-gather.3 = bf16[160,1024]{1,0:T(8,128)(2,1)S(1)} all-gather(bf16[80,1024]{1,0:T(8,128)(2,1)S(1)} %collective-permute-done.3), channel_id=5, replica_groups={{0,8},{16,24},{32,40},{48,56},{64,72},{80,88},{96,104},{112,120},{128,1..., dimensions={0}, use_global_device_ids=true | all-gather | bytes 491520 | tf_op jit(solution)/shard_map/all_gather | solution.py:264
  67.1 0.0 all-to-all-done.2.x_ref
  67.1 0.5 project.1
  67.6 0.0 copy-start.3
  67.6 10.7 %all_to_all.20 = f32[32,4,80]{2,1,0:T(4,128)S(1)} all-to-all(f32[32,4,80]{2,1,0:T(4,128)S(1)} %bitcast.24), channel_id=1, replica_groups={{13,14,15,8,9,10,11,12,21,22,23,16,17,18,19,20,29,30,31,24,25,26,27,28,..., dimensions={0} | all-to-all | bytes 81920 | tf_op jit(solution)/shard_map/all_to_all | solution.py:328
  78.3 0.6 finish.1
  (12 shorter events, 0.1 us)
Async XLA Ops:
  1.1 22.8 %collective-permute-start.2 = (bf16[2048,128]{1,0:T(8,128)(2,1)S(1)}, bf16[2048,128]{1,0:T(8,128)(2,1)S(1)}, u32[]{:S(2)}, u32[]{:S(2)}) collective-permute-start(bf16[2048,128]{1,0:T(8,128)(2,1)S(1)} %pad_maximum_fusion.kv_ref), channel_id=1, source_target_pairs={{0,16},{8,24},{16,0},{24,8},{32,48},{40,56},{48,32},{56,40},{64,80... | collective-permute-start | bytes 1572872 | tf_op jit(solution)/shard_map/ppermute | solution.py:236
  5.1 8.4 %copy-start.2 = (bf16[2,1,8,128]{3,2,1,0:T(8,128)(2,1)S(1)}, bf16[2,1,8,128]{3,2,1,0:T(8,128)(2,1)}, u32[]{:S(2)}) copy-start(bf16[2,1,8,128]{3,2,1,0:T(8,128)(2,1)} %param.14) | copy-start | bytes 12292
  5.2 8.3 %collective-permute-start = (bf16[2048,128]{1,0:T(8,128)(2,1)S(1)}, bf16[2048,128]{1,0:T(8,128)(2,1)}, u32[]{:S(2)}, u32[]{:S(2)}) collective-permute-start(bf16[2048,128]{1,0:T(8,128)(2,1)S(1)} %param.1), channel_id=1, source_target_pairs={{0,8},{8,0},{16,24},{24,16},{32,40},{40,32},{48,56},{56,48},{64,72... | collective-permute-start | bytes 1572872 | tf_op jit(solution)/shard_map/cond/branch_1_fun/ppermute | solution.py:236
  14.1 14.7 %all-to-all-start = ((bf16[16,16,128]{2,1,0:T(8,128)(2,1)}), bf16[16,16,128]{2,1,0:T(8,128)(2,1)S(1)}, u32[]{:S(2)}, u32[]{:S(2)}) async-start(bf16[16,16,128]{2,1,0:T(8,128)(2,1)} %broadcast_in_dim.2), calls=%async_computation | async-start | bytes 131072 | tf_op jit(solution)/shard_map/all_to_all | solution.py:261
  28.8 14.9 %copy-start.6 = (bf16[1024,80]{0,1:T(8,128)(2,1)S(1)}, bf16[1024,80]{0,1:T(8,128)(2,1)}, u32[]{:S(2)}) copy-start(bf16[1024,80]{0,1:T(8,128)(2,1)} %param.22) | copy-start | bytes 491524
  28.8 19.3 %copy-start.1 = (bf16[1,512,1,128]{3,1,2,0:T(8,128)(2,1)S(1)}, bf16[1,512,1,128]{3,1,2,0:T(8,128)(2,1)}, u32[]{:S(2)}) copy-start(bf16[1,512,1,128]{3,1,2,0:T(8,128)(2,1)} %param.18) | copy-start | bytes 393220
  32.2 15.9 %copy-start = (bf16[1,512,1,128]{3,1,2,0:T(8,128)(2,1)S(1)}, bf16[1,512,1,128]{3,1,2,0:T(8,128)(2,1)}, u32[]{:S(2)}) copy-start(bf16[1,512,1,128]{3,1,2,0:T(8,128)(2,1)} %param.17) | copy-start | bytes 393220
  32.2 17.1 %all-to-all-start.1 = ((bf16[16,9,2,128]{3,2,1,0:T(2,128)(2,1)}), bf16[16,9,2,128]{3,2,1,0:T(2,128)(2,1)S(1)}, u32[]{:S(2)}, u32[]{:S(2)}) async-start(bf16[16,9,2,128]{3,2,1,0:T(2,128)(2,1)} %prefix_state.1), calls=%async_computation.1 | async-start | bytes 147456 | tf_op jit(solution)/shard_map/all_to_all | solution.py:261
  43.8 21.3 %collective-permute-start.3 = (bf16[80,1024]{1,0:T(8,128)(2,1)S(1)}, bf16[80,1024]{1,0:T(8,128)(2,1)S(1)}, u32[]{:S(2)}, u32[]{:S(2)}) collective-permute-start(bf16[80,1024]{1,0:T(8,128)(2,1)S(1)} %bitcast.32), channel_id=1, source_target_pairs={{0,16},{8,24},{16,0},{24,8},{32,48},{40,56},{48,32},{56,40},{64,80... | collective-permute-start | bytes 491528 | tf_op jit(solution)/shard_map/ppermute | solution.py:236
  48.1 0.7 copy-start.4
  48.1 0.7 copy-start.5
  50.4 16.8 %all-to-all-start.2 = ((bf16[16,16,128]{2,1,0:T(8,128)(2,1)}), bf16[16,16,128]{2,1,0:T(8,128)(2,1)S(1)}, u32[]{:S(2)}, u32[]{:S(2)}) async-start(bf16[16,16,128]{2,1,0:T(8,128)(2,1)} %combine.1), calls=%async_computation.2 | async-start | bytes 131072 | tf_op jit(solution)/shard_map/all_to_all | solution.py:261
  67.6 10.7 %copy-start.3 = (bf16[2,8,80]{2,1,0:T(8,128)(2,1)S(1)}, bf16[2,8,80]{2,1,0:T(8,128)(2,1)}, u32[]{:S(2)}) copy-start(bf16[2,8,80]{2,1,0:T(8,128)(2,1)} %residual_ref.1) | copy-start | bytes 7684

commit v8 on v7

--- a/solution.py
+++ b/solution.py
@@ -13,7 +13,7 @@
 SCALE = math.log2(math.e) / math.sqrt(128)
 NT = (((1,), (1,)), ((), ()))
 EARLY_Z = 5
-LINE_ORDER = [10, 9, 8, 7, 6, 5, 4, 3, 2, 1, 0, 15, 14, 13, 12, 11]
+LINE_ORDER = [11, 10, 9, 8, 7, 6, 5, 4, 3, 2, 1, 0, 15, 14, 13, 12]
 SIDE_ORDER, HEAD_ORDER = [1, 2, 3, 0], [5, 6, 7, 0, 1, 2, 3, 4]
 
 

time: 79.4 us -> 80.3 us (1.011)
  starting transfers between devices: 46.9 us -> 43.4 us
  waiting for transfers between devices: 1.87 us -> 4.99 us
  blocking collectives: 21 us -> 22.3 us
    all_to_all x3, waiting for transfers between devices: 0.21 us -> 3.34 us  [exchange(): return lax.all_to_all(x, 'ctx', 0, 0, axis_index_groups=groups, tiled=True)]
    all_to_all x3, starting transfers between devices: 32.6 us -> 29.8 us  [exchange(): return lax.all_to_all(x, 'ctx', 0, 0, axis_index_groups=groups, tiled=True)]
    all_to_all x1, blocking collectives: 10.7 us -> 11.9 us  [body(): lax.all_to_all(product, ('ctx', 'head'), 0, 0, axis_index_groups=planes,...]
  transfers between devices with their start and end apart: 6 -> 6, of which waited for: 2 -> 4; matrix products, arithmetic and copies ran while one was open for 1% -> 1% of each run, Pallas kernels for 2% -> 2%
where the time goes in v8:
time: 80.3 us; the launch traced here: 79.8 us
  starting transfers between devices  43.4 us (54%)
  blocking collectives  22.3 us (28%)
  Pallas kernels  5.86 us (7%)
  waiting for transfers between devices  4.99 us (6%)
  local copies, waits for them, and re-layouts  1.34 us (2%)
  other arithmetic  1.07 us (1%)
    all_to_all x3, starting transfers between devices, exchange(): return lax.all_to_all(x, 'ctx', 0, 0, axis_index_groups=groups, tiled=True)  29.8 us
    ppermute x3, starting transfers between devices, swap(): return lax.ppermute(x, 'ctx', [(i, i ^ bit) for i in range(ctx)])  13.6 us
    all_to_all x1, blocking collectives, body(): lax.all_to_all(product, ('ctx', 'head'), 0, 0, axis_index_groups=planes,...  11.9 us
    all_gather x4, blocking collectives, both(): return lax.all_gather(x, 'ctx', axis=0, axis_index_groups=pairs)  10.4 us
    pallas_call x1, Pallas kernels, body(): pl.pallas_call(prefix_kernel, out_shape=jax.ShapeDtypeStruct((depth, rows...  3.35 us
    all_to_all x3, waiting for transfers between devices, exchange(): return lax.all_to_all(x, 'ctx', 0, 0, axis_index_groups=groups, tiled=True)  3.34 us
    ppermute x3, waiting for transfers between devices, swap(): return lax.ppermute(x, 'ctx', [(i, i ^ bit) for i in range(ctx)])  1.65 us
  transfers between devices with their start and end apart: 6, of which 4 were waited for; matrix products, arithmetic and copies ran while one was open for 1% of the time, Pallas kernels for 2%

profile of v8, /device:TPU:1, one launch (start us, length us, event | category | flops | bytes accessed | tf_op | source)
XLA Modules:
  0.0 79.8 jit_solution(15692150403397563388)
XLA Ops:
  0.0 1.1 %pad_maximum_fusion.kv_ref = bf16[2048,128]{1,0:T(8,128)(2,1)S(1)} fusion(bf16[1024,128]{1,0:T(8,128)(2,1)} %bitcast.30, bf16[1024,128]{1,0:T(8,128)(2,1)} %bitcast.31), kind=kLoop, calls=%fused_computation | loop fusion | flops 1048576 | bytes 1048576 | tf_op jit(solution)/shard_map/concatenate | solution.py:267
  1.1 4.0 %collective-permute-start.2 = (bf16[2048,128]{1,0:T(8,128)(2,1)S(1)}, bf16[2048,128]{1,0:T(8,128)(2,1)S(1)}, u32[]{:S(2)}, u32[]{:S(2)}) collective-permute-start(bf16[2048,128]{1,0:T(8,128)(2,1)S(1)} %pad_maximum_fusion.kv_ref), channel_id=1, source_target_pairs={{0,16},{8,24},{16,0},{24,8},{32,48},{40,56},{48,32},{56,40},{64,80... | collective-permute-start | bytes 1572872 | tf_op jit(solution)/shard_map/ppermute | solution.py:236
  5.1 0.0 copy-start.2
  5.1 8.4 %conditional.2 = (bf16[2048,128]{1,0:T(8,128)(2,1)}, bf16[16,128]{1,0:T(8,128)(2,1)S(1)}) conditional(s32[]{:T(128)} %convert_element_type.2, bf16[2048,128]{1,0:T(8,128)(2,1)S(1)} %pad_maximum_fusion.kv_ref, bf16[2048,128]{1,0:T(8,128)(2,1)S(1)} %pad_maximum_fusion.kv_ref), branch_computations={%region_0.1_spmd, %region_1.2_spmd} | conditional | bytes 2097208 | solution.py:270
  5.2 6.7 %collective-permute-start = (bf16[2048,128]{1,0:T(8,128)(2,1)S(1)}, bf16[2048,128]{1,0:T(8,128)(2,1)}, u32[]{:S(2)}, u32[]{:S(2)}) collective-permute-start(bf16[2048,128]{1,0:T(8,128)(2,1)S(1)} %param.1), channel_id=1, source_target_pairs={{0,8},{8,0},{16,24},{24,16},{32,40},{40,32},{48,56},{56,48},{64,72... | collective-permute-start | bytes 1572872 | tf_op jit(solution)/shard_map/cond/branch_1_fun/ppermute | solution.py:236
  11.8 1.6 %collective-permute-done._ = bf16[2048,128]{1,0:T(8,128)(2,1)} collective-permute-done((bf16[2048,128]{1,0:T(8,128)(2,1)S(1)}, bf16[2048,128]{1,0:T(8,128)(2,1)}, u32[]{:S(2)}, u32[]{:S(2)}) %collective-permute-start) | collective-permute-done | bytes 524320 | tf_op jit(solution)/shard_map/cond/branch_1_fun/ppermute | solution.py:236
  13.5 0.6 broadcast_in_dim.2
  14.1 9.5 %all-to-all-start = ((bf16[16,16,128]{2,1,0:T(8,128)(2,1)}), bf16[16,16,128]{2,1,0:T(8,128)(2,1)S(1)}, u32[]{:S(2)}, u32[]{:S(2)}) async-start(bf16[16,16,128]{2,1,0:T(8,128)(2,1)} %broadcast_in_dim.2), calls=%async_computation | async-start | bytes 131072 | tf_op jit(solution)/shard_map/all_to_all | solution.py:261
  23.6 0.0 collective-permute-done.2
  23.7 2.7 %all-gather = bf16[2048,128]{1,0:T(8,128)(2,1)S(1)} all-gather(bf16[1024,128]{1,0:T(8,128)(2,1)S(1)} %get-tuple-element.23), channel_id=2, replica_groups={{0,8},{16,24},{32,40},{48,56},{64,72},{80,88},{96,104},{112,120},{128,1..., dimensions={0}, use_global_device_ids=true | all-gather | bytes 786432 | tf_op jit(solution)/shard_map/all_gather | solution.py:264
  26.4 2.2 %all-gather.1 = bf16[2048,128]{1,0:T(8,128)(2,1)S(1)} all-gather(bf16[1024,128]{1,0:T(8,128)(2,1)S(1)} %get-tuple-element.22), channel_id=3, replica_groups={{0,8},{16,24},{32,40},{48,56},{64,72},{80,88},{96,104},{112,120},{128,1..., dimensions={0}, use_global_device_ids=true | all-gather | bytes 786432 | tf_op jit(solution)/shard_map/all_gather | solution.py:264
  28.6 1.2 %all-to-all-done = bf16[16,16,128]{2,1,0:T(8,128)(2,1)S(1)} async-done(((bf16[16,16,128]{2,1,0:T(8,128)(2,1)}), bf16[16,16,128]{2,1,0:T(8,128)(2,1)S(1)}, u32[]{:S(2)}, u32[]{:S(2)}) %all-to-all-start) | async-done | bytes 65568 | tf_op jit(solution)/shard_map/all_to_all | solution.py:261
  29.8 3.3 %prefix_state.1 = bf16[16,9,2,128]{3,2,1,0:T(2,128)(2,1)} custom-call(s32[1]{0:T(128)} %bitcast.1.early_ref, bf16[256,128]{1,0:T(8,128)(2,1)S(1)} %bitcast.22, bf16[2048,128]{1,0:T(8,128)(2,1)S(1)} %pad_maximum_fusion.kv_ref, bf16[2048,128]{1,0:T(8,128)(2,1)} %get-tuple-element.18.early_near_ref, bf16[2048,128]{1,0:T(8,128)(2,1)S(1)} %get-tuple-element.28.late_near_ref, ...), custom_call_target="tpu_custom_call" | custom-call | tf_op jit(solution)/shard_map/prefix_state/pallas_call | solution.py:293
  33.1 0.0 copy-start
  33.1 10.8 %all-to-all-start.1 = ((bf16[16,9,2,128]{3,2,1,0:T(2,128)(2,1)}), bf16[16,9,2,128]{3,2,1,0:T(2,128)(2,1)S(1)}, u32[]{:S(2)}, u32[]{:S(2)}) async-start(bf16[16,9,2,128]{3,2,1,0:T(2,128)(2,1)} %prefix_state.1), calls=%async_computation.1 | async-start | bytes 147456 | tf_op jit(solution)/shard_map/all_to_all | solution.py:261
  43.9 2.9 %collective-permute-start.3 = (bf16[80,1024]{1,0:T(8,128)(2,1)S(1)}, bf16[80,1024]{1,0:T(8,128)(2,1)S(1)}, u32[]{:S(2)}, u32[]{:S(2)}) collective-permute-start(bf16[80,1024]{1,0:T(8,128)(2,1)S(1)} %bitcast.32), channel_id=1, source_target_pairs={{0,16},{8,24},{16,0},{24,8},{32,48},{40,56},{48,32},{56,40},{64,80... | collective-permute-start | bytes 491528 | tf_op jit(solution)/shard_map/ppermute | solution.py:236
  47.5 0.0 copy-start.4
  47.5 0.0 copy-start.5
  47.5 0.6 copy-done.4
  48.2 0.0 copy-done.5
  48.2 0.4 suffix_state.1
  48.5 1.9 %all-to-all-done.1.got_ref = bf16[16,9,2,128]{3,2,1,0:T(2,128)(2,1)S(1)} async-done(((bf16[16,9,2,128]{3,2,1,0:T(2,128)(2,1)}), bf16[16,9,2,128]{3,2,1,0:T(2,128)(2,1)S(1)}, u32[]{:S(2)}, u32[]{:S(2)}) %all-to-all-start.1) | async-done | bytes 73760 | tf_op jit(solution)/shard_map/all_to_all | solution.py:261
  50.5 1.1 %combine.1 = bf16[16,16,128]{2,1,0:T(8,128)(2,1)} custom-call(bf16[16,9,2,128]{3,2,1,0:T(2,128)(2,1)S(1)} %all-to-all-done.1.got_ref, f32[16,128]{1,0:T(8,128)S(1)} %get-tuple-element.19.so_ref, f32[16,128]{1,0:T(8,128)S(1)} %get-tuple-element.20.sm_ref, f32[16,128]{1,0:T(8,128)S(1)} %get-tuple-element.21.sl_ref), custom_call_target="tpu_custom_call" | custom-call | tf_op jit(solution)/shard_map/combine/pallas_call | solution.py:308
  51.6 9.5 %all-to-all-start.2 = ((bf16[16,16,128]{2,1,0:T(8,128)(2,1)}), bf16[16,16,128]{2,1,0:T(8,128)(2,1)S(1)}, u32[]{:S(2)}, u32[]{:S(2)}) async-start(bf16[16,16,128]{2,1,0:T(8,128)(2,1)} %combine.1), calls=%async_computation.2 | async-start | bytes 131072 | tf_op jit(solution)/shard_map/all_to_all | solution.py:261
  61.1 3.4 %all-gather.2 = bf16[160,1024]{1,0:T(8,128)(2,1)S(1)} all-gather(bf16[80,1024]{1,0:T(8,128)(2,1)S(1)} %bitcast.33), channel_id=4, replica_groups={{0,8},{16,24},{32,40},{48,56},{64,72},{80,88},{96,104},{112,120},{128,1..., dimensions={0}, use_global_device_ids=true | all-gather | bytes 491520 | tf_op jit(solution)/shard_map/all_gather | solution.py:264
  64.5 0.0 collective-permute-done.3
  64.5 2.0 %all-gather.3 = bf16[160,1024]{1,0:T(8,128)(2,1)S(1)} all-gather(bf16[80,1024]{1,0:T(8,128)(2,1)S(1)} %collective-permute-done.3), channel_id=5, replica_groups={{0,8},{16,24},{32,40},{48,56},{64,72},{80,88},{96,104},{112,120},{128,1..., dimensions={0}, use_global_device_ids=true | all-gather | bytes 491520 | tf_op jit(solution)/shard_map/all_gather | solution.py:264
  66.6 0.2 all-to-all-done.2.x_ref
  66.8 0.5 project.1
  67.3 0.0 copy-start.3
  67.3 11.9 %all_to_all.20 = f32[32,4,80]{2,1,0:T(4,128)S(1)} all-to-all(f32[32,4,80]{2,1,0:T(4,128)S(1)} %bitcast.24), channel_id=1, replica_groups={{13,14,15,8,9,10,11,12,21,22,23,16,17,18,19,20,29,30,31,24,25,26,27,28,..., dimensions={0} | all-to-all | bytes 81920 | tf_op jit(solution)/shard_map/all_to_all | solution.py:328
  79.2 0.6 finish.1
  (12 shorter events, 0.1 us)
Async XLA Ops:
  1.1 22.6 %collective-permute-start.2 = (bf16[2048,128]{1,0:T(8,128)(2,1)S(1)}, bf16[2048,128]{1,0:T(8,128)(2,1)S(1)}, u32[]{:S(2)}, u32[]{:S(2)}) collective-permute-start(bf16[2048,128]{1,0:T(8,128)(2,1)S(1)} %pad_maximum_fusion.kv_ref), channel_id=1, source_target_pairs={{0,16},{8,24},{16,0},{24,8},{32,48},{40,56},{48,32},{56,40},{64,80... | collective-permute-start | bytes 1572872 | tf_op jit(solution)/shard_map/ppermute | solution.py:236
  5.1 8.4 %copy-start.2 = (bf16[2,1,8,128]{3,2,1,0:T(8,128)(2,1)S(1)}, bf16[2,1,8,128]{3,2,1,0:T(8,128)(2,1)}, u32[]{:S(2)}) copy-start(bf16[2,1,8,128]{3,2,1,0:T(8,128)(2,1)} %param.14) | copy-start | bytes 12292
  5.2 8.3 %collective-permute-start = (bf16[2048,128]{1,0:T(8,128)(2,1)S(1)}, bf16[2048,128]{1,0:T(8,128)(2,1)}, u32[]{:S(2)}, u32[]{:S(2)}) collective-permute-start(bf16[2048,128]{1,0:T(8,128)(2,1)S(1)} %param.1), channel_id=1, source_target_pairs={{0,8},{8,0},{16,24},{24,16},{32,40},{40,32},{48,56},{56,48},{64,72... | collective-permute-start | bytes 1572872 | tf_op jit(solution)/shard_map/cond/branch_1_fun/ppermute | solution.py:236
  14.1 15.6 %all-to-all-start = ((bf16[16,16,128]{2,1,0:T(8,128)(2,1)}), bf16[16,16,128]{2,1,0:T(8,128)(2,1)S(1)}, u32[]{:S(2)}, u32[]{:S(2)}) async-start(bf16[16,16,128]{2,1,0:T(8,128)(2,1)} %broadcast_in_dim.2), calls=%async_computation | async-start | bytes 131072 | tf_op jit(solution)/shard_map/all_to_all | solution.py:261
  29.8 14.1 %copy-start.6 = (bf16[1024,80]{0,1:T(8,128)(2,1)S(1)}, bf16[1024,80]{0,1:T(8,128)(2,1)}, u32[]{:S(2)}) copy-start(bf16[1024,80]{0,1:T(8,128)(2,1)} %param.22) | copy-start | bytes 491524
  29.8 17.8 %copy-start.1 = (bf16[1,512,1,128]{3,1,2,0:T(8,128)(2,1)S(1)}, bf16[1,512,1,128]{3,1,2,0:T(8,128)(2,1)}, u32[]{:S(2)}) copy-start(bf16[1,512,1,128]{3,1,2,0:T(8,128)(2,1)} %param.18) | copy-start | bytes 393220
  33.1 14.4 %copy-start = (bf16[1,512,1,128]{3,1,2,0:T(8,128)(2,1)S(1)}, bf16[1,512,1,128]{3,1,2,0:T(8,128)(2,1)}, u32[]{:S(2)}) copy-start(bf16[1,512,1,128]{3,1,2,0:T(8,128)(2,1)} %param.17) | copy-start | bytes 393220
  33.1 17.3 %all-to-all-start.1 = ((bf16[16,9,2,128]{3,2,1,0:T(2,128)(2,1)}), bf16[16,9,2,128]{3,2,1,0:T(2,128)(2,1)S(1)}, u32[]{:S(2)}, u32[]{:S(2)}) async-start(bf16[16,9,2,128]{3,2,1,0:T(2,128)(2,1)} %prefix_state.1), calls=%async_computation.1 | async-start | bytes 147456 | tf_op jit(solution)/shard_map/all_to_all | solution.py:261
  43.9 20.6 %collective-permute-start.3 = (bf16[80,1024]{1,0:T(8,128)(2,1)S(1)}, bf16[80,1024]{1,0:T(8,128)(2,1)S(1)}, u32[]{:S(2)}, u32[]{:S(2)}) collective-permute-start(bf16[80,1024]{1,0:T(8,128)(2,1)S(1)} %bitcast.32), channel_id=1, source_target_pairs={{0,16},{8,24},{16,0},{24,8},{32,48},{40,56},{48,32},{56,40},{64,80... | collective-permute-start | bytes 491528 | tf_op jit(solution)/shard_map/ppermute | solution.py:236
  47.5 0.7 copy-start.4
  47.5 0.7 copy-start.5
  51.6 15.2 %all-to-all-start.2 = ((bf16[16,16,128]{2,1,0:T(8,128)(2,1)}), bf16[16,16,128]{2,1,0:T(8,128)(2,1)S(1)}, u32[]{:S(2)}, u32[]{:S(2)}) async-start(bf16[16,16,128]{2,1,0:T(8,128)(2,1)} %combine.1), calls=%async_computation.2 | async-start | bytes 131072 | tf_op jit(solution)/shard_map/all_to_all | solution.py:261
  67.3 11.9 %copy-start.3 = (bf16[2,8,80]{2,1,0:T(8,128)(2,1)S(1)}, bf16[2,8,80]{2,1,0:T(8,128)(2,1)}, u32[]{:S(2)}) copy-start(bf16[2,8,80]{2,1,0:T(8,128)(2,1)} %residual_ref.1) | copy-start | bytes 7684
